TPU v7x, 32 devices: a whole 2x2x4 slice. The times are simulated.
32 devices in a mesh: seq: 2 (over x), fsdp: 4 (over z), tensor: 4 (over y, core).
Axes of the slice: x: 2, y: 2, z: 4, core: 2. Of those that a mesh axis runs over, the one named last changes fastest.
Arguments:
- layer_in: bfloat16 [1, 5120, 2304], P(None, ('seq', 'fsdp')), may hold values from -6 to 6
- segment_ids: int32 [1, 5120], replicated, may hold values from 0 to 3, as said below
- attn_pre_gain: bfloat16 [2304], P('fsdp'), may hold values from 0.099609375 to 1.8984375
- query_weight: bfloat16 [2304, 2048], P('fsdp', 'tensor'), may hold values from -0.125 to 0.125
- key_weight: bfloat16 [2304, 1024], P('fsdp', 'tensor'), may hold values from -0.125 to 0.125
- value_weight: bfloat16 [2304, 1024], P('fsdp', 'tensor'), may hold values from -0.125 to 0.125
- out_weight: bfloat16 [2048, 2304], P('tensor', 'fsdp'), may hold values from -0.125 to 0.125
- attn_post_gain: bfloat16 [2304], P('fsdp'), may hold values from 0.099609375 to 1.8984375
- ffn_pre_gain: bfloat16 [2304], P('fsdp'), may hold values from 0.099609375 to 1.8984375
- gate_weight: bfloat16 [2304, 9216], P('fsdp', 'tensor'), may hold values from -0.125 to 0.125
- up_weight: bfloat16 [2304, 9216], P('fsdp', 'tensor'), may hold values from -0.125 to 0.125
- down_weight: bfloat16 [9216, 2304], P('tensor', 'fsdp'), may hold values from -0.0625 to 0.0625
- ffn_post_gain: bfloat16 [2304], P('fsdp'), may hold values from 0.099609375 to 1.8984375
- out_grad: bfloat16 [1, 5120, 2304], P(None, ('seq', 'fsdp')), may hold values from -6 to 6
Outputs:
- layer_out: bfloat16 [1, 5120, 2304], P(None, ('seq', 'fsdp'))
- input_grad: float32 [1, 5120, 2304], P(None, ('seq', 'fsdp'))
- attn_pre_gain_grad: float32 [2304], P('fsdp')
- query_weight_grad: float32 [2304, 2048], P('fsdp', 'tensor')
- key_weight_grad: float32 [2304, 1024], P('fsdp', 'tensor')
- value_weight_grad: float32 [2304, 1024], P('fsdp', 'tensor')
- out_weight_grad: float32 [2048, 2304], P('tensor', 'fsdp')
- attn_post_gain_grad: float32 [2304], P('fsdp')
- ffn_pre_gain_grad: float32 [2304], P('fsdp')
- gate_weight_grad: float32 [2304, 9216], P('fsdp', 'tensor')
- up_weight_grad: float32 [2304, 9216], P('fsdp', 'tensor')
- down_weight_grad: float32 [9216, 2304], P('tensor', 'fsdp')
- ffn_post_gain_grad: float32 [2304], P('fsdp')
Inputs may be any that keep to these rules, and one draw needn't show every extreme that they name: `segment_ids`: along each sequence the ids start at 0 and rise by one at each document start; every sequence holds four documents, and the starts of the second to fourth lie within the last 640 tokens.
All inputs are finite; a program needn't handle non-finite values.
Results may differ from a plain program's by a relative error of at most 0.022.
Values may be sent and summed in bfloat16 or wider, within the bound.
No kernel may reach another device: no remote copies, remote signals or barrier semaphores. Data moves between devices by JAX's collectives and lax.ppermute only.
A program may use at most 320 MiB of HBM per device.

v0:
```python
import math

import jax
import jax.numpy as jnp
from jax import lax
from jax.sharding import PartitionSpec as P

HD = 256
WINDOW = 4096


epsilon = 1e-06
soft_cap = 50.0


def from_behind(block, axis, distance):
    devices = range(lax.axis_size(axis))
    route = [(i - distance, i) for i in devices if i - distance in devices]
    return lax.ppermute(block, axis, route)


def rms_norm(field, gain_vec):
    return field * lax.rsqrt(jnp.mean(field * field, axis=-1, keepdims=True) + epsilon) * gain_vec


def norm_back(field, gain_vec, incoming):
    unused, pullback = jax.vjp(rms_norm, field, gain_vec)
    return pullback(incoming)


def tables(positions):
    frequency = jnp.exp(jnp.arange(HD // 2, dtype=jnp.float32) * (-2.0 * math.log(10000.0) / HD))
    angles = positions[:, None] * frequency[None, :]
    return (jnp.cos(angles), jnp.sin(angles))


def rotate(field, cos_tab, sine_tab):
    half_dim = field.shape[-1] // 2
    front_part = field[..., :half_dim]
    back_part = field[..., half_dim:]
    cos_b = cos_tab[:, None, :]
    sin_b = sine_tab[:, None, :]
    return jnp.concatenate(
        [front_part * cos_b - back_part * sin_b, back_part * cos_b + front_part * sin_b], axis=-1
    )


def matmul(left, right):
    return jnp.dot(left, right, preferred_element_type=jnp.float32)


def scores_of(q_row, k_row, allowed_row):
    raw_scores = jnp.einsum("gqd,kgd->gqk", q_row, k_row, preferred_element_type=jnp.float32)
    bent_tanh = jnp.tanh(raw_scores / soft_cap)
    capped = jnp.where(allowed_row[None], soft_cap * bent_tanh, -1e30)
    return (capped, bent_tanh)


def forward_row(inputs):
    q_row, k_row, v_row, allowed_row = inputs
    capped, unused = scores_of(q_row, k_row, allowed_row)
    maximum = jnp.max(capped, axis=-1, keepdims=True)
    exponent = jnp.exp(capped - maximum)
    totals = jnp.sum(exponent, axis=-1, keepdims=True)
    attn_probs = (exponent / totals).astype(jnp.bfloat16)
    mixed = jnp.einsum("gqk,kgd->gqd", attn_probs, v_row, preferred_element_type=jnp.float32)
    return (mixed.astype(jnp.bfloat16), (maximum + jnp.log(totals))[..., 0])


def backward_row(inputs):
    q_row, k_row, v_row, allowed_row, log_total, d_mixed = inputs
    capped, bent_tanh = scores_of(q_row, k_row, allowed_row)
    attn_probs = jnp.exp(capped - log_total[..., None])
    d_probs = jnp.einsum("gqd,kgd->gqk", d_mixed, v_row, preferred_element_type=jnp.float32)
    inner_sum = jnp.sum(attn_probs * d_probs, axis=-1, keepdims=True)
    d_raw = (attn_probs * (d_probs - inner_sum) * (1.0 - bent_tanh * bent_tanh)).astype(
        jnp.bfloat16
    )
    d_query = jnp.einsum("gqk,kgd->gqd", d_raw, k_row, preferred_element_type=jnp.float32)
    d_key = jnp.einsum("gqk,gqd->kgd", d_raw, q_row, preferred_element_type=jnp.float32)
    d_value = jnp.einsum(
        "gqk,gqd->kgd", attn_probs.astype(jnp.bfloat16), d_mixed, preferred_element_type=jnp.float32
    )
    return (d_query, d_key, d_value)


def shards(
    layer_in,
    segment_ids,
    attn_pre_gain,
    query_weight,
    key_weight,
    value_weight,
    out_weight,
    attn_post_gain,
    ffn_pre_gain,
    gate_weight,
    up_weight,
    down_weight,
    ffn_post_gain,
    out_grad,
):
    seq_count, piece_len, model_width = layer_in.shape
    fsdp_size = lax.axis_size("fsdp")
    seq_index = lax.axis_index("seq")
    fsdp_index = lax.axis_index("fsdp")
    half_len = piece_len * fsdp_size
    edge_len = min(WINDOW, half_len)
    span_len = WINDOW + piece_len
    kv_local = key_weight.shape[1] // HD
    q_local = query_weight.shape[1] // HD
    repeat = q_local // kv_local
    kv_width = kv_local * HD
    row_count = seq_count * piece_len
    q_scale = HD ** (-0.5)
    pre_gain, w_query, w_key, w_value, w_out, post_gain, mlp_pre, w_gate, w_up, w_down, mlp_post = (
        lax.all_gather(attn_pre_gain, "fsdp", axis=0, tiled=True),
        lax.all_gather(query_weight, "fsdp", axis=0, tiled=True),
        lax.all_gather(key_weight, "fsdp", axis=0, tiled=True),
        lax.all_gather(value_weight, "fsdp", axis=0, tiled=True),
        lax.all_gather(out_weight, "fsdp", axis=1, tiled=True),
        lax.all_gather(attn_post_gain, "fsdp", axis=0, tiled=True),
        lax.all_gather(ffn_pre_gain, "fsdp", axis=0, tiled=True),
        lax.all_gather(gate_weight, "fsdp", axis=0, tiled=True),
        lax.all_gather(up_weight, "fsdp", axis=0, tiled=True),
        lax.all_gather(down_weight, "fsdp", axis=1, tiled=True),
        lax.all_gather(ffn_post_gain, "fsdp", axis=0, tiled=True),
    )
    pre_gain = pre_gain.astype(jnp.float32)
    post_gain = post_gain.astype(jnp.float32)
    mlp_pre = mlp_pre.astype(jnp.float32)
    mlp_post = mlp_post.astype(jnp.float32)
    flat = layer_in.reshape(row_count, model_width).astype(jnp.float32)
    h_one = rms_norm(flat, pre_gain).astype(jnp.bfloat16)
    q_pre = matmul(h_one, w_query).reshape(seq_count, piece_len, q_local, HD)
    k_pre = matmul(h_one, w_key).reshape(seq_count, piece_len, kv_local, HD)
    v_cast = matmul(h_one, w_value).astype(jnp.bfloat16).reshape(seq_count, piece_len, kv_width)
    first_pos = (seq_index * fsdp_size + fsdp_index) * piece_len
    cos_tab, sine_tab = tables(
        (first_pos + jnp.arange(piece_len, dtype=jnp.int32)).astype(jnp.float32)
    )
    q_cast = (rotate(q_pre, cos_tab, sine_tab) * q_scale).astype(jnp.bfloat16)
    k_cast = (
        rotate(k_pre, cos_tab, sine_tab)
        .astype(jnp.bfloat16)
        .reshape(seq_count, piece_len, kv_width)
    )
    k_half, v_half = (
        lax.all_gather(k_cast, "fsdp", axis=1, tiled=True),
        lax.all_gather(v_cast, "fsdp", axis=1, tiled=True),
    )
    k_edge, v_edge = from_behind((k_half, v_half), "seq", 1)
    k_all = jnp.concatenate([k_edge, k_half], axis=1)
    v_all = jnp.concatenate([v_edge, v_half], axis=1)
    key_start = jnp.maximum(fsdp_index * piece_len + edge_len - WINDOW, 0)
    k_span = lax.dynamic_slice_in_dim(k_all, key_start, span_len, 1).reshape(
        seq_count, span_len, kv_local, HD
    )
    v_span = lax.dynamic_slice_in_dim(v_all, key_start, span_len, 1).reshape(
        seq_count, span_len, kv_local, HD
    )
    key_first = seq_index * half_len - edge_len + key_start
    padded = jnp.concatenate([jnp.full((seq_count, edge_len), -1, jnp.int32), segment_ids], axis=1)
    key_seg = lax.dynamic_slice_in_dim(padded, key_first + edge_len, span_len, 1)
    query_seg = lax.dynamic_slice_in_dim(segment_ids, first_pos, piece_len, 1)
    offsets = (first_pos + jnp.arange(piece_len, dtype=jnp.int32))[:, None] - (
        key_first + jnp.arange(span_len, dtype=jnp.int32)
    )[None, :]
    allowed = (
        (offsets >= 0)[None]
        & (offsets < WINDOW)[None]
        & (query_seg[:, :, None] == key_seg[:, None, :])
    )
    allowed_rep = jnp.tile(allowed, (1, repeat, 1))
    q_rows = (
        q_cast.reshape(seq_count, piece_len, kv_local, repeat, HD)
        .transpose(0, 2, 3, 1, 4)
        .reshape(seq_count, kv_local, repeat * piece_len, HD)
    )
    mixed, log_total = lax.map(forward_row, (q_rows, k_span, v_span, allowed_rep))
    attended = (
        mixed.reshape(seq_count, kv_local, repeat, piece_len, HD)
        .transpose(0, 3, 1, 2, 4)
        .reshape(row_count, q_local * HD)
    )
    a_sum = lax.psum(matmul(attended, w_out), "tensor")
    r_one = flat + rms_norm(a_sum, post_gain)
    h_two = rms_norm(r_one, mlp_pre).astype(jnp.bfloat16)
    gate_pre = matmul(h_two, w_gate)
    up_pre = matmul(h_two, w_up)
    hidden = (jax.nn.gelu(gate_pre, approximate=True) * up_pre).astype(jnp.bfloat16)
    m_sum = lax.psum(matmul(hidden, w_down), "tensor")
    layer_out = (
        (r_one + rms_norm(m_sum, mlp_post))
        .astype(jnp.bfloat16)
        .reshape(seq_count, piece_len, model_width)
    )
    incoming = out_grad.reshape(row_count, model_width).astype(jnp.float32)
    d_msum, dg_mlp_post = norm_back(m_sum, mlp_post, incoming)
    dm_cast = d_msum.astype(jnp.bfloat16)
    d_hidden = matmul(dm_cast, w_down.T)
    dw_down = matmul(hidden.T, dm_cast)
    unused, gelu_pull = jax.vjp(
        lambda gate_in, up_in: jax.nn.gelu(gate_in, approximate=True) * up_in, gate_pre, up_pre
    )
    d_gate, d_up = gelu_pull(d_hidden)
    d_gate = d_gate.astype(jnp.bfloat16)
    d_up = d_up.astype(jnp.bfloat16)
    dh_two = lax.psum(matmul(d_gate, w_gate.T) + matmul(d_up, w_up.T), "tensor")
    dw_gate = matmul(h_two.T, d_gate)
    dw_up = matmul(h_two.T, d_up)
    dr_add, dg_mlp_pre = norm_back(r_one, mlp_pre, dh_two)
    d_resid = incoming + dr_add
    d_asum, dg_post = norm_back(a_sum, post_gain, d_resid)
    da_cast = d_asum.astype(jnp.bfloat16)
    d_attended = matmul(da_cast, w_out.T).astype(jnp.bfloat16)
    dw_out = matmul(attended.T, da_cast)
    dout_rows = (
        d_attended.reshape(seq_count, piece_len, kv_local, repeat, HD)
        .transpose(0, 2, 3, 1, 4)
        .reshape(seq_count, kv_local, repeat * piece_len, HD)
    )
    d_query, d_key, d_value = lax.map(
        backward_row, (q_rows, k_span, v_span, allowed_rep, log_total, dout_rows)
    )
    empty_grad = jnp.zeros((seq_count, edge_len + half_len, kv_width), jnp.float32)
    dk_full = lax.dynamic_update_slice_in_dim(
        empty_grad, d_key.reshape(seq_count, span_len, kv_width), key_start, 1
    )
    dv_full = lax.dynamic_update_slice_in_dim(
        empty_grad, d_value.reshape(seq_count, span_len, kv_width), key_start, 1
    )
    dk_edge, dv_edge = (
        from_behind(dk_full[:, :edge_len].astype(jnp.bfloat16), "seq", -1).astype(jnp.float32),
        from_behind(dv_full[:, :edge_len].astype(jnp.bfloat16), "seq", -1).astype(jnp.float32),
    )
    dk_half = dk_full[:, edge_len:].at[:, half_len - edge_len :].add(dk_edge)
    dv_half = dv_full[:, edge_len:].at[:, half_len - edge_len :].add(dv_edge)
    dk_own, dv_own = (
        lax.psum_scatter(
            dk_half.astype(jnp.bfloat16), "fsdp", scatter_dimension=1, tiled=True
        ).astype(jnp.float32),
        lax.psum_scatter(
            dv_half.astype(jnp.bfloat16), "fsdp", scatter_dimension=1, tiled=True
        ).astype(jnp.float32),
    )
    dk_cast = (
        rotate(dk_own.reshape(seq_count, piece_len, kv_local, HD), cos_tab, -sine_tab)
        .astype(jnp.bfloat16)
        .reshape(row_count, kv_width)
    )
    dv_cast = dv_own.astype(jnp.bfloat16).reshape(row_count, kv_width)
    dq_heads = (
        d_query.reshape(seq_count, kv_local, repeat, piece_len, HD)
        .transpose(0, 3, 1, 2, 4)
        .reshape(seq_count, piece_len, q_local, HD)
    )
    dq_cast = (
        rotate(dq_heads * q_scale, cos_tab, -sine_tab)
        .astype(jnp.bfloat16)
        .reshape(row_count, q_local * HD)
    )
    dh_one = lax.psum(
        (matmul(dq_cast, w_query.T) + matmul(dk_cast, w_key.T) + matmul(dv_cast, w_value.T)).astype(
            jnp.bfloat16
        ),
        "tensor",
    ).astype(jnp.float32)
    dw_query = matmul(h_one.T, dq_cast)
    dw_key = matmul(h_one.T, dk_cast)
    dw_value = matmul(h_one.T, dv_cast)
    dx_add, dg_pre = norm_back(flat, pre_gain, dh_one)
    input_grad = (d_resid + dx_add).reshape(seq_count, piece_len, model_width)
    shard_sums = (
        lax.psum_scatter(
            dg_pre.astype(jnp.bfloat16), "fsdp", scatter_dimension=0, tiled=True
        ).astype(jnp.float32),
        lax.psum_scatter(
            dw_query.astype(jnp.bfloat16), "fsdp", scatter_dimension=0, tiled=True
        ).astype(jnp.float32),
        lax.psum_scatter(
            dw_key.astype(jnp.bfloat16), "fsdp", scatter_dimension=0, tiled=True
        ).astype(jnp.float32),
        lax.psum_scatter(
            dw_value.astype(jnp.bfloat16), "fsdp", scatter_dimension=0, tiled=True
        ).astype(jnp.float32),
        lax.psum_scatter(
            dw_out.astype(jnp.bfloat16), "fsdp", scatter_dimension=1, tiled=True
        ).astype(jnp.float32),
        lax.psum_scatter(
            dg_post.astype(jnp.bfloat16), "fsdp", scatter_dimension=0, tiled=True
        ).astype(jnp.float32),
        lax.psum_scatter(
            dg_mlp_pre.astype(jnp.bfloat16), "fsdp", scatter_dimension=0, tiled=True
        ).astype(jnp.float32),
        lax.psum_scatter(
            dw_gate.astype(jnp.bfloat16), "fsdp", scatter_dimension=0, tiled=True
        ).astype(jnp.float32),
        lax.psum_scatter(
            dw_up.astype(jnp.bfloat16), "fsdp", scatter_dimension=0, tiled=True
        ).astype(jnp.float32),
        lax.psum_scatter(
            dw_down.astype(jnp.bfloat16), "fsdp", scatter_dimension=1, tiled=True
        ).astype(jnp.float32),
        lax.psum_scatter(
            dg_mlp_post.astype(jnp.bfloat16), "fsdp", scatter_dimension=0, tiled=True
        ).astype(jnp.float32),
    )
    g_pre, g_query, g_key, g_value, g_out, g_post, g_mlp_pre, g_gate, g_up, g_down, g_mlp_post = (
        lax.psum(shard_sums[0].astype(jnp.bfloat16), "seq").astype(jnp.float32),
        lax.psum(shard_sums[1].astype(jnp.bfloat16), "seq").astype(jnp.float32),
        lax.psum(shard_sums[2].astype(jnp.bfloat16), "seq").astype(jnp.float32),
        lax.psum(shard_sums[3].astype(jnp.bfloat16), "seq").astype(jnp.float32),
        lax.psum(shard_sums[4].astype(jnp.bfloat16), "seq").astype(jnp.float32),
        lax.psum(shard_sums[5].astype(jnp.bfloat16), "seq").astype(jnp.float32),
        lax.psum(shard_sums[6].astype(jnp.bfloat16), "seq").astype(jnp.float32),
        lax.psum(shard_sums[7].astype(jnp.bfloat16), "seq").astype(jnp.float32),
        lax.psum(shard_sums[8].astype(jnp.bfloat16), "seq").astype(jnp.float32),
        lax.psum(shard_sums[9].astype(jnp.bfloat16), "seq").astype(jnp.float32),
        lax.psum(shard_sums[10].astype(jnp.bfloat16), "seq").astype(jnp.float32),
    )
    return (
        layer_out,
        input_grad,
        g_pre,
        g_query,
        g_key,
        g_value,
        g_out,
        g_post,
        g_mlp_pre,
        g_gate,
        g_up,
        g_down,
        g_mlp_post,
    )


def solution(mesh):
    return jax.shard_map(
        shards,
        mesh=mesh,
        in_specs=(
            P(None, ("seq", "fsdp"), None),
            P(),
            P("fsdp"),
            P("fsdp", "tensor"),
            P("fsdp", "tensor"),
            P("fsdp", "tensor"),
            P("tensor", "fsdp"),
            P("fsdp"),
            P("fsdp"),
            P("fsdp", "tensor"),
            P("fsdp", "tensor"),
            P("tensor", "fsdp"),
            P("fsdp"),
            P(None, ("seq", "fsdp"), None),
        ),
        out_specs=(
            P(None, ("seq", "fsdp"), None),
            P(None, ("seq", "fsdp"), None),
            P("fsdp"),
            P("fsdp", "tensor"),
            P("fsdp", "tensor"),
            P("fsdp", "tensor"),
            P("tensor", "fsdp"),
            P("fsdp"),
            P("fsdp"),
            P("fsdp", "tensor"),
            P("fsdp", "tensor"),
            P("tensor", "fsdp"),
            P("fsdp"),
        ),
        check_vma=False,
    )
```

profile of v0, /device:TPU:0, one launch (start us, length us, event | category | flops | bytes accessed | tf_op | source)
XLA Modules:
  0.0 2518.7 jit_solution(29680283499449940)
XLA Ops:
  14.2 21.5 all-reduce.10
  38.4 5.1 all-gather.17.cloned.1.call-done
  43.5 3.9 convolution_convert_fusion.9
  47.5 27.3 %all-gather.13.cloned.1.call-done = bf16[2304,256]{1,0:T(8,128)(2,1)} async-done(((bf16[576,256]{1,0:T(8,128)(2,1)}), bf16[2304,256]{1,0:T(8,128)(2,1)}) %all-gather.13.cloned.1.call-update) | async-done | bytes 1179664 | tf_op jit(solution)/shard_map/all_gather | solution.py:119
  81.0 27.8 %all-gather.27.cloned.1.call-done = bf16[2560,256]{1,0:T(8,128)(2,1)} async-done(((bf16[640,256]{1,0:T(8,128)(2,1)}), bf16[2560,256]{1,0:T(8,128)(2,1)}) %all-gather.27.cloned.1.call-update) | async-done | bytes 1310736 | tf_op jit(solution)/shard_map/all_gather | solution.py:150
  108.8 4.4 collective-permute-start.1
  113.2 28.9 %all-gather.15.cloned.1.call-done = bf16[1,2560,256]{1,2,0:T(8,128)(2,1)} async-done(((bf16[1,640,256]{1,2,0:T(8,128)(2,1)}), bf16[1,2560,256]{1,2,0:T(8,128)(2,1)}) %all-gather.15.cloned.1.call-update) | async-done | bytes 1310736 | tf_op jit(solution)/shard_map/all_gather | solution.py:149
  142.1 4.6 collective-permute-start
  146.7 4.0 fusion.4
  152.8 40.6 %all-gather.11.cloned.1.call-done = bf16[2304,512]{1,0:T(8,128)(2,1)} async-done(((bf16[576,512]{1,0:T(8,128)(2,1)}), bf16[2304,512]{1,0:T(8,128)(2,1)}) %all-gather.11.cloned.1.call-update) | async-done | bytes 2359312 | tf_op jit(solution)/shard_map/all_gather | solution.py:118
  193.4 4.3 copy.32
  197.7 4.8 fusion.52
  205.8 15.2 fusion.2
  220.9 14.4 fusion
  236.1 9.9 divide_convert_fusion
  246.1 8.5 convolution_convert_fusion.7
  254.9 6.2 fusion.103
  263.3 110.0 %all-reduce.19.cloned.1.call-done = f32[640,2304]{1,0:T(8,128)} async-done(((f32[640,2304]{1,0:T(8,128)}), f32[640,2304]{1,0:T(8,128)}) %all-reduce.19.cloned.1.call-update) | async-done | bytes 5898256 | tf_op jit(solution)/shard_map/psum | solution.py:186
  382.0 179.1 %all-gather.21.cloned.1.call-done = bf16[2304,2304]{1,0:T(8,128)(2,1)} async-done(((bf16[576,2304]{1,0:T(8,128)(2,1)}), bf16[2304,2304]{1,0:T(8,128)(2,1)}) %all-gather.21.cloned.1.call-update) | async-done | bytes 10616848 | tf_op jit(solution)/shard_map/all_gather | solution.py:124
  561.1 12.4 fusion.104
  573.5 173.4 %all-gather.23.cloned.1.call-done = bf16[2304,2304]{1,0:T(8,128)(2,1)} async-done(((bf16[576,2304]{1,0:T(8,128)(2,1)}), bf16[2304,2304]{1,0:T(8,128)(2,1)}) %all-gather.23.cloned.1.call-update) | async-done | bytes 10616848 | tf_op jit(solution)/shard_map/all_gather | solution.py:125
  746.9 14.2 multiply_convert_fusion.2
  761.1 171.5 %all-gather.25.cloned.1.call-done = bf16[2304,2304]{0,1:T(8,128)(2,1)} async-done(((bf16[2304,576]{0,1:T(8,128)(2,1)}), bf16[2304,2304]{0,1:T(8,128)(2,1)}) %all-gather.25.cloned.1.call-update) | async-done | bytes 10616848 | tf_op jit(solution)/shard_map/all_gather | solution.py:126
  932.6 13.4 fusion.105
  946.1 111.5 %all-reduce.21.cloned.1.call-done = f32[640,2304]{1,0:T(8,128)} async-done(((f32[640,2304]{1,0:T(8,128)}), f32[640,2304]{1,0:T(8,128)}) %all-reduce.21.cloned.1.call-update) | async-done | bytes 5898256 | tf_op jit(solution)/shard_map/psum | solution.py:192
  1060.9 5.2 fusion.32
  1066.2 4.4 fusion.28
  1070.6 19.0 multiply_convert_fusion.1
  1089.5 10.3 fusion.106
  1099.8 14.2 convolution_add_fusion
  1114.8 112.8 %all-reduce.23.cloned.1.call-done = f32[640,2304]{1,0:T(8,128)} async-done(((f32[640,2304]{1,0:T(8,128)}), f32[640,2304]{1,0:T(8,128)}) %all-reduce.23.cloned.1.call-update) | async-done | bytes 5898256 | tf_op jit(solution)/shard_map/psum | solution.py:209
  1227.6 6.5 multiply_reduce_fusion.1
  1234.2 8.6 multiply_reduce_fusion.2
  1251.4 24.2 fusion.1
  1275.7 23.9 multiply_convert_fusion
  1299.5 9.9 convolution_bitcast_fusion.1
  1312.4 20.6 dynamic_update_slice.20
  1336.2 30.9 %collective-permute-done.2 = bf16[1,2560,256]{1,2,0:T(8,128)(2,1)S(1)} collective-permute-done((bf16[1,2560,256]{1,2,0:T(8,128)(2,1)S(1)}, bf16[1,2560,256]{1,2,0:T(8,128)(2,1)S(1)}, u32[]{:S(2)}, u32[]{:S(2)}) %collective-permute-start.2) | collective-permute-done | bytes 1310752 | tf_op jit(solution)/shard_map/ppermute | solution.py:19
  1370.3 5.8 copy.36
  1377.5 9.6 convolution_bitcast_fusion
  1390.0 20.7 dynamic_update_slice.21
  1413.9 30.0 %collective-permute-done.3 = bf16[1,2560,256]{1,2,0:T(8,128)(2,1)S(1)} collective-permute-done((bf16[1,2560,256]{1,2,0:T(8,128)(2,1)S(1)}, bf16[1,2560,256]{1,2,0:T(8,128)(2,1)S(1)}, u32[]{:S(2)}, u32[]{:S(2)}) %collective-permute-start.3) | collective-permute-done | bytes 1310752 | tf_op jit(solution)/shard_map/ppermute | solution.py:19
  1447.1 5.7 copy.38
  1454.2 9.0 fusion.49
  1464.4 3.7 convolution_convert_fusion.4
  1468.3 5.5 convolution_convert_fusion.3
  1481.4 3.6 reduce-scatter.30.cloned.1.call-done
  1491.0 13.8 convolution_convert_fusion
  1505.1 13.4 convolution_convert_fusion.2
  1518.5 13.4 convolution_convert_fusion.1
  1532.3 3.7 fusion.107
  1540.0 44.3 %reduce-scatter.20.cloned.1.call-done = bf16[512,576]{0,1:T(8,128)(2,1)} async-done(((bf16[512,2304]{0,1:T(8,128)(2,1)}), bf16[512,576]{0,1:T(8,128)(2,1)}) %reduce-scatter.20.cloned.1.call-update) | async-done | bytes 589840 | tf_op jit(solution)/shard_map/reduce_scatter | solution.py:287
  1584.3 31.4 %reduce-scatter.16.cloned.1.call-done = bf16[576,256]{1,0:T(8,128)(2,1)} async-done(((bf16[2304,256]{1,0:T(8,128)(2,1)}), bf16[576,256]{1,0:T(8,128)(2,1)}) %reduce-scatter.16.cloned.1.call-update) | async-done | bytes 294928 | tf_op jit(solution)/shard_map/reduce_scatter | solution.py:281
  1615.8 30.7 %reduce-scatter.18.cloned.1.call-done = bf16[576,256]{1,0:T(8,128)(2,1)} async-done(((bf16[2304,256]{1,0:T(8,128)(2,1)}), bf16[576,256]{1,0:T(8,128)(2,1)}) %reduce-scatter.18.cloned.1.call-update) | async-done | bytes 294928 | tf_op jit(solution)/shard_map/reduce_scatter | solution.py:284
  1646.5 181.2 %reduce-scatter.26.cloned.1.call-done = bf16[2304,576]{0,1:T(8,128)(2,1)} async-done(((bf16[2304,2304]{0,1:T(8,128)(2,1)}), bf16[2304,576]{0,1:T(8,128)(2,1)}) %reduce-scatter.26.cloned.1.call-update) | async-done | bytes 2654224 | tf_op jit(solution)/shard_map/reduce_scatter | solution.py:302
  1827.7 183.5 %reduce-scatter.22.cloned.1.call-done = bf16[576,2304]{1,0:T(8,128)(2,1)} async-done(((bf16[2304,2304]{1,0:T(8,128)(2,1)}), bf16[576,2304]{1,0:T(8,128)(2,1)}) %reduce-scatter.22.cloned.1.call-update) | async-done | bytes 2654224 | tf_op jit(solution)/shard_map/reduce_scatter | solution.py:296
  2011.2 183.6 %reduce-scatter.24.cloned.1.call-done = bf16[576,2304]{1,0:T(8,128)(2,1)} async-done(((bf16[2304,2304]{1,0:T(8,128)(2,1)}), bf16[576,2304]{1,0:T(8,128)(2,1)}) %reduce-scatter.24.cloned.1.call-update) | async-done | bytes 2654224 | tf_op jit(solution)/shard_map/reduce_scatter | solution.py:299
  2195.5 68.7 %all-reduce.25.cloned.1.call-done = bf16[640,2304]{1,0:T(8,128)(2,1)} async-done(((bf16[640,2304]{1,0:T(8,128)(2,1)}), bf16[640,2304]{1,0:T(8,128)(2,1)}) %all-reduce.25.cloned.1.call-update) | async-done | bytes 2949136 | tf_op jit(solution)/shard_map/psum | solution.py:263
  2264.2 4.2 fusion.16
  2268.3 19.0 all-reduce.9
  2287.7 5.1 all-reduce.11
  2295.2 6.1 fusion.31
  2301.3 196.3 %all-reduce.27.cloned.1.call-done = (bf16[576,512]{1,0:T(8,128)(2,1)}, bf16[576,256]{1,0:T(8,128)(2,1)}, bf16[576,256]{1,0:T(8,128)(2,1)}, bf16[512,576]{0,1:T(8...) async-done(((bf16[576,512]{1,0:T(8,128)(2,1)}, bf16[576,256]{1,0:T(8,128)(2,1)}, bf16[576,256]{1,0:T(8,128)(2,1)}, ...) | async-done | bytes 9732112 | tf_op jit(solution)/shard_map/psum | solution.py:311
  2497.6 4.7 convert_element_type.299
  (256 shorter events, 98.1 us)
Async XLA Ops:
  7.2 36.3 %all-gather.17.cloned.1.call-start = ((), (), s32[]{:S(2)}) async-start(), calls=%async_computation.12 | async-start | bytes 1474560 | tf_op jit(solution)/shard_map/all_gather | solution.py:120
  7.9 66.9 %all-gather.13.cloned.1.call-start = ((), (), s32[]{:S(2)}) async-start(), calls=%async_computation.10 | async-start | bytes 1474560 | tf_op jit(solution)/shard_map/all_gather | solution.py:119
  8.7 100.1 %all-gather.27.cloned.1.call-start = ((), (), s32[]{:S(2)}) async-start(), calls=%async_computation.28 | async-start | bytes 1638400 | tf_op jit(solution)/shard_map/all_gather | solution.py:150
  35.7 162.0 %copy-start.36 = (f32[2304]{0:T(1024)}, f32[2304]{0:T(1024)S(1)}, u32[]{:S(2)}) copy-start(f32[2304]{0:T(1024)S(1)} %convert_element_type.253) | copy-start | bytes 27652
  35.7 39.1 %copy-start.7 = (bf16[1,640,2304]{2,1,0:T(8,128)(2,1)S(1)}, bf16[1,640,2304]{2,1,0:T(8,128)(2,1)}, u32[]{:S(2)}) copy-start(bf16[1,640,2304]{2,1,0:T(8,128)(2,1)} %param.22) | copy-start | bytes 8847364
  38.4 38.9 %copy-start.42 = (f32[640]{0:T(1024)}, f32[640]{0:T(1024)S(1)}, u32[]{:S(2)}) copy-start(f32[640]{0:T(1024)S(1)} %fusion.17) | copy-start | bytes 7684
  38.4 159.3 %copy-start.46 = (f32[640]{0:T(1024)}, f32[640]{0:T(1024)S(1)}, u32[]{:S(2)}) copy-start(f32[640]{0:T(1024)S(1)} %fusion.83) | copy-start | bytes 7684
  47.3 33.4 %copy-start.48 = (s32[1,5120]{1,0:T(1,128)S(1)}, s32[1,5120]{1,0:T(1,128)}, u32[]{:S(2)}) copy-start(s32[1,5120]{1,0:T(1,128)} %param.23) | copy-start | bytes 61444
  47.4 94.7 %all-gather.15.cloned.1.call-start = ((), (), s32[]{:S(2)}) async-start(), calls=%async_computation.11 | async-start | bytes 1638400 | tf_op jit(solution)/shard_map/all_gather | solution.py:149
  47.4 103.3 %copy-start.52 = (f32[128]{0:T(128)}, f32[128]{0:T(128)S(1)}, u32[]{:S(2)}) copy-start(f32[128]{0:T(128)S(1)} %multiply_exponential_fusion) | copy-start | bytes 1540
  47.4 103.3 %copy-start.40 = (f32[640]{0:T(1024)}, f32[640]{0:T(1024)S(1)}, u32[]{:S(2)}) copy-start(f32[640]{0:T(1024)S(1)} %fusion.87) | copy-start | bytes 7684
  79.5 113.9 %all-gather.11.cloned.1.call-start = ((), (), s32[]{:S(2)}) async-start(), calls=%async_computation.9 | async-start | bytes 2949120 | tf_op jit(solution)/shard_map/all_gather | solution.py:118
  80.1 174.7 %all-gather.19.cloned.1.call-start = ((), (), s32[]{:S(2)}) async-start(), calls=%async_computation.13 | async-start | bytes 2949120 | tf_op jit(solution)/shard_map/all_gather | solution.py:121
  80.7 292.5 %all-reduce.19.cloned.1.call-start = ((), (), s32[]{:S(2)}) async-start(), calls=%async_computation.14 | async-start | bytes 11796480 | tf_op jit(solution)/shard_map/psum | solution.py:186
  108.8 137.3 %collective-permute-start.1 = (bf16[1,2560,256]{2,1,0:T(8,128)(2,1)}, bf16[1,2560,256]{2,1,0:T(8,128)(2,1)}, u32[]{:S(2)}, u32[]{:S(2)}) collective-permute-start(bf16[1,2560,256]{2,1,0:T(8,128)(2,1)} %bitcast.220), channel_id=1, source_target_pairs={{0,16},{1,17},{2,18},{3,19},{4,20},{5,21},{6,22},{7,23},{8,24},{9,... | collective-permute-start | bytes 3932168 | tf_op jit(solution)/shard_map/ppermute | solution.py:19
  142.1 63.7 %collective-permute-start = (bf16[1,2560,256]{1,2,0:T(8,128)(2,1)}, bf16[1,2560,256]{1,2,0:T(8,128)(2,1)}, u32[]{:S(2)}, u32[]{:S(2)}) collective-permute-start(bf16[1,2560,256]{1,2,0:T(8,128)(2,1)} %all-gather.15.cloned.1.call-done), channel_id=1, source_target_pairs={{0,16},{1,17},{2,18},{3,19},{4,20},{5,21},{6,22},{7,23},{8,24},{9,... | collective-permute-start | bytes 3932168 | tf_op jit(solution)/shard_map/ppermute | solution.py:19
  150.7 84.6 %copy-start.2 = (pred[640,4736]{1,0:T(8,128)(4,1)}, pred[640,4736]{1,0:T(8,128)(4,1)S(1)}, u32[]{:S(2)}) copy-start(pred[640,4736]{1,0:T(8,128)(4,1)S(1)} %fusion.4) | copy-start | bytes 9093124
  152.8 49.7 %copy-start.17 = (f32[640,128]{0,1:T(8,128)}, f32[640,128]{0,1:T(8,128)S(1)}, u32[]{:S(2)}) copy-start(f32[640,128]{0,1:T(8,128)S(1)} %get-tuple-element.150) | copy-start | bytes 983044
  220.9 14.4 copy-start.34
  220.9 15.2 copy-start
  236.1 9.9 copy-start.38
  236.1 9.9 copy-start.25
  261.1 300.0 %all-gather.21.cloned.1.call-start = ((), (), s32[]{:S(2)}) async-start(), calls=%async_computation.15 | async-start | bytes 13271040 | tf_op jit(solution)/shard_map/all_gather | solution.py:124
  261.9 114.7 %copy-start.8 = (bf16[1,640,2304]{2,1,0:T(8,128)(2,1)S(1)}, bf16[1,640,2304]{2,1,0:T(8,128)(2,1)}, u32[]{:S(2)}) copy-start(bf16[1,640,2304]{2,1,0:T(8,128)(2,1)} %param.22) | copy-start | bytes 8847364
  261.9 485.1 %all-gather.23.cloned.1.call-start = ((), (), s32[]{:S(2)}) async-start(), calls=%async_computation.16 | async-start | bytes 13271040 | tf_op jit(solution)/shard_map/all_gather | solution.py:125
  262.6 670.0 %all-gather.25.cloned.1.call-start = ((), (), s32[]{:S(2)}) async-start(), calls=%async_computation.17 | async-start | bytes 13271040 | tf_op jit(solution)/shard_map/all_gather | solution.py:126
  263.2 794.4 %all-reduce.21.cloned.1.call-start = ((), (), s32[]{:S(2)}) async-start(), calls=%async_computation.18 | async-start | bytes 11796480 | tf_op jit(solution)/shard_map/psum | solution.py:192
  382.0 364.9 %copy-start.19 = (bf16[640,2304]{1,0:T(8,128)(2,1)}, bf16[640,2304]{1,0:T(8,128)(2,1)S(1)}, u32[]{:S(2)}) copy-start(bf16[640,2304]{1,0:T(8,128)(2,1)S(1)} %multiply_convert_fusion.3) | copy-start | bytes 8847364
  946.0 114.9 %copy-start.10 = (bf16[1,640,2304]{2,1,0:T(8,128)(2,1)S(1)}, bf16[1,640,2304]{2,1,0:T(8,128)(2,1)}, u32[]{:S(2)}) copy-start(bf16[1,640,2304]{2,1,0:T(8,128)(2,1)} %param.35) | copy-start | bytes 8847364
  946.0 281.5 %all-reduce.23.cloned.1.call-start = ((), (), s32[]{:S(2)}) async-start(), calls=%async_computation.19 | async-start | bytes 11796480 | tf_op jit(solution)/shard_map/psum | solution.py:209
  1057.6 8.5 slice-start
  1066.2 23.4 slice-start.4
  1070.5 19.0 copy-start.15
  1070.5 19.0 slice-start.5
  1070.5 19.0 slice-start.6
  1114.1 359.9 %reduce-scatter.28.cloned.1.call-start = ((), (), s32[]{:S(2)}) async-start(), calls=%async_computation.29 | async-start | bytes 1638400
  1227.6 15.2 slice-start.2
  1234.1 8.7 copy-start.45
  1234.1 8.7 slice-start.3
  1275.7 23.9 copy-start.12
  1334.9 32.2 %collective-permute-start.2 = (bf16[1,2560,256]{1,2,0:T(8,128)(2,1)S(1)}, bf16[1,2560,256]{1,2,0:T(8,128)(2,1)S(1)}, u32[]{:S(2)}, u32[]{:S(2)}) collective-permute-start(bf16[1,2560,256]{1,2,0:T(8,128)(2,1)S(1)} %slice.141), channel_id=1, source_target_pairs={{16,0},{17,1},{18,2},{19,3},{20,4},{21,5},{22,6},{23,7},{24,8},{25... | collective-permute-start | bytes 3932168 | tf_op jit(solution)/shard_map/ppermute | solution.py:19
  1370.3 7.2 copy-start.11
  1377.5 107.6 %reduce-scatter.30.cloned.1.call-start = ((), (), s32[]{:S(2)}) async-start(), calls=%async_computation.30 | async-start | bytes 1638400
  1412.6 31.3 %collective-permute-start.3 = (bf16[1,2560,256]{1,2,0:T(8,128)(2,1)S(1)}, bf16[1,2560,256]{1,2,0:T(8,128)(2,1)S(1)}, u32[]{:S(2)}, u32[]{:S(2)}) collective-permute-start(bf16[1,2560,256]{1,2,0:T(8,128)(2,1)S(1)} %slice.140), channel_id=1, source_target_pairs={{16,0},{17,1},{18,2},{19,3},{20,4},{21,5},{22,6},{23,7},{24,8},{25... | collective-permute-start | bytes 3932168 | tf_op jit(solution)/shard_map/ppermute | solution.py:19
  1454.1 85.9 %reduce-scatter.14.cloned.1.call-start = ((), (), s32[]{:S(2)}) async-start(), calls=%async_computation.21 | async-start | bytes 2949120 | tf_op jit(solution)/shard_map/reduce_scatter | solution.py:278
  1454.2 9.1 copy-start.18
  1454.2 9.1 copy-start.23
  1454.2 10.2 copy-start.9
  1454.2 10.2 copy-start.37
  1454.2 10.2 copy-start.47
  1468.1 9.4 copy-start.41
  1468.1 9.4 copy-start.53
  1468.1 116.3 %reduce-scatter.20.cloned.1.call-start = ((), (), s32[]{:S(2)}) async-start(), calls=%async_computation.24 | async-start | bytes 2949120 | tf_op jit(solution)/shard_map/reduce_scatter | solution.py:287
  1473.9 141.9 %reduce-scatter.16.cloned.1.call-start = ((), (), s32[]{:S(2)}) async-start(), calls=%async_computation.22 | async-start | bytes 1474560 | tf_op jit(solution)/shard_map/reduce_scatter | solution.py:281
  1481.4 165.1 %reduce-scatter.18.cloned.1.call-start = ((), (), s32[]{:S(2)}) async-start(), calls=%async_computation.23 | async-start | bytes 1474560 | tf_op jit(solution)/shard_map/reduce_scatter | solution.py:284
  1490.9 336.8 %reduce-scatter.26.cloned.1.call-start = ((), (), s32[]{:S(2)}) async-start(), calls=%async_computation.27 | async-start | bytes 13271040 | tf_op jit(solution)/shard_map/reduce_scatter | solution.py:302
  1504.8 506.4 %reduce-scatter.22.cloned.1.call-start = ((), (), s32[]{:S(2)}) async-start(), calls=%async_computation.25 | async-start | bytes 13271040 | tf_op jit(solution)/shard_map/reduce_scatter | solution.py:296
  1518.5 676.3 %reduce-scatter.24.cloned.1.call-start = ((), (), s32[]{:S(2)}) async-start(), calls=%async_computation.26 | async-start | bytes 13271040 | tf_op jit(solution)/shard_map/reduce_scatter | solution.py:299
  1532.0 732.2 %all-reduce.25.cloned.1.call-start = ((), (), s32[]{:S(2)}) async-start(), calls=%async_computation.20 | async-start | bytes 5898240 | tf_op jit(solution)/shard_map/psum | solution.py:263
  1539.9 957.7 %all-reduce.27.cloned.1.call-start = ((), (), s32[]{:S(2)}) async-start(), calls=%async_computation.31 | async-start | bytes 19464192 | tf_op jit(solution)/shard_map/psum | solution.py:311
  2194.8 73.6 %copy-start.49 = (bf16[2304]{0:T(1024)(128)(2,1)S(1)}, bf16[2304]{0:T(1024)(128)(2,1)}, u32[]{:S(2)}) copy-start(bf16[2304]{0:T(1024)(128)(2,1)} %get-tuple-element.108) | copy-start | bytes 13828
  2194.8 73.6 %copy-start.50 = (bf16[2304]{0:T(1024)(128)(2,1)S(1)}, bf16[2304]{0:T(1024)(128)(2,1)}, u32[]{:S(2)}) copy-start(bf16[2304]{0:T(1024)(128)(2,1)} %get-tuple-element.104) | copy-start | bytes 13828
  2194.8 73.6 %copy-start.51 = (bf16[2304]{0:T(1024)(128)(2,1)S(1)}, bf16[2304]{0:T(1024)(128)(2,1)}, u32[]{:S(2)}) copy-start(bf16[2304]{0:T(1024)(128)(2,1)} %get-tuple-element.106) | copy-start | bytes 13828
  2194.8 100.4 %copy-start.43 = (f32[640]{0:T(1024)S(1)}, f32[640]{0:T(1024)}, u32[]{:S(2)}) copy-start(f32[640]{0:T(1024)} %copy-done.42) | copy-start | bytes 7684
  (24 other events, 84.0 us)
Sparse Core Ops, SparseCore 0:
  9.6 33.8 all-gather.16
  45.0 29.7 all-gather.12
  76.9 31.8 all-gather.26
  110.8 31.2 all-gather.14
  143.5 49.9 all-gather.10
  194.9 49.2 all-gather.18
  261.2 111.9 all-reduce.18
  374.8 186.2 all-gather.20
  562.6 184.2 all-gather.22
  748.3 184.2 all-gather.24
  946.2 111.3 all-reduce.20
  1114.2 113.3 all-reduce.22
  1377.6 30.5 reduce-scatter.27
  1454.2 30.7 reduce-scatter.29
  1487.8 46.8 reduce-scatter.13
  1536.8 47.5 reduce-scatter.19
  1587.1 28.6 reduce-scatter.15
  1618.5 27.8 reduce-scatter.17
  1648.8 178.8 reduce-scatter.25
  1830.0 181.1 reduce-scatter.21
  2013.6 181.1 reduce-scatter.23
  2197.8 66.2 all-reduce.24
  2267.2 230.2 all-reduce.26
where the time goes:
time: 2530 us; the launch traced here: 2520 us
  waiting for transfers between devices  1980 us (78%)
  matrix products  242 us (10%)
  other arithmetic  130 us (5%)
  local copies, waits for them, and re-layouts  94.8 us (4%)
  blocking collectives  45.7 us (2%)
    psum x1, waiting for transfers between devices, shards(): lax.psum(shard_sums[1].astype(jnp.bfloat16), 'seq').astype(jnp.float32)  196 us
    reduce_scatter x1, waiting for transfers between devices, shards(): lax.psum_scatter(dw_up.astype(jnp.bfloat16), 'fsdp', scatter_dimension=0,...  184 us
    reduce_scatter x1, waiting for transfers between devices, shards(): lax.psum_scatter(dw_gate.astype(jnp.bfloat16), 'fsdp', scatter_dimension=...  184 us
    reduce_scatter x1, waiting for transfers between devices, shards(): lax.psum_scatter(dw_down.astype(jnp.bfloat16), 'fsdp', scatter_dimension=...  181 us
    all_gather x1, waiting for transfers between devices, shards(): lax.all_gather(gate_weight, 'fsdp', axis=0, tiled=True)  179 us
    all_gather x1, waiting for transfers between devices, shards(): lax.all_gather(up_weight, 'fsdp', axis=0, tiled=True)  173 us
    all_gather x1, waiting for transfers between devices, shards(): lax.all_gather(down_weight, 'fsdp', axis=1, tiled=True)  171 us
    dot_general x21, matrix products, matmul(): return jnp.dot(left, right, preferred_element_type=jnp.float32)  166 us
  transfers between devices with their start and end apart: 27, of which 22 were waited for; matrix products, arithmetic and copies ran while one was open for 10% of the time, Pallas kernels for 0%

commit v1 on v0

v1 whole, which is shorter than its diff:
```python
import functools
import math

import jax
import jax.numpy as jnp
from jax import lax
from jax.experimental import pallas as pl
from jax.experimental.pallas import tpu as pltpu
from jax.sharding import PartitionSpec as P

HD = 256
WINDOW = 4096
epsilon = 1e-06
soft_cap = 50.0
f32 = jnp.float32
bf16 = jnp.bfloat16


def swap(value, axis, bit=1):
    return lax.ppermute(value, axis, [(i, i ^ bit) for i in range(lax.axis_size(axis))])


def swap_x(value):
    return swap(value, "seq")


def swap_y(value):
    return swap(value, "tensor", 2)


def swap_core(value):
    return swap(value, "tensor", 1)


def swap_z(value):
    return swap(value, "fsdp", 1)


def turn(value):
    size = lax.axis_size("fsdp")
    return lax.ppermute(value, "fsdp", [(i, (i + 1) % size) for i in range(size)])


def gather8(own):
    cut = own.shape[1] // 2
    a, b = own[:, :cut], own[:, cut:]
    a = jnp.stack([a, swap_x(a)])
    b = jnp.stack([b, swap_y(b)])
    a = jnp.stack([a, swap_y(a)])
    b = jnp.stack([b, swap_x(b)], axis=1)
    chip = jnp.concatenate([a, b], axis=-1)
    return jnp.stack([chip, swap_core(chip)]).reshape(8 * own.shape[0], -1)


def send(part, mover):
    return mover(part.astype(bf16)).astype(f32)


def scatter8(part):
    rows, width = part.shape[0] // 8, part.shape[1]
    cut = width // 2
    part = part.reshape(2, 2, 2, rows, width)
    part = part[0] + send(part[1], swap_core)
    a, b = part[..., :cut], part[..., cut:]
    a = a[:, 0] + send(a[:, 1], swap_x)
    b = b[0] + send(b[1], swap_y)
    a = a[0] + send(a[1], swap_y)
    b = b[0] + send(b[1], swap_x)
    return jnp.concatenate([a, b], axis=-1)


def gather16(own):
    cut = own.shape[1] // 3
    a, b, c = own[:, :cut], own[:, cut : 2 * cut], own[:, 2 * cut :]
    a, b, c = (jnp.stack([a, swap_x(a)]), jnp.stack([b, swap_y(b)]), jnp.stack([c, swap_z(c)]))
    a, b, c = (
        jnp.stack([a, swap_y(a)]),
        jnp.stack([b, swap_z(b)]),
        jnp.stack([c, swap_x(c)], axis=1),
    )
    a, b, c = (
        jnp.stack([a, swap_z(a)]),
        jnp.stack([b, swap_x(b)], axis=2),
        jnp.stack([c, swap_y(c)], axis=1),
    )
    chip = jnp.concatenate([a, b, c], axis=-1)
    return jnp.stack([chip, swap_core(chip)]).reshape(16 * own.shape[0], -1)


def scatter16(keep, give):
    rows, width = keep.shape[0] // 8, keep.shape[1]
    cut = width // 3
    part = (keep + send(give, swap_core)).reshape(2, 2, 2, rows, width)
    a, b, c = part[..., :cut], part[..., cut : 2 * cut], part[..., 2 * cut :]
    a = a[0] + send(a[1], swap_z)
    b = b[:, :, 0] + send(b[:, :, 1], swap_x)
    c = c[:, 0] + send(c[:, 1], swap_y)
    a = a[0] + send(a[1], swap_y)
    b = b[0] + send(b[1], swap_z)
    c = c[:, 0] + send(c[:, 1], swap_x)
    a = a[0] + send(a[1], swap_x)
    b = b[0] + send(b[1], swap_y)
    c = c[0] + send(c[1], swap_z)
    return jnp.concatenate([a, b, c], axis=-1)


def rms_norm(field, gain_vec):
    return field * lax.rsqrt(jnp.mean(field * field, axis=-1, keepdims=True) + epsilon) * gain_vec


def norm_back(field, gain_vec, incoming):
    unused, pullback = jax.vjp(rms_norm, field, gain_vec)
    return pullback(incoming)


def tables(positions):
    frequency = jnp.exp(jnp.arange(HD // 2, dtype=f32) * (-2.0 * math.log(10000.0) / HD))
    angles = positions[..., None] * frequency
    return (jnp.cos(angles), jnp.sin(angles))


def rotate(field, cos_tab, sine_tab):
    half_dim = field.shape[-1] // 2
    front, back = field[..., :half_dim], field[..., half_dim:]
    return jnp.concatenate(
        [front * cos_tab - back * sine_tab, back * cos_tab + front * sine_tab], axis=-1
    )


def dot(left, right, dims):
    return lax.dot_general(left, right, (dims, ((), ())), preferred_element_type=f32)


def nn(left, right):
    return dot(left, right, ((1,), (0,)))


def nt(left, right):
    return dot(left, right, ((1,), (1,)))


def tn(left, right):
    return dot(left, right, ((0,), (0,)))


def block_place(info, zs, rows, block):
    x, z = info[0], info[1]
    piece, step = pl.program_id(0), pl.program_id(1)
    home = jnp.where(piece == 0, x, 1 - x) * zs + z
    first = home * rows + step * block
    return x, z, home, first, info[2 + step]


def key_loop(info, zs, rows, block, masked, plain):
    x, z, home, first, first_doc = block_place(info, zs, rows, block)
    last = 2 * zs - 1
    low = jnp.maximum(first - (WINDOW - 1), 0) // rows
    low = jnp.where((home == last) & (first_doc > 0), last, low)

    def visit(g, carry):
        half = (g >= zs).astype(jnp.int32)
        ring = lax.rem(z - (g - half * zs) + zs, zs)
        far = first + block - 1 - g * rows >= WINDOW
        need = (g == home) | far | (home == last)

        @pl.when(need)
        def _():
            masked(x, ring, half, home, g, first)

        @pl.when(jnp.logical_not(need))
        def _():
            plain(x, ring, half, home, g, first)

        return carry

    lax.fori_loop(low, home + 1, visit, 0)


def forward_kernel(zs, rows, block, info, q_ref, kv_ref, col_ref, row_ref, o_ref, lse_ref, acc, tot):
    acc[...] = jnp.zeros_like(acc)
    tot[...] = jnp.zeros_like(tot)
    last = 2 * zs - 1

    def visit(with_mask, x, ring, half, home, g, first):
        raw = nt(q_ref[0], kv_ref[x, ring, half])
        weight = jnp.exp(soft_cap * jnp.tanh(raw * (1.0 / soft_cap)))
        if with_mask:
            row_at = first + lax.broadcasted_iota(jnp.int32, (block, rows), 0)
            col_at = g * rows + lax.broadcasted_iota(jnp.int32, (block, rows), 1)
            gap = row_at - col_at
            row_doc = jnp.where(home == last, col_ref[...], 0)
            col_doc = jnp.where(g == last, row_ref[...], 0)
            weight = jnp.where((gap >= 0) & (gap < WINDOW) & (row_doc == col_doc), weight, 0.0)
        part = weight[:, :128]
        for lane in range(128, rows, 128):
            width = min(128, rows - lane)
            if width < 128:
                tail = jnp.concatenate(
                    [weight[:, lane:], jnp.zeros((block, 128 - width), f32)], axis=1
                )
            else:
                tail = weight[:, lane : lane + 128]
            part = part + tail
        tot[...] += part
        acc[...] += nn(weight.astype(bf16), kv_ref[1 - x, ring, 1 - half])

    key_loop(
        info, zs, rows, block, functools.partial(visit, True), functools.partial(visit, False)
    )
    total = jnp.sum(tot[...], axis=-1, keepdims=True)
    o_ref[0] = (acc[...] / total).astype(bf16)
    lse_ref[0] = jnp.log(total)


def backward_kernel(
    zs, rows, block, info, q_ref, do_ref, lse_ref, delta_ref, kv_ref, col_ref, row_ref, dq_ref, dkv_ref, acc, dkv
):
    piece, step = pl.program_id(0), pl.program_id(1)
    last = 2 * zs - 1

    @pl.when((piece == 0) & (step == 0))
    def _():
        dkv[...] = jnp.zeros_like(dkv)

    acc[...] = jnp.zeros_like(acc)

    def visit(with_mask, x, ring, half, home, g, first):
        q, do = q_ref[0], do_ref[0]
        k, v = kv_ref[x, ring, half], kv_ref[1 - x, ring, 1 - half]
        bent = jnp.tanh(nt(k, q) * (1.0 / soft_cap))
        weight = jnp.exp(soft_cap * bent - lse_ref[0])
        if with_mask:
            row_at = first + lax.broadcasted_iota(jnp.int32, (rows, block), 1)
            col_at = g * rows + lax.broadcasted_iota(jnp.int32, (rows, block), 0)
            gap = row_at - col_at
            row_doc = jnp.where(home == last, row_ref[0], 0)
            col_doc = jnp.where(g == last, col_ref[...], 0)
            weight = jnp.where((gap >= 0) & (gap < WINDOW) & (row_doc == col_doc), weight, 0.0)
        draw = (weight * (nt(v, do) - delta_ref[0]) * (1.0 - bent * bent)).astype(bf16)
        dkv[x, ring, half] += nn(draw, q)
        dkv[1 - x, ring, 1 - half] += nn(weight.astype(bf16), do)
        acc[...] += tn(draw, k)

    key_loop(
        info, zs, rows, block, functools.partial(visit, True), functools.partial(visit, False)
    )
    dq_ref[0] = acc[...]

    @pl.when((piece == 1) & (step == pl.num_programs(1) - 1))
    def _():
        dkv_ref[...] = dkv[...].astype(bf16)


def whole_block(shape):
    return pl.BlockSpec(shape, lambda i, j, info: (0,) * len(shape))


def attend(info, q, kv, doc_col, doc_row, block):
    unused, zs, unused2, rows, unused3 = kv.shape
    steps = rows // block
    return pl.pallas_call(
        functools.partial(forward_kernel, zs, rows, block),
        grid_spec=pltpu.PrefetchScalarGridSpec(
            num_scalar_prefetch=1,
            grid=(2, steps),
            in_specs=[
                pl.BlockSpec((1, block, HD), lambda i, j, info: (i, j, 0)),
                whole_block(kv.shape),
                pl.BlockSpec((block, 1), lambda i, j, info: (j, 0)),
                whole_block((1, rows)),
            ],
            out_specs=[
                pl.BlockSpec((1, block, HD), lambda i, j, info: (i, j, 0)),
                pl.BlockSpec((1, block, 1), lambda i, j, info: (i, j, 0)),
            ],
            scratch_shapes=[pltpu.VMEM((block, HD), f32), pltpu.VMEM((block, 128), f32)],
        ),
        out_shape=[
            jax.ShapeDtypeStruct((2, rows, HD), bf16),
            jax.ShapeDtypeStruct((2, rows, 1), f32),
        ],
        compiler_params=pltpu.CompilerParams(vmem_limit_bytes=48 * 1024 * 1024),
        cost_estimate=pl.CostEstimate(
            flops=4 * 10 * rows * rows * HD, bytes_accessed=8_000_000, transcendentals=20 * rows * rows
        ),
    )(info, q, kv, doc_col, doc_row)


def attend_back(info, q, d_out, lse, delta, kv, doc_col, doc_row, block):
    unused, zs, unused2, rows, unused3 = kv.shape
    steps = rows // block
    piece_block = pl.BlockSpec((1, block, HD), lambda i, j, info: (i, j, 0))
    row_block = pl.BlockSpec((1, 1, block), lambda i, j, info: (i * steps + j, 0, 0))
    return pl.pallas_call(
        functools.partial(backward_kernel, zs, rows, block),
        grid_spec=pltpu.PrefetchScalarGridSpec(
            num_scalar_prefetch=1,
            grid=(2, steps),
            in_specs=[
                piece_block,
                piece_block,
                row_block,
                row_block,
                whole_block(kv.shape),
                whole_block((rows, 1)),
                pl.BlockSpec((1, 1, block), lambda i, j, info: (j, 0, 0)),
            ],
            out_specs=[piece_block, whole_block(kv.shape)],
            scratch_shapes=[pltpu.VMEM((block, HD), f32), pltpu.VMEM(kv.shape, f32)],
        ),
        out_shape=[
            jax.ShapeDtypeStruct((2, rows, HD), f32),
            jax.ShapeDtypeStruct(kv.shape, bf16),
        ],
        compiler_params=pltpu.CompilerParams(vmem_limit_bytes=56 * 1024 * 1024),
        cost_estimate=pl.CostEstimate(
            flops=10 * 10 * rows * rows * HD, bytes_accessed=16_000_000, transcendentals=20 * rows * rows
        ),
    )(info, q, d_out, lse, delta, kv, doc_col, doc_row)


def shards(
    layer_in,
    segment_ids,
    attn_pre_gain,
    query_weight,
    key_weight,
    value_weight,
    out_weight,
    attn_post_gain,
    ffn_pre_gain,
    gate_weight,
    up_weight,
    down_weight,
    ffn_post_gain,
    out_grad,
):
    unused, rows, width = layer_in.shape
    zs, ts = lax.axis_size("fsdp"), lax.axis_size("tensor")
    x, z, t = lax.axis_index("seq"), lax.axis_index("fsdp"), lax.axis_index("tensor")
    b, pair = z % 2, z // 2
    depth = attn_pre_gain.shape[0]
    sub = rows // ts
    quarter = gate_weight.shape[1] // 4
    first = x == 0

    def in_order(parts):
        return jnp.stack(
            [lax.dynamic_index_in_dim(parts, j ^ t, 1, keepdims=False) for j in range(ts)], axis=1
        )

    def to_exchange(pieces):
        parts = in_order(pieces.reshape(2, ts, sub, -1)).reshape(2, 2, 2, sub, -1)
        return parts.transpose(2, 1, 0, 3, 4).reshape(2 * rows, -1)

    def to_sequence(blocks):
        parts = blocks.reshape(2, 2, 2, sub, -1).transpose(2, 1, 0, 3, 4)
        return in_order(parts.reshape(2, ts, sub, -1)).reshape(2, rows, -1)

    gains = jnp.stack([attn_pre_gain, attn_post_gain, ffn_pre_gain, ffn_post_gain])
    all_gains = lax.dynamic_update_slice_in_dim(
        jnp.zeros((zs,) + gains.shape, bf16), gains[None], z, 0
    )
    for j in range(1, zs):
        all_gains = lax.dynamic_update_slice_in_dim(
            all_gains, swap(gains, "fsdp", j)[None], z ^ j, 0
        )
    all_gains = all_gains.transpose(1, 0, 2).reshape(4, width).astype(f32)
    pre_gain, post_gain, mlp_pre, mlp_post = (all_gains[i] for i in range(4))

    own_x = layer_in.reshape(1, ts, sub, width)
    own_x = in_order(own_x)[0].reshape(2, 2, sub, width).transpose(1, 0, 2, 3)
    far_x = swap_x(own_x[0])
    far_x = jnp.stack([far_x, swap_core(far_x)])
    x_rows = jnp.stack([own_x, far_x], axis=2).reshape(2 * rows, width)

    w_qkv = jnp.concatenate(
        [
            lax.dynamic_slice_in_dim(query_weight, x * HD, HD, 1),
            jnp.where(first, key_weight, value_weight),
        ],
        axis=1,
    )
    ring = [w_qkv]
    for unused in range(zs - 1):
        ring.append(turn(ring[-1]))
    w_qkv = jnp.zeros((width, 2 * HD), bf16)
    for i, block in enumerate(ring):
        w_qkv = lax.dynamic_update_slice_in_dim(w_qkv, block, (z - i) % zs * depth, 0)
    w_out = lax.all_gather(
        lax.dynamic_slice_in_dim(out_weight, x * HD, HD, 0).T, "fsdp", axis=0, tiled=True
    )

    def fetch(packs):
        same, other = packs
        whole = jnp.zeros((width, same.shape[1]), bf16)
        for j in range(zs):
            block = same if j == 0 else swap(other if j % 2 else same, "fsdp", j)
            whole = lax.dynamic_update_slice_in_dim(whole, block, (z ^ j) * depth, 0)
        return whole

    def columns(weight, at):
        return lax.dynamic_slice_in_dim(weight, at * quarter, quarter, 1)

    places = (2 * x + b, 2 * x + 1 - b)
    w_gu = fetch(
        [jnp.concatenate([columns(gate_weight, at), columns(up_weight, at)], axis=1) for at in places]
    )
    w_down = fetch(
        [lax.dynamic_slice_in_dim(down_weight, at * quarter, quarter, 0).T for at in places]
    )

    h_one = rms_norm(x_rows.astype(f32), pre_gain).astype(bf16)
    projected = to_sequence(nn(h_one, w_qkv))
    starts = jnp.stack([x * zs + z, (1 - x) * zs + z]) * rows
    positions = starts[:, None] + jnp.arange(rows, dtype=jnp.int32)[None, :]
    cos_tab, sine_tab = tables(positions.astype(f32))
    kv_cos = jnp.where(first, cos_tab, 1.0)
    kv_sine = jnp.where(first, sine_tab, 0.0)
    q_scale = HD ** (-0.5)
    q_cast = (rotate(projected[..., :HD], cos_tab, sine_tab) * q_scale).astype(bf16)
    kv_own = rotate(projected[..., HD:], kv_cos, kv_sine).astype(bf16)
    kv_ring = [kv_own]
    for unused in range(zs - 1):
        kv_ring.append(turn(kv_ring[-1]))
    kv_far = [swap_x(block) for block in kv_ring]
    kv_all = jnp.stack(kv_ring + kv_far).reshape(2, zs, 2, rows, HD)

    block = rows // 2 if rows >= 512 else rows
    last_doc = segment_ids.reshape(2 * zs, rows)[-1]
    info = jnp.concatenate([jnp.stack([x, z]), last_doc[::block]]).astype(jnp.int32)
    doc_col, doc_row = last_doc[:, None], last_doc[None, :]
    mixed, lse = attend(info, q_cast, kv_all, doc_col, doc_row, block)

    o_rows = to_exchange(mixed)
    a_sum = scatter8(nt(o_rows, w_out))

    x_own = lax.dynamic_slice_in_dim(layer_in[0], t * sub, sub, 0).astype(f32)
    r_one = x_own + rms_norm(a_sum, post_gain)
    h_two = gather16(rms_norm(r_one, mlp_pre).astype(bf16))
    gu = nn(h_two, w_gu)
    gate_pre, up_pre = gu[:, :quarter], gu[:, quarter:]
    hidden = (jax.nn.gelu(gate_pre, approximate=True) * up_pre).astype(bf16)
    split = 8 * sub
    m_sum = scatter16(nt(hidden[:split], w_down), nt(hidden[split:], w_down))
    layer_own = (r_one + rms_norm(m_sum, mlp_post)).astype(bf16)
    layer_out = lax.all_gather(layer_own, "tensor", axis=0, tiled=True)[None]

    incoming = lax.dynamic_slice_in_dim(out_grad[0], t * sub, sub, 0).astype(f32)
    d_msum, dg_mlp_post = norm_back(m_sum, mlp_post, incoming)
    dm = gather16(d_msum.astype(bf16))
    d_hidden = nn(dm, w_down)
    unused, gelu_pull = jax.vjp(
        lambda gate_in, up_in: jax.nn.gelu(gate_in, approximate=True) * up_in, gate_pre, up_pre
    )
    d_gate, d_up = gelu_pull(d_hidden)
    d_gu = jnp.concatenate([d_gate.astype(bf16), d_up.astype(bf16)], axis=1)
    dh_two = scatter16(nt(d_gu[:split], w_gu), nt(d_gu[split:], w_gu))
    dw_down = tn(dm, hidden)
    dw_gu = tn(h_two, d_gu)

    dr_add, dg_mlp_pre = norm_back(r_one, mlp_pre, dh_two)
    d_resid = incoming + dr_add
    d_asum, dg_post = norm_back(a_sum, post_gain, d_resid)

    da = gather8(d_asum.astype(bf16))
    d_mixed_rows = nn(da, w_out).astype(bf16)
    d_mixed = to_sequence(d_mixed_rows)
    dw_out = tn(da, o_rows)
    delta = jnp.sum(d_mixed.astype(f32) * mixed.astype(f32), axis=-1)
    steps = rows // block
    d_query, dkv_all = attend_back(
        info,
        q_cast,
        d_mixed,
        lse.reshape(2 * steps, 1, block),
        delta.reshape(2 * steps, 1, block),
        kv_all,
        doc_col,
        doc_row.reshape(steps, 1, block),
        block,
    )
    kept, given = dkv_all[0], dkv_all[1]
    summed = [kept[i].astype(f32) + swap_x(given[i]).astype(f32) for i in range(zs)]
    acc = summed[1] if zs > 1 else summed[0]
    for i in list(range(2, zs)) + [0]:
        acc = send(acc, turn) + summed[i]
    dq_cast = rotate(d_query * q_scale, cos_tab, -sine_tab).astype(bf16)
    dkv_cast = rotate(acc, kv_cos, -kv_sine).astype(bf16)
    d_proj = to_exchange(jnp.concatenate([dq_cast, dkv_cast], axis=-1))
    dh_one = scatter8(nt(d_proj, w_qkv))
    dw_qkv = tn(h_one, d_proj)
    dx_add, dg_pre = norm_back(x_own, pre_gain, dh_one)
    grad_own = (d_resid + dx_add).astype(bf16)
    grad_own = jnp.stack([grad_own, swap_y(grad_own)])
    grad_own = jnp.stack([grad_own, swap_core(grad_own)], axis=1).reshape(1, ts, sub, width)
    input_grad = in_order(grad_own).reshape(1, rows, width).astype(f32)

    def give_back(grad):
        both = 2 * depth
        kept = lax.dynamic_slice_in_dim(grad, pair * both, both, 0)
        for s in range(1, zs // 2):
            part = lax.dynamic_slice_in_dim(grad, (pair ^ s) * both, both, 0)
            kept = kept + swap(part.astype(bf16), "fsdp", 2 * s).astype(f32)
        mine = lax.dynamic_slice_in_dim(kept, b * depth, depth, 0)
        theirs = swap_z(lax.dynamic_slice_in_dim(kept, (1 - b) * depth, depth, 0).astype(bf16))
        far = swap_x(jnp.stack([mine.astype(bf16), theirs]))
        return mine, theirs.astype(f32), far[0].astype(f32), far[1].astype(f32)

    def side_by_side(parts):
        mine, theirs, far_mine, far_theirs = parts
        even = b == 0
        near = jnp.where(
            even, jnp.concatenate([mine, theirs], 1), jnp.concatenate([theirs, mine], 1)
        )
        far = jnp.where(
            even,
            jnp.concatenate([far_mine, far_theirs], 1),
            jnp.concatenate([far_theirs, far_mine], 1),
        )
        return jnp.where(
            first, jnp.concatenate([near, far], 1), jnp.concatenate([far, near], 1)
        )

    g_down = side_by_side(give_back(dw_down)).T
    gu_parts = give_back(dw_gu)
    g_gate = side_by_side([part[:, :quarter] for part in gu_parts])
    g_up = side_by_side([part[:, quarter:] for part in gu_parts])

    def heads(near, far):
        return jnp.where(
            first, jnp.concatenate([near, far], 1), jnp.concatenate([far, near], 1)
        )

    near_out = lax.psum_scatter(dw_out.astype(bf16), "fsdp", scatter_dimension=0, tiled=True)
    g_out = heads(near_out.astype(f32), swap_x(near_out).astype(f32)).T

    def part_of(grad, i):
        return lax.dynamic_slice_in_dim(grad, (z - i) % zs * depth, depth, 0)

    acc = part_of(dw_qkv, 1)
    for i in list(range(2, zs)) + [0]:
        acc = send(acc, turn) + part_of(dw_qkv, i)
    far = swap_x(acc.astype(bf16)).astype(f32)
    g_query = heads(acc[:, :HD], far[:, :HD])
    g_key = jnp.where(first, acc[:, HD:], far[:, HD:])
    g_value = jnp.where(first, far[:, HD:], acc[:, HD:])

    gain_grads = lax.psum(
        jnp.stack([dg_pre, dg_post, dg_mlp_pre, dg_mlp_post]), ("seq", "fsdp", "tensor")
    )
    gain_grads = lax.dynamic_slice_in_dim(gain_grads, z * depth, depth, 1)
    return (
        layer_out,
        input_grad,
        gain_grads[0],
        g_query,
        g_key,
        g_value,
        g_out,
        gain_grads[1],
        gain_grads[2],
        g_gate,
        g_up,
        g_down,
        gain_grads[3],
    )


def solution(mesh):
    return jax.shard_map(
        shards,
        mesh=mesh,
        in_specs=(
            P(None, ("seq", "fsdp"), None),
            P(),
            P("fsdp"),
            P("fsdp", "tensor"),
            P("fsdp", "tensor"),
            P("fsdp", "tensor"),
            P("tensor", "fsdp"),
            P("fsdp"),
            P("fsdp"),
            P("fsdp", "tensor"),
            P("fsdp", "tensor"),
            P("tensor", "fsdp"),
            P("fsdp"),
            P(None, ("seq", "fsdp"), None),
        ),
        out_specs=(
            P(None, ("seq", "fsdp"), None),
            P(None, ("seq", "fsdp"), None),
            P("fsdp"),
            P("fsdp", "tensor"),
            P("fsdp", "tensor"),
            P("fsdp", "tensor"),
            P("tensor", "fsdp"),
            P("fsdp"),
            P("fsdp"),
            P("fsdp", "tensor"),
            P("fsdp", "tensor"),
            P("tensor", "fsdp"),
            P("fsdp"),
        ),
        check_vma=False,
    )
```

time: 2530 us -> 1280 us (0.51)
  waiting for transfers between devices: 1980 us -> 675 us
  starting transfers between devices: 13.2 us -> 149 us
  matrix products: 242 us -> 134 us
  Pallas kernels: 0 us -> 32.4 us
    all_gather x9 -> x2, waiting for transfers between devices: 654 us -> 0.02 us  [the longest x1 0.02 us: shards(): lax.all_gather(lax.dynamic_slice_in_dim(out_weight, x * HD, HD, 0).T, 'fs...]
    reduce_scatter x7 -> x1, waiting for transfers between devices: 655 us -> 20.3 us  [shards(): lax.psum_scatter(dw_out.astype(bf16), 'fsdp', scatter_dimension=0, tiled=...]
    psum x5 -> x0, waiting for transfers between devices: 599 us -> none  [the longest x1 196 us: shards(): lax.psum(shard_sums[1].astype(jnp.bfloat16), 'seq').astype(jnp.float32)]
    ppermute x4 -> x96, waiting for transfers between devices: 60.9 us -> 654 us  [the longest x84 545 us: swap(): lax.ppermute(value, axis, [(i, i ^ bit) for i in range(lax.axis_size(axis...]
    ppermute x4 -> x96, starting transfers between devices: 11.6 us -> 149 us  [the longest x84 130 us: swap(): lax.ppermute(value, axis, [(i, i ^ bit) for i in range(lax.axis_size(axis...]
    dot_general x27 -> x14, matrix products: 242 us -> 134 us  [dot(): lax.dot_general(left, right, (dims, ((), ())), preferred_element_type=f32)]
    convert_element_type x24 -> x22, other arithmetic: 62.9 us -> 22.4 us  [the longest x1 5.59 us: shards(): hidden = (jax.nn.gelu(gate_pre, approximate=True) * up_pre).astype(bf16)]
    unnamed x2 -> x0, blocking collectives: 40.5 us -> none
  transfers between devices with their start and end apart: 27 -> 99, of which waited for: 22 -> 61; matrix products, arithmetic and copies ran while one was open for 10% -> 16% of each run, Pallas kernels for 0% -> 3%
where the time goes in v1:
time: 1280 us
  waiting for transfers between devices  675 us (53%)
  starting transfers between devices  149 us (12%)
  matrix products  134 us (10%)
  other arithmetic  118 us (9%)
  local copies, waits for them, and re-layouts  112 us (9%)
  blocking collectives  39.7 us (3%)
  Pallas kernels  32.4 us (3%)
  between operations  16.2 us (1%)
    ppermute x84, waiting for transfers between devices, swap(): lax.ppermute(value, axis, [(i, i ^ bit) for i in range(lax.axis_size(axis...  545 us
    dot_general x14, matrix products, dot(): lax.dot_general(left, right, (dims, ((), ())), preferred_element_type=f32)  134 us
    ppermute x84, starting transfers between devices, swap(): lax.ppermute(value, axis, [(i, i ^ bit) for i in range(lax.axis_size(axis...  130 us
    ppermute x12, waiting for transfers between devices, turn(): lax.ppermute(value, 'fsdp', [(i, (i + 1) % size) for i in range(size)])  109 us
    psum x1, blocking collectives, shards(): lax.psum(jnp.stack([dg_pre, dg_post, dg_mlp_pre, dg_mlp_post]), ('seq', '...  39.7 us
  transfers between devices with their start and end apart: 99, of which 61 were waited for; matrix products, arithmetic and copies ran while one was open for 16% of the time, Pallas kernels for 3%

profile of v1, /device:TPU:0, one launch (start us, length us, event | category | flops | bytes accessed | tf_op | source)
XLA Modules:
  0.0 1276.6 jit_solution(5782158461478086032)
XLA Ops:
  25.1 21.4 %collective-permute-done = bf16[2,160,2304]{2,1,0:T(8,128)(2,1)} collective-permute-done((bf16[2,160,2304]{2,1,0:T(8,128)(2,1)}, bf16[2,160,2304]{2,1,0:T(8,128)(2,1)}, u32[]{:S(2)}, u32[]{:S(2)}) %collective-permute-start) | collective-permute-done | bytes 1474592 | tf_op jit(solution)/shard_map/ppermute | solution.py:20
  53.9 12.8 %collective-permute-done.6 = bf16[576,512]{1,0:T(8,128)(2,1)S(1)} collective-permute-done((bf16[576,512]{1,0:T(8,128)(2,1)S(1)}, bf16[576,512]{1,0:T(8,128)(2,1)S(1)}, u32[]{:S(2)}, u32[]{:S(2)}) %collective-permute-start.6) | collective-permute-done | bytes 589856 | tf_op jit(solution)/shard_map/ppermute | solution.py:41
  69.4 14.3 %collective-permute-done.7 = bf16[576,512]{1,0:T(8,128)(2,1)S(1)} collective-permute-done((bf16[576,512]{1,0:T(8,128)(2,1)S(1)}, bf16[576,512]{1,0:T(8,128)(2,1)S(1)}, u32[]{:S(2)}, u32[]{:S(2)}) %collective-permute-start.7) | collective-permute-done | bytes 589856 | tf_op jit(solution)/shard_map/ppermute | solution.py:41
  88.6 5.0 fusion.38
  98.0 17.5 %collective-permute-done.8 = bf16[2,640,256]{2,1,0:T(8,128)(2,1)S(1)} collective-permute-done((bf16[2,640,256]{2,1,0:T(8,128)(2,1)S(1)}, bf16[2,640,256]{2,1,0:T(8,128)(2,1)S(1)}, u32[]{:S(2)}, u32[]{:S(2)}) %collective-permute-start.8) | collective-permute-done | bytes 655392 | tf_op jit(solution)/shard_map/ppermute | solution.py:41
  118.6 19.2 %collective-permute-done.9 = bf16[2,640,256]{2,1,0:T(8,128)(2,1)} collective-permute-done((bf16[2,640,256]{2,1,0:T(8,128)(2,1)S(1)}, bf16[2,640,256]{2,1,0:T(8,128)(2,1)}, u32[]{:S(2)}, u32[]{:S(2)}) %collective-permute-start.9) | collective-permute-done | bytes 655392 | tf_op jit(solution)/shard_map/ppermute | solution.py:41
  141.6 23.6 %collective-permute-done.10 = bf16[2,640,256]{2,1,0:T(8,128)(2,1)S(1)} collective-permute-done((bf16[2,640,256]{2,1,0:T(8,128)(2,1)}, bf16[2,640,256]{2,1,0:T(8,128)(2,1)S(1)}, u32[]{:S(2)}, u32[]{:S(2)}) %collective-permute-start.10) | collective-permute-done | bytes 655392 | tf_op jit(solution)/shard_map/ppermute | solution.py:41
  166.5 10.5 collective-permute-done.14
  179.4 11.2 shard_map.237
  195.6 5.0 collective-permute-done.15
  206.8 16.1 %collective-permute-done.16 = bf16[2,160,1152]{2,1,0:T(8,128)(2,1)S(1)} collective-permute-done((bf16[2,160,1152]{2,1,0:T(8,128)(2,1)}, bf16[2,160,1152]{2,1,0:T(8,128)(2,1)S(1)}, u32[]{:S(2)}, u32[]{:S(2)}) %collective-permute-start.16) | collective-permute-done | bytes 737312 | tf_op jit(solution)/shard_map/ppermute | solution.py:20
  227.7 7.3 collective-permute-done.17
  250.6 6.8 collective-permute-done.21
  262.5 16.8 %collective-permute-done.22 = bf16[2,2,160,768]{3,2,1,0:T(8,128)(2,1)S(1)} collective-permute-done((bf16[2,2,160,768]{3,2,1,0:T(8,128)(2,1)S(1)}, bf16[2,2,160,768]{3,2,1,0:T(8,128)(2,1)S(1)}, u32[]{:S(2)}, u32[]{:S(2)}) %collective-permute-start.22) | collective-permute-done | bytes 983072 | tf_op jit(solution)/shard_map/ppermute | solution.py:20
  280.6 4.9 maximum_maximum_fusion
  292.1 4.9 collective-permute-start.34
  307.4 12.1 collective-permute-done.33
  320.4 10.0 collective-permute-done.34
  338.0 62.1 %collective-permute-done.35 = bf16[576,576]{1,0:T(8,128)(2,1)} collective-permute-done((bf16[576,576]{1,0:T(8,128)(2,1)S(1)}, bf16[576,576]{1,0:T(8,128)(2,1)}, u32[]{:S(2)}, u32[]{:S(2)}) %collective-permute-start.35) | collective-permute-done | bytes 663584 | tf_op jit(solution)/shard_map/ppermute | solution.py:20
  404.7 26.8 %collective-permute-done.31 = bf16[576,1152]{1,0:T(8,128)(2,1)} collective-permute-done((bf16[576,1152]{1,0:T(8,128)(2,1)}, bf16[576,1152]{1,0:T(8,128)(2,1)}, u32[]{:S(2)}, u32[]{:S(2)}) %collective-permute-start.31) | collective-permute-done | bytes 1327136 | tf_op jit(solution)/shard_map/ppermute | solution.py:20
  437.0 4.6 pad_maximum_fusion
  441.6 5.2 copy.123
  446.8 21.3 %fusion.183 = f32[2560,1152]{0,1:T(8,128)} fusion(bf16[2560,2304]{1,0:T(8,128)(2,1)} %bitcast.492, bf16[2304,1152]{1,0:T(8,128)(2,1)} %constant_dynamic-update-slice_fusion.4), kind=kOutput, calls=%fused_computation.455 | convolution fusion | flops 13589544960 | bytes 28901376 | tf_op jit(solution)/shard_map/dot_general | solution.py:131
  468.2 5.6 multiply_convert_fusion.1
  473.8 5.3 convolution_convert_fusion.1
  479.2 9.6 collective-permute-done.36
  488.8 4.8 convolution_add_fusion
  494.8 41.9 %collective-permute-start.37 = (bf16[2,2,160,768]{3,2,1,0:T(8,128)(2,1)}, bf16[2,2,160,768]{3,2,1,0:T(8,128)(2,1)}, u32[]{:S(2)}, u32[]{:S(2)}) collective-permute-start(bf16[2,2,160,768]{3,2,1,0:T(8,128)(2,1)} %slice_bitcast_fusion.21), channel_id=1, source_target_pairs={{0,4},{4,0},{8,12},{12,8},{1,5},{5,1},{9,13},{13,9},{2,6},{6,2},{1... | collective-permute-start | bytes 2949128 | tf_op jit(solution)/shard_map/ppermute | solution.py:20
  540.6 18.5 %collective-permute-done.37 = bf16[2,2,160,768]{3,2,1,0:T(8,128)(2,1)} collective-permute-done((bf16[2,2,160,768]{3,2,1,0:T(8,128)(2,1)}, bf16[2,2,160,768]{3,2,1,0:T(8,128)(2,1)}, u32[]{:S(2)}, u32[]{:S(2)}) %collective-permute-start.37) | collective-permute-done | bytes 983072 | tf_op jit(solution)/shard_map/ppermute | solution.py:20
  569.9 4.0 collective-permute-done.38
  579.0 4.6 collective-permute-done.44
  593.9 7.4 collective-permute-done.46
  604.4 8.0 collective-permute-done.47
  618.7 13.2 %collective-permute-done.48 = bf16[2,2,160,768]{3,2,1,0:T(8,128)(2,1)S(1)} collective-permute-done((bf16[2,2,160,768]{3,2,1,0:T(8,128)(2,1)S(1)}, bf16[2,2,160,768]{3,2,1,0:T(8,128)(2,1)S(1)}, u32[]{:S(2)}, u32[]{:S(2)}) %collective-permute-start.48) | collective-permute-done | bytes 983072 | tf_op jit(solution)/shard_map/ppermute | solution.py:20
  633.6 9.1 collective-permute-done.55
  643.9 5.2 copy.131
  649.0 19.3 %multiply_convert_fusion = (bf16[2560,576]{0,1:T(8,128)(2,1)}, bf16[2560,576]{0,1:T(8,128)(2,1)}) fusion(f32[2560,1152]{0,1:T(8,128)} %fusion.183, bf16[2560,2304]{1,0:T(8,128)(2,1)} %bitcast.494, bf16[2304,576]{1,0:T(8,128)(2,1)} %constant_dynamic-update-slice_fusion), kind=kOutput, calls=%fused_computation.36 | convolution fusion | flops 6830161920 | bytes 32145408 | tf_op jit(solution)/shard_map/dot_general | solution.py:131
  668.3 12.7 convolution_convert_fusion
  682.8 22.2 %fusion.3 = f32[2304,1152]{1,0:T(8,128)} fusion(bf16[2560,2304]{1,0:T(8,128)(2,1)} %bitcast.493, bf16[2560,576]{0,1:T(8,128)(2,1)} %get-tuple-element.50, bf16[2560,576]{0,1:T(8,128)(2,1)} %get-tuple-element.51), kind=kOutput, calls=%fused_computation.19 | convolution fusion | flops 13601341440 | bytes 28311552 | tf_op jit(solution)/shard_map/dot_general | solution.py:131
  705.0 14.7 %convolution_add_fusion.1 = f32[1280,2304]{1,0:T(8,128)} fusion(bf16[2304,1152]{1,0:T(8,128)(2,1)} %constant_dynamic-update-slice_fusion.4, bf16[1280,2304]{1,0:T(8,128)(2,1)} %collective-permute-done.56, bf16[2560,576]{0,1:T(8,128)(2,1)} %get-tuple-element.51, bf16[2560,576]{0,1:T(8,128)(2,1)} %get-tuple-element.50), kind=kOutput, calls=%fused_computation.3 | convolution fusion | flops 6806568960 | bytes 28901376 | tf_op jit(solution)/shard_map/dot_general | solution.py:131
  723.1 10.8 fusion.185
  742.1 10.1 collective-permute-done.57
  758.5 7.2 collective-permute-done.63
  766.1 8.5 collective-permute-done.58
  775.1 8.5 collective-permute-done.61
  791.3 12.5 collective-permute-done.65
  809.7 4.3 dynamic-slice_convert_fusion
  831.9 10.5 collective-permute-done.67
  849.7 44.2 %collective-permute-done.94 = bf16[576,576]{1,0:T(8,128)(2,1)S(1)} collective-permute-done((bf16[576,576]{1,0:T(8,128)(2,1)}, bf16[576,576]{1,0:T(8,128)(2,1)S(1)}, u32[]{:S(2)}, u32[]{:S(2)}) %collective-permute-start.94) | collective-permute-done | bytes 663584 | tf_op jit(solution)/shard_map/ppermute | solution.py:20
  897.2 40.0 %collective-permute-done.90 = bf16[1152,1152]{1,0:T(8,128)(2,1)} collective-permute-done((bf16[1152,1152]{1,0:T(8,128)(2,1)}, bf16[1152,1152]{1,0:T(8,128)(2,1)}, u32[]{:S(2)}, u32[]{:S(2)}) %collective-permute-start.90) | collective-permute-done | bytes 2654240 | tf_op jit(solution)/shard_map/ppermute | solution.py:20
  953.9 21.3 %shard_map.238 = (f32[2,640,256]{2,1,0:T(8,128)}, bf16[2,4,2,640,256]{4,3,2,1,0:T(8,128)(2,1)}) custom-call(s32[4]{0:T(128)} %copy-done.6, bf16[2,640,256]{2,1,0:T(8,128)(2,1)} %copy-done.4, bf16[2,640,256]{2,1,0:T(8,128)(2,1)} %bitcast.547, f32[4,1,320]{2,1,0:T(1,128)} %reshape.678.lse_ref, f32[4,1,320]{2,1,0:T(1,128)} %reshape.656.delta_ref, ...), custom_call_target="tpu_custom_call" | custom-call | flops 10485760000 | bytes 16000000 | tf_op jit(solution)/shard_map/pallas_call | solution.py:294
  982.0 12.9 %collective-permute-done.71 = bf16[2,640,256]{2,1,0:T(8,128)(2,1)S(1)} collective-permute-done((bf16[2,640,256]{2,1,0:T(8,128)(2,1)S(1)}, bf16[2,640,256]{2,1,0:T(8,128)(2,1)S(1)}, u32[]{:S(2)}, u32[]{:S(2)}) %collective-permute-start.71) | collective-permute-done | bytes 655392 | tf_op jit(solution)/shard_map/ppermute | solution.py:20
  995.0 6.4 collective-permute-start.72
  1006.0 59.8 %collective-permute-done.73 = bf16[2,640,256]{2,1,0:T(8,128)(2,1)S(1)} collective-permute-done((bf16[2,640,256]{2,1,0:T(8,128)(2,1)S(1)}, bf16[2,640,256]{2,1,0:T(8,128)(2,1)S(1)}, u32[]{:S(2)}, u32[]{:S(2)}) %collective-permute-start.73) | collective-permute-done | bytes 655392 | tf_op jit(solution)/shard_map/ppermute | solution.py:20
  1066.1 6.4 collective-permute-start.74
  1079.8 8.1 collective-permute-done.74
  1092.3 12.0 collective-permute-done.76
  1108.2 4.9 fusion.184
  1121.6 4.7 fusion.19
  1146.4 20.3 %reduce-scatter.2.cloned.1.call-done = bf16[576,256]{1,0:T(8,128)(2,1)} async-done(((bf16[2304,256]{1,0:T(8,128)(2,1)}), bf16[576,256]{1,0:T(8,128)(2,1)}) %reduce-scatter.2.cloned.1.call-update) | async-done | bytes 294928 | tf_op jit(solution)/shard_map/reduce_scatter | solution.py:535
  1174.2 7.7 collective-permute-done.80
  1190.7 11.2 collective-permute-done.83
  1210.7 8.8 collective-permute-done.88
  1222.2 39.7 %psum.7 = f32[4,2304]{1,0:T(4,128)S(1)} all-reduce(f32[4,2304]{1,0:T(4,128)S(1)} %pad_maximum_fusion.39), channel_id=1, replica_groups=mesh['seq'=2,'fsdp'=4,'tensor'=4] {'seq','fsdp','tensor'}, use_global_device_ids=true, to_apply=%region_14.15 | all-reduce | flops 9216 | bytes 73728 | tf_op jit(solution)/shard_map/psum | solution.py:549
  (610 shorter events, 334.2 us)
Async XLA Ops:
  7.2 184.5 %all-gather.3.cloned.1.call-start = ((), (), s32[]{:S(2)}) async-start(), calls=%async_computation.1 | async-start | bytes 1474560 | tf_op jit(solution)/shard_map/all_gather | solution.py:390
  10.9 35.5 %collective-permute-start = (bf16[2,160,2304]{2,1,0:T(8,128)(2,1)}, bf16[2,160,2304]{2,1,0:T(8,128)(2,1)}, u32[]{:S(2)}, u32[]{:S(2)}) collective-permute-start(bf16[2,160,2304]{2,1,0:T(8,128)(2,1)} %slice_bitcast_fusion.7), channel_id=1, source_target_pairs={{0,16},{16,0},{1,17},{17,1},{2,18},{18,2},{3,19},{19,3},{4,20},{20... | collective-permute-start | bytes 4423688 | tf_op jit(solution)/shard_map/ppermute | solution.py:20
  17.6 31.2 %collective-permute-start.5 = (bf16[576,512]{1,0:T(8,128)(2,1)}, bf16[576,512]{1,0:T(8,128)(2,1)S(1)}, u32[]{:S(2)}, u32[]{:S(2)}) collective-permute-start(bf16[576,512]{1,0:T(8,128)(2,1)} %get-tuple-element.152), channel_id=1, source_target_pairs={{0,4},{4,8},{8,12},{12,0},{1,5},{5,9},{9,13},{13,1},{2,6},{6,10},{... | collective-permute-start | bytes 1769480 | tf_op jit(solution)/shard_map/ppermute | solution.py:41
  20.5 30.2 %collective-permute-start.2 = (bf16[4,576]{1,0:T(4,128)(2,1)}, bf16[4,576]{1,0:T(4,128)(2,1)}, u32[]{:S(2)}, u32[]{:S(2)}) collective-permute-start(bf16[4,576]{1,0:T(4,128)(2,1)} %get-tuple-element.49), channel_id=1, source_target_pairs={{0,4},{4,0},{8,12},{12,8},{1,5},{5,1},{9,13},{13,9},{2,6},{6,2},{1... | collective-permute-start | bytes 13832 | tf_op jit(solution)/shard_map/ppermute | solution.py:20
  22.1 29.9 %collective-permute-start.3 = (bf16[4,576]{1,0:T(4,128)(2,1)}, bf16[4,576]{1,0:T(4,128)(2,1)}, u32[]{:S(2)}, u32[]{:S(2)}) collective-permute-start(bf16[4,576]{1,0:T(4,128)(2,1)} %get-tuple-element.49), channel_id=1, source_target_pairs={{0,8},{4,12},{8,0},{12,4},{1,9},{5,13},{9,1},{13,5},{2,10},{6,14},... | collective-permute-start | bytes 13832 | tf_op jit(solution)/shard_map/ppermute | solution.py:20
  23.3 29.9 %collective-permute-start.4 = (bf16[4,576]{1,0:T(4,128)(2,1)}, bf16[4,576]{1,0:T(4,128)(2,1)S(1)}, u32[]{:S(2)}, u32[]{:S(2)}) collective-permute-start(bf16[4,576]{1,0:T(4,128)(2,1)} %get-tuple-element.49), channel_id=1, source_target_pairs={{0,12},{4,8},{8,4},{12,0},{1,13},{5,9},{9,5},{13,1},{2,14},{6,10},... | collective-permute-start | bytes 13832 | tf_op jit(solution)/shard_map/ppermute | solution.py:20
  46.5 38.1 %collective-permute-start.1 = (bf16[2,160,2304]{2,1,0:T(8,128)(2,1)}, bf16[2,160,2304]{2,1,0:T(8,128)(2,1)}, u32[]{:S(2)}, u32[]{:S(2)}) collective-permute-start(bf16[2,160,2304]{2,1,0:T(8,128)(2,1)} %collective-permute-done), channel_id=1, source_target_pairs={{0,1},{1,0},{2,3},{3,2},{4,5},{5,4},{6,7},{7,6},{8,9},{9,8},{10,11... | collective-permute-start | bytes 4423688 | tf_op jit(solution)/shard_map/ppermute | solution.py:20
  48.9 17.9 %collective-permute-start.6 = (bf16[576,512]{1,0:T(8,128)(2,1)S(1)}, bf16[576,512]{1,0:T(8,128)(2,1)S(1)}, u32[]{:S(2)}, u32[]{:S(2)}) collective-permute-start(bf16[576,512]{1,0:T(8,128)(2,1)S(1)} %collective-permute-done.5), channel_id=1, source_target_pairs={{0,4},{4,8},{8,12},{12,0},{1,5},{5,9},{9,13},{13,1},{2,6},{6,10},{... | collective-permute-start | bytes 1769480 | tf_op jit(solution)/shard_map/ppermute | solution.py:41
  66.7 17.0 %collective-permute-start.7 = (bf16[576,512]{1,0:T(8,128)(2,1)S(1)}, bf16[576,512]{1,0:T(8,128)(2,1)S(1)}, u32[]{:S(2)}, u32[]{:S(2)}) collective-permute-start(bf16[576,512]{1,0:T(8,128)(2,1)S(1)} %collective-permute-done.6), channel_id=1, source_target_pairs={{0,4},{4,8},{8,12},{12,0},{1,5},{5,9},{9,13},{13,1},{2,6},{6,10},{... | collective-permute-start | bytes 1769480 | tf_op jit(solution)/shard_map/ppermute | solution.py:41
  98.0 17.6 %collective-permute-start.8 = (bf16[2,640,256]{2,1,0:T(8,128)(2,1)S(1)}, bf16[2,640,256]{2,1,0:T(8,128)(2,1)S(1)}, u32[]{:S(2)}, u32[]{:S(2)}) collective-permute-start(bf16[2,640,256]{2,1,0:T(8,128)(2,1)S(1)} %pad_maximum_fusion.29), channel_id=1, source_target_pairs={{0,4},{4,8},{8,12},{12,0},{1,5},{5,9},{9,13},{13,1},{2,6},{6,10},{... | collective-permute-start | bytes 1966088 | tf_op jit(solution)/shard_map/ppermute | solution.py:41
  115.5 22.4 %collective-permute-start.9 = (bf16[2,640,256]{2,1,0:T(8,128)(2,1)S(1)}, bf16[2,640,256]{2,1,0:T(8,128)(2,1)}, u32[]{:S(2)}, u32[]{:S(2)}) collective-permute-start(bf16[2,640,256]{2,1,0:T(8,128)(2,1)S(1)} %collective-permute-done.8), channel_id=1, source_target_pairs={{0,4},{4,8},{8,12},{12,0},{1,5},{5,9},{9,13},{13,1},{2,6},{6,10},{... | collective-permute-start | bytes 1966088 | tf_op jit(solution)/shard_map/ppermute | solution.py:41
  116.3 731.9 %all-gather.5.cloned.1.call-start = ((), (), s32[]{:S(2)}) async-start(), calls=%async_computation.2 | async-start | bytes 3686400 | tf_op jit(solution)/shard_map/all_gather | solution.py:447
  117.4 48.9 %collective-permute-start.11 = (bf16[2,640,256]{2,1,0:T(8,128)(2,1)}, bf16[2,640,256]{2,1,0:T(8,128)(2,1)S(1)}, u32[]{:S(2)}, u32[]{:S(2)}) collective-permute-start(bf16[2,640,256]{2,1,0:T(8,128)(2,1)} %copy-done.64), channel_id=1, source_target_pairs={{0,16},{16,0},{1,17},{17,1},{2,18},{18,2},{3,19},{19,3},{4,20},{20... | collective-permute-start | bytes 1966088 | tf_op jit(solution)/shard_map/ppermute | solution.py:20
  137.9 27.3 %collective-permute-start.10 = (bf16[2,640,256]{2,1,0:T(8,128)(2,1)}, bf16[2,640,256]{2,1,0:T(8,128)(2,1)S(1)}, u32[]{:S(2)}, u32[]{:S(2)}) collective-permute-start(bf16[2,640,256]{2,1,0:T(8,128)(2,1)} %collective-permute-done.9), channel_id=1, source_target_pairs={{0,4},{4,8},{8,12},{12,0},{1,5},{5,9},{9,13},{13,1},{2,6},{6,10},{... | collective-permute-start | bytes 1966088 | tf_op jit(solution)/shard_map/ppermute | solution.py:41
  138.2 28.1 %collective-permute-start.12 = (bf16[2,640,256]{2,1,0:T(8,128)(2,1)S(1)}, bf16[2,640,256]{2,1,0:T(8,128)(2,1)S(1)}, u32[]{:S(2)}, u32[]{:S(2)}) collective-permute-start(bf16[2,640,256]{2,1,0:T(8,128)(2,1)S(1)} %collective-permute-done.8), channel_id=1, source_target_pairs={{0,16},{16,0},{1,17},{17,1},{2,18},{18,2},{3,19},{19,3},{4,20},{20... | collective-permute-start | bytes 1966088 | tf_op jit(solution)/shard_map/ppermute | solution.py:20
  138.3 28.1 %collective-permute-start.13 = (bf16[2,640,256]{2,1,0:T(8,128)(2,1)}, bf16[2,640,256]{2,1,0:T(8,128)(2,1)S(1)}, u32[]{:S(2)}, u32[]{:S(2)}) collective-permute-start(bf16[2,640,256]{2,1,0:T(8,128)(2,1)} %collective-permute-done.9), channel_id=1, source_target_pairs={{0,16},{16,0},{1,17},{17,1},{2,18},{18,2},{3,19},{19,3},{4,20},{20... | collective-permute-start | bytes 1966088 | tf_op jit(solution)/shard_map/ppermute | solution.py:20
  204.0 18.8 %collective-permute-start.16 = (bf16[2,160,1152]{2,1,0:T(8,128)(2,1)}, bf16[2,160,1152]{2,1,0:T(8,128)(2,1)S(1)}, u32[]{:S(2)}, u32[]{:S(2)}) collective-permute-start(bf16[2,160,1152]{2,1,0:T(8,128)(2,1)} %slice_bitcast_fusion.31), channel_id=1, source_target_pairs={{0,16},{16,0},{1,17},{17,1},{2,18},{18,2},{3,19},{19,3},{4,20},{20... | collective-permute-start | bytes 2211848 | tf_op jit(solution)/shard_map/ppermute | solution.py:20
  205.1 18.2 %collective-permute-start.18 = (bf16[2,160,1152]{2,1,0:T(8,128)(2,1)S(1)}, bf16[2,160,1152]{2,1,0:T(8,128)(2,1)S(1)}, u32[]{:S(2)}, u32[]{:S(2)}) collective-permute-start(bf16[2,160,1152]{2,1,0:T(8,128)(2,1)S(1)} %slice_bitcast_fusion.29), channel_id=1, source_target_pairs={{0,2},{1,3},{2,0},{3,1},{4,6},{5,7},{6,4},{7,5},{8,10},{9,11},{10,... | collective-permute-start | bytes 2211848 | tf_op jit(solution)/shard_map/ppermute | solution.py:20
  257.6 21.7 %collective-permute-start.22 = (bf16[2,2,160,768]{3,2,1,0:T(8,128)(2,1)S(1)}, bf16[2,2,160,768]{3,2,1,0:T(8,128)(2,1)S(1)}, u32[]{:S(2)}, u32[]{:S(2)}) collective-permute-start(bf16[2,2,160,768]{3,2,1,0:T(8,128)(2,1)S(1)} %get-tuple-element.119), channel_id=1, source_target_pairs={{0,4},{4,0},{8,12},{12,8},{1,5},{5,1},{9,13},{13,9},{2,6},{6,2},{1... | collective-permute-start | bytes 2949128 | tf_op jit(solution)/shard_map/ppermute | solution.py:20
  259.1 20.2 %collective-permute-start.25 = (bf16[2,2,160,768]{3,2,0,1:T(8,128)(2,1)S(1)}, bf16[2,2,160,768]{3,2,0,1:T(8,128)(2,1)S(1)}, u32[]{:S(2)}, u32[]{:S(2)}) collective-permute-start(bf16[2,2,160,768]{3,2,0,1:T(8,128)(2,1)S(1)} %get-tuple-element.121), channel_id=1, source_target_pairs={{0,16},{16,0},{1,17},{17,1},{2,18},{18,2},{3,19},{19,3},{4,20},{20... | collective-permute-start | bytes 2949128 | tf_op jit(solution)/shard_map/ppermute | solution.py:20
  259.9 20.7 %collective-permute-start.28 = (bf16[2,2,160,768]{3,2,0,1:T(8,128)(2,1)S(1)}, bf16[2,2,160,768]{3,2,0,1:T(8,128)(2,1)S(1)}, u32[]{:S(2)}, u32[]{:S(2)}) collective-permute-start(bf16[2,2,160,768]{3,2,0,1:T(8,128)(2,1)S(1)} %get-tuple-element.123), channel_id=1, source_target_pairs={{0,2},{1,3},{2,0},{3,1},{4,6},{5,7},{6,4},{7,5},{8,10},{9,11},{10,... | collective-permute-start | bytes 2949128 | tf_op jit(solution)/shard_map/ppermute | solution.py:20
  285.6 151.4 %collective-permute-start.29 = (bf16[2,2,2,160,2304]{4,3,0,2,1:T(8,128)(2,1)}, bf16[2,2,2,160,2304]{4,3,0,2,1:T(8,128)(2,1)}, u32[]{:S(2)}, u32[]{:S(2)}) collective-permute-start(bf16[2,2,2,160,2304]{4,3,0,2,1:T(8,128)(2,1)} %maximum_maximum_fusion), channel_id=1, source_target_pairs={{0,1},{1,0},{2,3},{3,2},{4,5},{5,4},{6,7},{7,6},{8,9},{9,8},{10,11... | collective-permute-start | bytes 17694728 | tf_op jit(solution)/shard_map/ppermute | solution.py:20
  287.2 32.3 %collective-permute-start.33 = (bf16[576,576]{1,0:T(8,128)(2,1)S(1)}, bf16[576,576]{1,0:T(8,128)(2,1)}, u32[]{:S(2)}, u32[]{:S(2)}) collective-permute-start(bf16[576,576]{1,0:T(8,128)(2,1)S(1)} %dynamic-slice_bitcast_fusion), channel_id=1, source_target_pairs={{0,4},{4,0},{8,12},{12,8},{1,5},{5,1},{9,13},{13,9},{2,6},{6,2},{1... | collective-permute-start | bytes 1990664 | tf_op jit(solution)/shard_map/ppermute | solution.py:20
  292.1 38.3 %collective-permute-start.34 = (bf16[576,576]{1,0:T(8,128)(2,1)S(1)}, bf16[576,576]{1,0:T(8,128)(2,1)}, u32[]{:S(2)}, u32[]{:S(2)}) collective-permute-start(bf16[576,576]{1,0:T(8,128)(2,1)S(1)} %get-tuple-element.47), channel_id=1, source_target_pairs={{0,8},{4,12},{8,0},{12,4},{1,9},{5,13},{9,1},{13,5},{2,10},{6,14},... | collective-permute-start | bytes 1990664 | tf_op jit(solution)/shard_map/ppermute | solution.py:20
  301.6 100.5 %collective-permute-start.30 = (bf16[576,1152]{1,0:T(8,128)(2,1)}, bf16[576,1152]{1,0:T(8,128)(2,1)}, u32[]{:S(2)}, u32[]{:S(2)}) collective-permute-start(bf16[576,1152]{1,0:T(8,128)(2,1)} %pad_maximum_fusion.18), channel_id=1, source_target_pairs={{0,4},{4,0},{8,12},{12,8},{1,5},{5,1},{9,13},{13,9},{2,6},{6,2},{1... | collective-permute-start | bytes 3981320 | tf_op jit(solution)/shard_map/ppermute | solution.py:20
  307.4 124.1 %collective-permute-start.31 = (bf16[576,1152]{1,0:T(8,128)(2,1)}, bf16[576,1152]{1,0:T(8,128)(2,1)}, u32[]{:S(2)}, u32[]{:S(2)}) collective-permute-start(bf16[576,1152]{1,0:T(8,128)(2,1)} %get-tuple-element.43), channel_id=1, source_target_pairs={{0,8},{4,12},{8,0},{12,4},{1,9},{5,13},{9,1},{13,5},{2,10},{6,14},... | collective-permute-start | bytes 3981320 | tf_op jit(solution)/shard_map/ppermute | solution.py:20
  319.5 80.5 %collective-permute-start.35 = (bf16[576,576]{1,0:T(8,128)(2,1)S(1)}, bf16[576,576]{1,0:T(8,128)(2,1)}, u32[]{:S(2)}, u32[]{:S(2)}) collective-permute-start(bf16[576,576]{1,0:T(8,128)(2,1)S(1)} %dynamic-slice_bitcast_fusion), channel_id=1, source_target_pairs={{0,12},{4,8},{8,4},{12,0},{1,13},{5,9},{9,5},{13,1},{2,14},{6,10},... | collective-permute-start | bytes 1990664 | tf_op jit(solution)/shard_map/ppermute | solution.py:20
  330.4 103.5 %collective-permute-start.32 = (bf16[576,1152]{1,0:T(8,128)(2,1)}, bf16[576,1152]{1,0:T(8,128)(2,1)}, u32[]{:S(2)}, u32[]{:S(2)}) collective-permute-start(bf16[576,1152]{1,0:T(8,128)(2,1)} %pad_maximum_fusion.18), channel_id=1, source_target_pairs={{0,12},{4,8},{8,4},{12,0},{1,13},{5,9},{9,5},{13,1},{2,14},{6,10},... | collective-permute-start | bytes 3981320 | tf_op jit(solution)/shard_map/ppermute | solution.py:20
  494.8 64.3 %collective-permute-start.37 = (bf16[2,2,160,768]{3,2,1,0:T(8,128)(2,1)}, bf16[2,2,160,768]{3,2,1,0:T(8,128)(2,1)}, u32[]{:S(2)}, u32[]{:S(2)}) collective-permute-start(bf16[2,2,160,768]{3,2,1,0:T(8,128)(2,1)} %slice_bitcast_fusion.21), channel_id=1, source_target_pairs={{0,4},{4,0},{8,12},{12,8},{1,5},{5,1},{9,13},{13,9},{2,6},{6,2},{1... | collective-permute-start | bytes 2949128 | tf_op jit(solution)/shard_map/ppermute | solution.py:20
  537.7 24.0 %collective-permute-start.40 = (bf16[2,2,160,768]{3,2,0,1:T(8,128)(2,1)}, bf16[2,2,160,768]{3,2,0,1:T(8,128)(2,1)}, u32[]{:S(2)}, u32[]{:S(2)}) collective-permute-start(bf16[2,2,160,768]{3,2,0,1:T(8,128)(2,1)} %slice_bitcast_fusion.19), channel_id=1, source_target_pairs={{0,16},{16,0},{1,17},{17,1},{2,18},{18,2},{3,19},{19,3},{4,20},{20... | collective-permute-start | bytes 2949128 | tf_op jit(solution)/shard_map/ppermute | solution.py:20
  539.9 27.6 %collective-permute-start.43 = (bf16[2,2,160,768]{3,2,0,1:T(8,128)(2,1)S(1)}, bf16[2,2,160,768]{3,2,0,1:T(8,128)(2,1)S(1)}, u32[]{:S(2)}, u32[]{:S(2)}) collective-permute-start(bf16[2,2,160,768]{3,2,0,1:T(8,128)(2,1)S(1)} %slice_bitcast_fusion.17), channel_id=1, source_target_pairs={{0,2},{1,3},{2,0},{3,1},{4,6},{5,7},{6,4},{7,5},{8,10},{9,11},{10,... | collective-permute-start | bytes 2949128 | tf_op jit(solution)/shard_map/ppermute | solution.py:20
  612.5 19.4 %collective-permute-start.48 = (bf16[2,2,160,768]{3,2,1,0:T(8,128)(2,1)S(1)}, bf16[2,2,160,768]{3,2,1,0:T(8,128)(2,1)S(1)}, u32[]{:S(2)}, u32[]{:S(2)}) collective-permute-start(bf16[2,2,160,768]{3,2,1,0:T(8,128)(2,1)S(1)} %get-tuple-element.113), channel_id=1, source_target_pairs={{0,4},{4,0},{8,12},{12,8},{1,5},{5,1},{9,13},{13,9},{2,6},{6,2},{1... | collective-permute-start | bytes 2949128 | tf_op jit(solution)/shard_map/ppermute | solution.py:20
  615.7 16.8 %collective-permute-start.51 = (bf16[2,2,160,768]{3,2,0,1:T(8,128)(2,1)S(1)}, bf16[2,2,160,768]{3,2,0,1:T(8,128)(2,1)S(1)}, u32[]{:S(2)}, u32[]{:S(2)}) collective-permute-start(bf16[2,2,160,768]{3,2,0,1:T(8,128)(2,1)S(1)} %get-tuple-element.115), channel_id=1, source_target_pairs={{0,16},{16,0},{1,17},{17,1},{2,18},{18,2},{3,19},{19,3},{4,20},{20... | collective-permute-start | bytes 2949128 | tf_op jit(solution)/shard_map/ppermute | solution.py:20
  681.0 24.0 %collective-permute-start.56 = (bf16[1280,2304]{1,0:T(8,128)(2,1)}, bf16[1280,2304]{1,0:T(8,128)(2,1)}, u32[]{:S(2)}, u32[]{:S(2)}) collective-permute-start(bf16[1280,2304]{1,0:T(8,128)(2,1)} %convolution_convert_fusion), channel_id=1, source_target_pairs={{0,1},{1,0},{2,3},{3,2},{4,5},{5,4},{6,7},{7,6},{8,9},{9,8},{10,11... | collective-permute-start | bytes 17694728 | tf_op jit(solution)/shard_map/ppermute | solution.py:20
  682.8 483.9 %reduce-scatter.2.cloned.1.call-start = ((), (), s32[]{:S(2)}) async-start(), calls=%async_computation.3 | async-start | bytes 1474560 | tf_op jit(solution)/shard_map/reduce_scatter | solution.py:535
  721.6 30.6 %collective-permute-start.57 = (bf16[2,2,160,768]{3,2,0,1:T(8,128)(2,1)S(1)}, bf16[2,2,160,768]{3,2,0,1:T(8,128)(2,1)S(1)}, u32[]{:S(2)}, u32[]{:S(2)}) collective-permute-start(bf16[2,2,160,768]{3,2,0,1:T(8,128)(2,1)S(1)} %slice_bitcast_fusion.15), channel_id=1, source_target_pairs={{0,4},{4,0},{8,12},{12,8},{1,5},{5,1},{9,13},{13,9},{2,6},{6,2},{1... | collective-permute-start | bytes 2949128 | tf_op jit(solution)/shard_map/ppermute | solution.py:20
  734.1 23.8 %collective-permute-start.60 = (bf16[2,2,160,768]{3,2,1,0:T(8,128)(2,1)S(1)}, bf16[2,2,160,768]{3,2,1,0:T(8,128)(2,1)S(1)}, u32[]{:S(2)}, u32[]{:S(2)}) collective-permute-start(bf16[2,2,160,768]{3,2,1,0:T(8,128)(2,1)S(1)} %slice_bitcast_fusion.13), channel_id=1, source_target_pairs={{0,16},{16,0},{1,17},{17,1},{2,18},{18,2},{3,19},{19,3},{4,20},{20... | collective-permute-start | bytes 2949128 | tf_op jit(solution)/shard_map/ppermute | solution.py:20
  738.1 83.2 %collective-permute-start.93 = (bf16[1152,576]{0,1:T(8,128)(2,1)}, bf16[1152,576]{0,1:T(8,128)(2,1)}, u32[]{:S(2)}, u32[]{:S(2)}) collective-permute-start(bf16[1152,576]{0,1:T(8,128)(2,1)} %dynamic-slice_convert_fusion.1), channel_id=1, source_target_pairs={{0,8},{4,12},{8,0},{12,4},{1,9},{5,13},{9,1},{13,5},{2,10},{6,14},... | collective-permute-start | bytes 3981320 | tf_op jit(solution)/shard_map/ppermute | solution.py:20
  741.0 24.8 %collective-permute-start.63 = (bf16[2,2,160,768]{3,2,0,1:T(8,128)(2,1)S(1)}, bf16[2,2,160,768]{3,2,0,1:T(8,128)(2,1)S(1)}, u32[]{:S(2)}, u32[]{:S(2)}) collective-permute-start(bf16[2,2,160,768]{3,2,0,1:T(8,128)(2,1)S(1)} %slice_bitcast_fusion.11), channel_id=1, source_target_pairs={{0,2},{1,3},{2,0},{3,1},{4,6},{5,7},{6,4},{7,5},{8,10},{9,11},{10,... | collective-permute-start | bytes 2949128 | tf_op jit(solution)/shard_map/ppermute | solution.py:20
  752.5 22.1 %collective-permute-start.58 = (bf16[2,160,768]{2,1,0:T(8,128)(2,1)S(1)}, bf16[2,160,768]{2,1,0:T(8,128)(2,1)S(1)}, u32[]{:S(2)}, u32[]{:S(2)}) collective-permute-start(bf16[2,160,768]{2,1,0:T(8,128)(2,1)S(1)} %fusion.129), channel_id=1, source_target_pairs={{0,2},{1,3},{2,0},{3,1},{4,6},{5,7},{6,4},{7,5},{8,10},{9,11},{10,... | collective-permute-start | bytes 1474568 | tf_op jit(solution)/shard_map/ppermute | solution.py:20
  758.1 25.5 %collective-permute-start.61 = (bf16[2,160,768]{2,1,0:T(8,128)(2,1)S(1)}, bf16[2,160,768]{2,1,0:T(8,128)(2,1)S(1)}, u32[]{:S(2)}, u32[]{:S(2)}) collective-permute-start(bf16[2,160,768]{2,1,0:T(8,128)(2,1)S(1)} %fusion.130), channel_id=1, source_target_pairs={{0,4},{4,0},{8,12},{12,8},{1,5},{5,1},{9,13},{13,9},{2,6},{6,2},{1... | collective-permute-start | bytes 1474568 | tf_op jit(solution)/shard_map/ppermute | solution.py:20
  766.0 18.9 %collective-permute-start.64 = (bf16[2,160,768]{2,1,0:T(8,128)(2,1)S(1)}, bf16[2,160,768]{2,1,0:T(8,128)(2,1)S(1)}, u32[]{:S(2)}, u32[]{:S(2)}) collective-permute-start(bf16[2,160,768]{2,1,0:T(8,128)(2,1)S(1)} %fusion.131), channel_id=1, source_target_pairs={{0,16},{16,0},{1,17},{17,1},{2,18},{18,2},{3,19},{19,3},{4,20},{20... | collective-permute-start | bytes 1474568 | tf_op jit(solution)/shard_map/ppermute | solution.py:20
  785.1 18.7 %collective-permute-start.65 = (bf16[160,768]{1,0:T(8,128)(2,1)S(1)}, bf16[160,768]{1,0:T(8,128)(2,1)S(1)}, u32[]{:S(2)}, u32[]{:S(2)}) collective-permute-start(bf16[160,768]{1,0:T(8,128)(2,1)S(1)} %fusion.147), channel_id=1, source_target_pairs={{0,4},{4,0},{8,12},{12,8},{1,5},{5,1},{9,13},{13,9},{2,6},{6,2},{1... | collective-permute-start | bytes 737288 | tf_op jit(solution)/shard_map/ppermute | solution.py:20
  820.1 117.0 %collective-permute-start.90 = (bf16[1152,1152]{1,0:T(8,128)(2,1)}, bf16[1152,1152]{1,0:T(8,128)(2,1)}, u32[]{:S(2)}, u32[]{:S(2)}) collective-permute-start(bf16[1152,1152]{1,0:T(8,128)(2,1)} %dynamic-slice_convert_fusion), channel_id=1, source_target_pairs={{0,8},{4,12},{8,0},{12,4},{1,9},{5,13},{9,1},{13,5},{2,10},{6,14},... | collective-permute-start | bytes 7962632 | tf_op jit(solution)/shard_map/ppermute | solution.py:20
  824.8 17.6 %collective-permute-start.67 = (bf16[2,160,1152]{2,1,0:T(8,128)(2,1)S(1)}, bf16[2,160,1152]{2,1,0:T(8,128)(2,1)S(1)}, u32[]{:S(2)}, u32[]{:S(2)}) collective-permute-start(bf16[2,160,1152]{2,1,0:T(8,128)(2,1)S(1)} %get-tuple-element.125), channel_id=1, source_target_pairs={{0,2},{1,3},{2,0},{3,1},{4,6},{5,7},{6,4},{7,5},{8,10},{9,11},{10,... | collective-permute-start | bytes 2211848 | tf_op jit(solution)/shard_map/ppermute | solution.py:20
  827.1 17.4 %collective-permute-start.69 = (bf16[2,160,1152]{2,1,0:T(8,128)(2,1)S(1)}, bf16[2,160,1152]{2,1,0:T(8,128)(2,1)S(1)}, u32[]{:S(2)}, u32[]{:S(2)}) collective-permute-start(bf16[2,160,1152]{2,1,0:T(8,128)(2,1)S(1)} %get-tuple-element.131), channel_id=1, source_target_pairs={{0,16},{16,0},{1,17},{17,1},{2,18},{18,2},{3,19},{19,3},{4,20},{20... | collective-permute-start | bytes 2211848 | tf_op jit(solution)/shard_map/ppermute | solution.py:20
  829.4 64.4 %collective-permute-start.94 = (bf16[576,576]{1,0:T(8,128)(2,1)}, bf16[576,576]{1,0:T(8,128)(2,1)S(1)}, u32[]{:S(2)}, u32[]{:S(2)}) collective-permute-start(bf16[576,576]{1,0:T(8,128)(2,1)} %dynamic-slice_convert_fusion.4), channel_id=1, source_target_pairs={{0,4},{4,0},{8,12},{12,8},{1,5},{5,1},{9,13},{13,9},{2,6},{6,2},{1... | collective-permute-start | bytes 1990664 | tf_op jit(solution)/shard_map/ppermute | solution.py:20
  847.4 99.0 %collective-permute-start.70 = (bf16[2,2,160,2304]{3,2,1,0:T(8,128)(2,1)}, bf16[2,2,160,2304]{3,2,1,0:T(8,128)(2,1)}, u32[]{:S(2)}, u32[]{:S(2)}) collective-permute-start(bf16[2,2,160,2304]{3,2,1,0:T(8,128)(2,1)} %get-tuple-element.70), channel_id=1, source_target_pairs={{0,1},{1,0},{2,3},{3,2},{4,5},{5,4},{6,7},{7,6},{8,9},{9,8},{10,11... | collective-permute-start | bytes 8847368 | tf_op jit(solution)/shard_map/ppermute | solution.py:20
  894.1 50.6 %collective-permute-start.95 = (bf16[2,576,576]{2,1,0:T(8,128)(2,1)S(1)}, bf16[2,576,576]{2,1,0:T(8,128)(2,1)S(1)}, u32[]{:S(2)}, u32[]{:S(2)}) collective-permute-start(bf16[2,576,576]{2,1,0:T(8,128)(2,1)S(1)} %pad_maximum_fusion.16), channel_id=1, source_target_pairs={{0,16},{16,0},{1,17},{17,1},{2,18},{18,2},{3,19},{19,3},{4,20},{20... | collective-permute-start | bytes 3981320 | tf_op jit(solution)/shard_map/ppermute | solution.py:20
  942.6 35.5 %collective-permute-start.91 = (bf16[576,1152]{1,0:T(8,128)(2,1)}, bf16[576,1152]{1,0:T(8,128)(2,1)S(1)}, u32[]{:S(2)}, u32[]{:S(2)}) collective-permute-start(bf16[576,1152]{1,0:T(8,128)(2,1)} %get-tuple-element.59), channel_id=1, source_target_pairs={{0,4},{4,0},{8,12},{12,8},{1,5},{5,1},{9,13},{13,9},{2,6},{6,2},{1... | collective-permute-start | bytes 3981320 | tf_op jit(solution)/shard_map/ppermute | solution.py:20
  977.1 17.7 %collective-permute-start.71 = (bf16[2,640,256]{2,1,0:T(8,128)(2,1)S(1)}, bf16[2,640,256]{2,1,0:T(8,128)(2,1)S(1)}, u32[]{:S(2)}, u32[]{:S(2)}) collective-permute-start(bf16[2,640,256]{2,1,0:T(8,128)(2,1)S(1)} %get-tuple-element.60), channel_id=1, source_target_pairs={{0,16},{16,0},{1,17},{17,1},{2,18},{18,2},{3,19},{19,3},{4,20},{20... | collective-permute-start | bytes 1966088 | tf_op jit(solution)/shard_map/ppermute | solution.py:20
  978.4 111.9 %collective-permute-start.92 = (bf16[2,576,1152]{2,1,0:T(8,128)(2,1)S(1)}, bf16[2,576,1152]{2,1,0:T(8,128)(2,1)S(1)}, u32[]{:S(2)}, u32[]{:S(2)}) collective-permute-start(bf16[2,576,1152]{2,1,0:T(8,128)(2,1)S(1)} %pad_maximum_fusion.9), channel_id=1, source_target_pairs={{0,16},{16,0},{1,17},{17,1},{2,18},{18,2},{3,19},{19,3},{4,20},{20... | collective-permute-start | bytes 7962632 | tf_op jit(solution)/shard_map/ppermute | solution.py:20
  980.8 84.9 %collective-permute-start.73 = (bf16[2,640,256]{2,1,0:T(8,128)(2,1)S(1)}, bf16[2,640,256]{2,1,0:T(8,128)(2,1)S(1)}, u32[]{:S(2)}, u32[]{:S(2)}) collective-permute-start(bf16[2,640,256]{2,1,0:T(8,128)(2,1)S(1)} %get-tuple-element.63), channel_id=1, source_target_pairs={{0,16},{16,0},{1,17},{17,1},{2,18},{18,2},{3,19},{19,3},{4,20},{20... | collective-permute-start | bytes 1966088 | tf_op jit(solution)/shard_map/ppermute | solution.py:20
  995.0 70.7 %collective-permute-start.72 = (bf16[2,640,256]{2,1,0:T(8,128)(2,1)S(1)}, bf16[2,640,256]{2,1,0:T(8,128)(2,1)S(1)}, u32[]{:S(2)}, u32[]{:S(2)}) collective-permute-start(bf16[2,640,256]{2,1,0:T(8,128)(2,1)S(1)} %fusion.76), channel_id=1, source_target_pairs={{0,4},{4,8},{8,12},{12,0},{1,5},{5,9},{9,13},{13,1},{2,6},{6,10},{... | collective-permute-start | bytes 1966088 | tf_op jit(solution)/shard_map/ppermute | solution.py:41
  1004.9 74.9 %collective-permute-start.75 = (bf16[2,640,256]{2,1,0:T(8,128)(2,1)S(1)}, bf16[2,640,256]{2,1,0:T(8,128)(2,1)S(1)}, u32[]{:S(2)}, u32[]{:S(2)}) collective-permute-start(bf16[2,640,256]{2,1,0:T(8,128)(2,1)S(1)} %get-tuple-element.62), channel_id=1, source_target_pairs={{0,16},{16,0},{1,17},{17,1},{2,18},{18,2},{3,19},{19,3},{4,20},{20... | collective-permute-start | bytes 1966088 | tf_op jit(solution)/shard_map/ppermute | solution.py:20
  1066.1 21.8 %collective-permute-start.74 = (bf16[2,640,256]{2,1,0:T(8,128)(2,1)S(1)}, bf16[2,640,256]{2,1,0:T(8,128)(2,1)S(1)}, u32[]{:S(2)}, u32[]{:S(2)}) collective-permute-start(bf16[2,640,256]{2,1,0:T(8,128)(2,1)S(1)} %fusion.75), channel_id=1, source_target_pairs={{0,4},{4,8},{8,12},{12,0},{1,5},{5,9},{9,13},{13,1},{2,6},{6,10},{... | collective-permute-start | bytes 1966088 | tf_op jit(solution)/shard_map/ppermute | solution.py:41
  1115.3 18.7 %collective-permute-start.78 = (bf16[2,2,160,2304]{3,2,1,0:T(8,128)(2,1)}, bf16[2,2,160,2304]{3,2,1,0:T(8,128)(2,1)}, u32[]{:S(2)}, u32[]{:S(2)}) collective-permute-start(bf16[2,2,160,2304]{3,2,1,0:T(8,128)(2,1)} %bitcast.177), channel_id=1, source_target_pairs={{0,1},{1,0},{2,3},{3,2},{4,5},{5,4},{6,7},{7,6},{8,9},{9,8},{10,11... | collective-permute-start | bytes 8847368 | tf_op jit(solution)/shard_map/ppermute | solution.py:20
  1133.8 34.3 %collective-permute-start.85 = (bf16[576,512]{1,0:T(8,128)(2,1)}, bf16[576,512]{1,0:T(8,128)(2,1)}, u32[]{:S(2)}, u32[]{:S(2)}) collective-permute-start(bf16[576,512]{1,0:T(8,128)(2,1)} %dynamic-slice_convert_fusion.5), channel_id=1, source_target_pairs={{0,4},{4,8},{8,12},{12,0},{1,5},{5,9},{9,13},{13,1},{2,6},{6,10},{... | collective-permute-start | bytes 1769480 | tf_op jit(solution)/shard_map/ppermute | solution.py:41
  1141.8 28.0 %collective-permute-start.79 = (bf16[2,160,1152]{2,1,0:T(8,128)(2,1)}, bf16[2,160,1152]{2,1,0:T(8,128)(2,1)S(1)}, u32[]{:S(2)}, u32[]{:S(2)}) collective-permute-start(bf16[2,160,1152]{2,1,0:T(8,128)(2,1)} %slice_bitcast_fusion.27), channel_id=1, source_target_pairs={{0,16},{16,0},{1,17},{17,1},{2,18},{18,2},{3,19},{19,3},{4,20},{20... | collective-permute-start | bytes 2211848 | tf_op jit(solution)/shard_map/ppermute | solution.py:20
  1142.3 27.5 %collective-permute-start.81 = (bf16[2,160,1152]{2,1,0:T(8,128)(2,1)}, bf16[2,160,1152]{2,1,0:T(8,128)(2,1)S(1)}, u32[]{:S(2)}, u32[]{:S(2)}) collective-permute-start(bf16[2,160,1152]{2,1,0:T(8,128)(2,1)} %slice_bitcast_fusion.25), channel_id=1, source_target_pairs={{0,2},{1,3},{2,0},{3,1},{4,6},{5,7},{6,4},{7,5},{8,10},{9,11},{10,... | collective-permute-start | bytes 2211848 | tf_op jit(solution)/shard_map/ppermute | solution.py:20
  1166.6 42.9 %collective-permute-start.89 = (bf16[576,256]{1,0:T(8,128)(2,1)}, bf16[576,256]{1,0:T(8,128)(2,1)S(1)}, u32[]{:S(2)}, u32[]{:S(2)}) collective-permute-start(bf16[576,256]{1,0:T(8,128)(2,1)} %reduce-scatter.2.cloned.1.call-done), channel_id=1, source_target_pairs={{0,16},{16,0},{1,17},{17,1},{2,18},{18,2},{3,19},{19,3},{4,20},{20... | collective-permute-start | bytes 884744 | tf_op jit(solution)/shard_map/ppermute | solution.py:20
  1169.7 16.5 %collective-permute-start.86 = (bf16[576,512]{1,0:T(8,128)(2,1)S(1)}, bf16[576,512]{1,0:T(8,128)(2,1)S(1)}, u32[]{:S(2)}, u32[]{:S(2)}) collective-permute-start(bf16[576,512]{1,0:T(8,128)(2,1)S(1)} %add_convert_fusion.2), channel_id=1, source_target_pairs={{0,4},{4,8},{8,12},{12,0},{1,5},{5,9},{9,13},{13,1},{2,6},{6,10},{... | collective-permute-start | bytes 1769480 | tf_op jit(solution)/shard_map/ppermute | solution.py:41
  1184.6 17.3 %collective-permute-start.83 = (bf16[160,2304]{1,0:T(8,128)(2,1)S(1)}, bf16[160,2304]{1,0:T(8,128)(2,1)S(1)}, u32[]{:S(2)}, u32[]{:S(2)}) collective-permute-start(bf16[160,2304]{1,0:T(8,128)(2,1)S(1)} %fusion.52), channel_id=1, source_target_pairs={{0,2},{1,3},{2,0},{3,1},{4,6},{5,7},{6,4},{7,5},{8,10},{9,11},{10,... | collective-permute-start | bytes 2211848 | tf_op jit(solution)/shard_map/ppermute | solution.py:20
  1202.2 60.4 %collective-permute-start.84 = (bf16[2,160,2304]{2,1,0:T(8,128)(2,1)S(1)}, bf16[2,160,2304]{2,1,0:T(8,128)(2,1)}, u32[]{:S(2)}, u32[]{:S(2)}) collective-permute-start(bf16[2,160,2304]{2,1,0:T(8,128)(2,1)S(1)} %get-tuple-element.100), channel_id=1, source_target_pairs={{0,1},{1,0},{2,3},{3,2},{4,5},{5,4},{6,7},{7,6},{8,9},{9,8},{10,11... | collective-permute-start | bytes 4423688 | tf_op jit(solution)/shard_map/ppermute | solution.py:20
  (141 other events, 1762.6 us)
Sparse Core Ops, SparseCore 0:
  116.4 47.2 all-gather.2
  682.9 27.7 all-gather.4
  1126.5 40.1 reduce-scatter.1

commit v2 on v1

--- a/solution.py
+++ b/solution.py
@@ -5,6 +5,7 @@
 import jax.numpy as jnp
 from jax import lax
 from jax.experimental import pallas as pl
+from jax.experimental.layout import Layout, with_layout_constraint
 from jax.experimental.pallas import tpu as pltpu
 from jax.sharding import PartitionSpec as P
 
@@ -32,23 +33,39 @@
     return swap(value, "tensor", 1)
 
 
-def swap_z(value):
-    return swap(value, "fsdp", 1)
-
-
 def turn(value):
     size = lax.axis_size("fsdp")
     return lax.ppermute(value, "fsdp", [(i, (i + 1) % size) for i in range(size)])
 
 
-def gather8(own):
+class Move:
+    def __init__(self, value, mover):
+        self.value, self.mover, self.result = value, mover, None
+
+
+def step(values, begin=(), end=()):
+    values, given, taken = lax.optimization_barrier(
+        (list(values), [move.value for move in begin], [move.result for move in end])
+    )
+    for move, value in zip(begin, given):
+        move.value, move.result = value, move.mover(value)
+    for move, result in zip(end, taken):
+        move.result = result
+    return values
+
+
+def at(plan, place, values):
+    return step(values, *plan[place]) if place in plan else step(values)
+
+
+def gather8(own, plan):
     cut = own.shape[1] // 2
-    a, b = own[:, :cut], own[:, cut:]
-    a = jnp.stack([a, swap_x(a)])
-    b = jnp.stack([b, swap_y(b)])
-    a = jnp.stack([a, swap_y(a)])
-    b = jnp.stack([b, swap_x(b)], axis=1)
+    a, b = at(plan, 0, [own[:, :cut], own[:, cut:]])
+    a, b = jnp.stack([a, swap_x(a)]), jnp.stack([b, swap_y(b)])
+    a, b = at(plan, 1, [a, b])
+    a, b = jnp.stack([a, swap_y(a)]), jnp.stack([b, swap_x(b)], axis=1)
     chip = jnp.concatenate([a, b], axis=-1)
+    (chip,) = at(plan, 2, [chip])
     return jnp.stack([chip, swap_core(chip)]).reshape(8 * own.shape[0], -1)
 
 
@@ -56,52 +73,20 @@
     return mover(part.astype(bf16)).astype(f32)
 
 
-def scatter8(part):
-    rows, width = part.shape[0] // 8, part.shape[1]
+def scatter8(keep, give, plan):
+    (given,) = at(plan, 0, [give()])
+    part = keep(swap_core(given))
+    rows, width = part.shape[0] // 4, part.shape[1]
     cut = width // 2
-    part = part.reshape(2, 2, 2, rows, width)
-    part = part[0] + send(part[1], swap_core)
+    part = part.reshape(2, 2, rows, width)
     a, b = part[..., :cut], part[..., cut:]
-    a = a[:, 0] + send(a[:, 1], swap_x)
-    b = b[0] + send(b[1], swap_y)
-    a = a[0] + send(a[1], swap_y)
-    b = b[0] + send(b[1], swap_x)
+    give_a, give_b = at(plan, 1, [a[:, 1].astype(bf16), b[1].astype(bf16)])
+    a = a[:, 0] + swap_x(give_a).astype(f32)
+    b = b[0] + swap_y(give_b).astype(f32)
+    give_a, give_b = at(plan, 2, [a[1].astype(bf16), b[1].astype(bf16)])
+    a = a[0] + swap_y(give_a).astype(f32)
+    b = b[0] + swap_x(give_b).astype(f32)
     return jnp.concatenate([a, b], axis=-1)
-
-
-def gather16(own):
-    cut = own.shape[1] // 3
-    a, b, c = own[:, :cut], own[:, cut : 2 * cut], own[:, 2 * cut :]
-    a, b, c = (jnp.stack([a, swap_x(a)]), jnp.stack([b, swap_y(b)]), jnp.stack([c, swap_z(c)]))
-    a, b, c = (
-        jnp.stack([a, swap_y(a)]),
-        jnp.stack([b, swap_z(b)]),
-        jnp.stack([c, swap_x(c)], axis=1),
-    )
-    a, b, c = (
-        jnp.stack([a, swap_z(a)]),
-        jnp.stack([b, swap_x(b)], axis=2),
-        jnp.stack([c, swap_y(c)], axis=1),
-    )
-    chip = jnp.concatenate([a, b, c], axis=-1)
-    return jnp.stack([chip, swap_core(chip)]).reshape(16 * own.shape[0], -1)
-
-
-def scatter16(keep, give):
-    rows, width = keep.shape[0] // 8, keep.shape[1]
-    cut = width // 3
-    part = (keep + send(give, swap_core)).reshape(2, 2, 2, rows, width)
-    a, b, c = part[..., :cut], part[..., cut : 2 * cut], part[..., 2 * cut :]
-    a = a[0] + send(a[1], swap_z)
-    b = b[:, :, 0] + send(b[:, :, 1], swap_x)
-    c = c[:, 0] + send(c[:, 1], swap_y)
-    a = a[0] + send(a[1], swap_y)
-    b = b[0] + send(b[1], swap_z)
-    c = c[:, 0] + send(c[:, 1], swap_x)
-    a = a[0] + send(a[1], swap_x)
-    b = b[0] + send(b[1], swap_y)
-    c = c[0] + send(c[1], swap_z)
-    return jnp.concatenate([a, b, c], axis=-1)
 
 
 def rms_norm(field, gain_vec):
@@ -141,6 +126,9 @@
 
 def tn(left, right):
     return dot(left, right, ((0,), (0,)))
+
+
+LIGHT = pl.CostEstimate(flops=500_000_000, bytes_accessed=1_000_000, transcendentals=0)
 
 
 def block_place(info, zs, rows, block):
@@ -280,9 +268,7 @@
             jax.ShapeDtypeStruct((2, rows, 1), f32),
         ],
         compiler_params=pltpu.CompilerParams(vmem_limit_bytes=48 * 1024 * 1024),
-        cost_estimate=pl.CostEstimate(
-            flops=4 * 10 * rows * rows * HD, bytes_accessed=8_000_000, transcendentals=20 * rows * rows
-        ),
+        cost_estimate=LIGHT,
     )(info, q, kv, doc_col, doc_row)
 
 
@@ -313,10 +299,132 @@
             jax.ShapeDtypeStruct(kv.shape, bf16),
         ],
         compiler_params=pltpu.CompilerParams(vmem_limit_bytes=56 * 1024 * 1024),
-        cost_estimate=pl.CostEstimate(
-            flops=10 * 10 * rows * rows * HD, bytes_accessed=16_000_000, transcendentals=20 * rows * rows
-        ),
+        cost_estimate=LIGHT,
     )(info, q, d_out, lse, delta, kv, doc_col, doc_row)
+
+
+NN, NT, TN = ((1,), (0,)), ((1,), (1,)), ((0,), (0,))
+gelu_slope = math.sqrt(2.0 / math.pi)
+
+
+def held(shape):
+    return pl.BlockSpec(shape, lambda i: (0,) * len(shape), pipeline_mode=pl.Buffered(1))
+
+
+def row_tiles(tile, columns):
+    return pl.BlockSpec((tile, columns), lambda i: (i, 0))
+
+
+def tiled(body, rows, tile, in_specs, out_columns, out_types, operands):
+    return pl.pallas_call(
+        body,
+        grid=(rows // tile,),
+        in_specs=in_specs,
+        out_specs=[row_tiles(tile, columns) for columns in out_columns],
+        out_shape=[
+            jax.ShapeDtypeStruct((rows, columns), kind)
+            for columns, kind in zip(out_columns, out_types)
+        ],
+        compiler_params=pltpu.CompilerParams(vmem_limit_bytes=52 * 1024 * 1024),
+        cost_estimate=LIGHT,
+    )(*operands)
+
+
+def product_kernel(dims, count, *refs):
+    value = dot(refs[0][...], refs[count][...], dims)
+    for i in range(1, count):
+        value = value + dot(refs[i][...], refs[count + i][...], dims)
+    for added in refs[2 * count : -1]:
+        value = value + added[...].astype(f32)
+    refs[-1][...] = value.astype(refs[-1].dtype)
+
+
+def rows_product(lefts, rights, dims, kind, *added):
+    lefts, rights = [v if isinstance(v, (list, tuple)) else [v] for v in (lefts, rights)]
+    rows = lefts[0].shape[0]
+    tile = min(rows, 320)
+    columns = rights[0].shape[1 - dims[1][0]]
+    specs = [row_tiles(tile, left.shape[1]) for left in lefts]
+    specs += [held(right.shape) for right in rights]
+    specs += [row_tiles(tile, columns)] * len(added)
+    body = functools.partial(product_kernel, dims, len(lefts))
+    return tiled(body, rows, tile, specs, [columns], [kind], [*lefts, *rights, *added])[0]
+
+
+def halves(rows_in):
+    return jnp.split(rows_in, 2)
+
+
+def norm_product_kernel(x_ref, gain_ref, w_ref, h_ref, out_ref):
+    field = x_ref[...].astype(f32)
+    scale = lax.rsqrt(jnp.mean(field * field, axis=-1, keepdims=True) + epsilon)
+    h = (field * scale * gain_ref[...]).astype(bf16)
+    h_ref[...] = h
+    out_ref[...] = dot(h, w_ref[...], NN)
+
+
+def norm_product(rows_in, gain, right):
+    rows, columns = rows_in.shape
+    tile = min(rows, 320)
+    specs = [row_tiles(tile, columns), held((1, columns)), held(right.shape)]
+    operands = (rows_in, gain[None], right)
+    outs, kinds = [columns, right.shape[1]], [bf16, f32]
+    return tiled(norm_product_kernel, rows, tile, specs, outs, kinds, operands)
+
+
+def bend(gate):
+    return jnp.tanh(gelu_slope * (gate + 0.044715 * (gate * gate * gate)))
+
+
+def gated_kernel(h_ref, gate_w, up_w, gate_ref, up_ref, hidden_ref):
+    gate = dot(h_ref[...], gate_w[...], NN)
+    up = dot(h_ref[...], up_w[...], NN)
+    gate_ref[...] = gate
+    up_ref[...] = up
+    hidden_ref[...] = (0.5 * gate * (1.0 + bend(gate)) * up).astype(bf16)
+
+
+def gated_product(left, gate_w, up_w):
+    rows, depth = left.shape
+    tile, columns = min(rows, 160), gate_w.shape[1]
+    specs = [row_tiles(tile, depth), held(gate_w.shape), held(up_w.shape)]
+    outs, kinds = [columns] * 3, [f32, f32, bf16]
+    return tiled(gated_kernel, rows, tile, specs, outs, kinds, (left, gate_w, up_w))
+
+
+def gated_back_kernel(dm_ref, w_ref, gate_ref, up_ref, d_gate_ref, d_up_ref):
+    d_hidden = dot(dm_ref[...], w_ref[...], NN)
+    gate, up = gate_ref[...], up_ref[...]
+    bent = bend(gate)
+    share = 0.5 * (1.0 + bent)
+    slope = share + 0.5 * gate * (1.0 - bent * bent) * gelu_slope * (
+        1.0 + 3.0 * 0.044715 * (gate * gate)
+    )
+    d_gate_ref[...] = (d_hidden * up * slope).astype(bf16)
+    d_up_ref[...] = (d_hidden * gate * share).astype(bf16)
+
+
+def gated_back(left, right, gate, up):
+    rows, depth = left.shape
+    tile, columns = min(rows, 160), gate.shape[1]
+    specs = [row_tiles(tile, depth), held(right.shape)] + [row_tiles(tile, columns)] * 2
+    outs, kinds = [columns] * 2, [bf16] * 2
+    return tiled(gated_back_kernel, rows, tile, specs, outs, kinds, (left, right, gate, up))
+
+
+def sum_kernel(*refs):
+    count = len(refs) // 2
+    value = sum(dot(refs[i][...], refs[count + i][...], TN) for i in range(count))
+    refs[-1][...] = value.astype(refs[-1].dtype)
+
+
+def sum_over_rows(pairs, kind=f32):
+    lefts, rights = zip(*pairs)
+    depth, rows = lefts[0].shape
+    tile, columns = 384, rights[0].shape[1]
+    left_specs = [pl.BlockSpec((left.shape[0], tile), lambda i: (0, i)) for left in lefts]
+    specs = left_specs + [held(right.shape) for right in rights]
+    return tiled(sum_kernel, rows, tile, specs, [columns], [kind], lefts + rights)[0]
 
 
 def shards(
@@ -338,10 +446,9 @@
     unused, rows, width = layer_in.shape
     zs, ts = lax.axis_size("fsdp"), lax.axis_size("tensor")
     x, z, t = lax.axis_index("seq"), lax.axis_index("fsdp"), lax.axis_index("tensor")
-    b, pair = z % 2, z // 2
     depth = attn_pre_gain.shape[0]
     sub = rows // ts
-    quarter = gate_weight.shape[1] // 4
+    units = gate_weight.shape[1] // 2
     first = x == 0
 
     def in_order(parts):
@@ -357,61 +464,70 @@
         parts = blocks.reshape(2, 2, 2, sub, -1).transpose(2, 1, 0, 3, 4)
         return in_order(parts.reshape(2, ts, sub, -1)).reshape(2, rows, -1)
 
-    gains = jnp.stack([attn_pre_gain, attn_post_gain, ffn_pre_gain, ffn_post_gain])
-    all_gains = lax.dynamic_update_slice_in_dim(
-        jnp.zeros((zs,) + gains.shape, bf16), gains[None], z, 0
-    )
-    for j in range(1, zs):
-        all_gains = lax.dynamic_update_slice_in_dim(
-            all_gains, swap(gains, "fsdp", j)[None], z ^ j, 0
-        )
-    all_gains = all_gains.transpose(1, 0, 2).reshape(4, width).astype(f32)
-    pre_gain, post_gain, mlp_pre, mlp_post = (all_gains[i] for i in range(4))
-
-    own_x = layer_in.reshape(1, ts, sub, width)
-    own_x = in_order(own_x)[0].reshape(2, 2, sub, width).transpose(1, 0, 2, 3)
-    far_x = swap_x(own_x[0])
-    far_x = jnp.stack([far_x, swap_core(far_x)])
-    x_rows = jnp.stack([own_x, far_x], axis=2).reshape(2 * rows, width)
-
-    w_qkv = jnp.concatenate(
+    def z_move(value, bits):
+        return Move(value, functools.partial(swap, axis="fsdp", bit=bits))
+
+    w_own = jnp.concatenate(
         [
             lax.dynamic_slice_in_dim(query_weight, x * HD, HD, 1),
             jnp.where(first, key_weight, value_weight),
         ],
         axis=1,
     )
-    ring = [w_qkv]
-    for unused in range(zs - 1):
-        ring.append(turn(ring[-1]))
+    gains = jnp.concatenate([attn_pre_gain, attn_post_gain, ffn_pre_gain, ffn_post_gain])
+    gain_rows = -(-4 * depth // (32 * HD)) * 16
+    gains = jnp.pad(gains, (0, gain_rows * 2 * HD - 4 * depth)).reshape(gain_rows, 2 * HD)
+    w_own = jnp.concatenate([w_own, gains])
+    own_x = in_order(layer_in.reshape(1, ts, sub, width))[0]
+    own_x = own_x.reshape(2, 2, sub, width).transpose(1, 0, 2, 3)
+    w_own, to_far = lax.optimization_barrier((w_own, own_x[0]))
+    ring = [w_own]
+    far_move = Move(to_far, swap_x)
+    far_move.result = swap_x(to_far)
+    for i in range(1, zs):
+        (block,) = step([ring[-1]], end=[far_move] if i == zs - 1 else [])
+        ring.append(turn(block))
+    far_x = far_move.result
+    far_x = jnp.concatenate([far_x, swap_core(far_x)]).reshape(rows, width)
+
+    def gathered(part):
+        return lax.all_gather(part, "fsdp", axis=0, tiled=True)
+
+    gate_w, up_w = (
+        Move(lax.dynamic_slice_in_dim(weight, x * units, units, 1), gathered)
+        for weight in (gate_weight, up_weight)
+    )
+    down_w = Move(lax.dynamic_slice_in_dim(down_weight, x * units, units, 0).T, gathered)
+    down_w.result = gathered(down_w.value)
+    w_out_own = lax.dynamic_slice_in_dim(out_weight, x * HD, HD, 0).T
+    out_moves = {j: z_move(w_out_own, j) for j in range(1, zs)}
+    def assemble(own, moves):
+        whole = jnp.zeros((width, own.shape[1]), bf16)
+        whole = lax.dynamic_update_slice_in_dim(whole, own, z * depth, 0)
+        for j, parts in moves.items():
+            offset = 0
+            for part in parts if isinstance(parts, list) else [parts]:
+                part = part.result if isinstance(part, Move) else part
+                whole = lax.dynamic_update_slice_in_dim(whole, part, (z ^ j) * depth + offset, 0)
+                offset += part.shape[0]
+        return whole
+
     w_qkv = jnp.zeros((width, 2 * HD), bf16)
-    for i, block in enumerate(ring):
-        w_qkv = lax.dynamic_update_slice_in_dim(w_qkv, block, (z - i) % zs * depth, 0)
-    w_out = lax.all_gather(
-        lax.dynamic_slice_in_dim(out_weight, x * HD, HD, 0).T, "fsdp", axis=0, tiled=True
-    )
-
-    def fetch(packs):
-        same, other = packs
-        whole = jnp.zeros((width, same.shape[1]), bf16)
-        for j in range(zs):
-            block = same if j == 0 else swap(other if j % 2 else same, "fsdp", j)
-            whole = lax.dynamic_update_slice_in_dim(whole, block, (z ^ j) * depth, 0)
-        return whole
-
-    def columns(weight, at):
-        return lax.dynamic_slice_in_dim(weight, at * quarter, quarter, 1)
-
-    places = (2 * x + b, 2 * x + 1 - b)
-    w_gu = fetch(
-        [jnp.concatenate([columns(gate_weight, at), columns(up_weight, at)], axis=1) for at in places]
-    )
-    w_down = fetch(
-        [lax.dynamic_slice_in_dim(down_weight, at * quarter, quarter, 0).T for at in places]
-    )
-
-    h_one = rms_norm(x_rows.astype(f32), pre_gain).astype(bf16)
-    projected = to_sequence(nn(h_one, w_qkv))
+    all_gains = jnp.zeros((zs, 4, depth), bf16)
+    for i, part in enumerate(ring):
+        place = (z - i) % zs
+        w_qkv = lax.dynamic_update_slice_in_dim(w_qkv, part[:depth], place * depth, 0)
+        part = part[depth:].reshape(-1)[: 4 * depth].reshape(1, 4, depth)
+        all_gains = lax.dynamic_update_slice_in_dim(all_gains, part, place, 0)
+    (w_qkv,) = step([w_qkv], begin=[gate_w])
+    all_gains = all_gains.transpose(1, 0, 2).reshape(4, width).astype(f32)
+    pre_gain, post_gain, mlp_pre, mlp_post = (all_gains[i] for i in range(4))
+    h_own, own_part = norm_product(own_x.reshape(rows, width), pre_gain, w_qkv)
+    h_far, far_part = norm_product(far_x, pre_gain, w_qkv)
+    projected = jnp.stack(
+        [part.reshape(2, 2, sub, 2 * HD) for part in (own_part, far_part)], axis=2
+    )
+    projected = to_sequence(projected)
     starts = jnp.stack([x * zs + z, (1 - x) * zs + z]) * rows
     positions = starts[:, None] + jnp.arange(rows, dtype=jnp.int32)[None, :]
     cos_tab, sine_tab = tables(positions.astype(f32))
@@ -419,56 +535,106 @@
     kv_sine = jnp.where(first, sine_tab, 0.0)
     q_scale = HD ** (-0.5)
     q_cast = (rotate(projected[..., :HD], cos_tab, sine_tab) * q_scale).astype(bf16)
-    kv_own = rotate(projected[..., HD:], kv_cos, kv_sine).astype(bf16)
-    kv_ring = [kv_own]
-    for unused in range(zs - 1):
-        kv_ring.append(turn(kv_ring[-1]))
-    kv_far = [swap_x(block) for block in kv_ring]
+    kv_ring, kv_far = [rotate(projected[..., HD:], kv_cos, kv_sine).astype(bf16)], []
+    for i in range(zs):
+        moves = []
+        if i == zs - 1:
+            moves = [out_moves[j] for j in range(1, zs - 1)] + [up_w]
+        (here,) = step([kv_ring[-1]], begin=moves)
+        if i < zs - 1:
+            kv_ring.append(turn(here))
+        kv_far.append(swap_x(here))
     kv_all = jnp.stack(kv_ring + kv_far).reshape(2, zs, 2, rows, HD)
 
     block = rows // 2 if rows >= 512 else rows
     last_doc = segment_ids.reshape(2 * zs, rows)[-1]
     info = jnp.concatenate([jnp.stack([x, z]), last_doc[::block]]).astype(jnp.int32)
     doc_col, doc_row = last_doc[:, None], last_doc[None, :]
+    early_out, late_out = [out_moves[j] for j in range(1, zs - 1)], [out_moves[zs - 1]]
+    q_cast, kv_all = step([q_cast, kv_all], begin=late_out, end=early_out + [gate_w])
     mixed, lse = attend(info, q_cast, kv_all, doc_col, doc_row, block)
+    (mixed,) = step([mixed], end=late_out)
+    w_out = assemble(w_out_own, out_moves)
 
     o_rows = to_exchange(mixed)
-    a_sum = scatter8(nt(o_rows, w_out))
+    o_halves = halves(o_rows)
+    a_sum = scatter8(
+        lambda got: rows_product(o_halves[0], w_out, NT, f32, got),
+        lambda: rows_product(o_halves[1], w_out, NT, bf16),
+        {},
+    )
 
     x_own = lax.dynamic_slice_in_dim(layer_in[0], t * sub, sub, 0).astype(f32)
     r_one = x_own + rms_norm(a_sum, post_gain)
-    h_two = gather16(rms_norm(r_one, mlp_pre).astype(bf16))
-    gu = nn(h_two, w_gu)
-    gate_pre, up_pre = gu[:, :quarter], gu[:, quarter:]
-    hidden = (jax.nn.gelu(gate_pre, approximate=True) * up_pre).astype(bf16)
-    split = 8 * sub
-    m_sum = scatter16(nt(hidden[:split], w_down), nt(hidden[split:], w_down))
+    h_two = gather8(rms_norm(r_one, mlp_pre).astype(bf16), {0: ((), [up_w])})
+    gate, up, hidden = gated_product(h_two, gate_w.result, up_w.result)
+    hidden_halves = halves(hidden)
+    m_sum = scatter8(
+        lambda got: rows_product(hidden_halves[0], down_w.result, NT, f32, got),
+        lambda: rows_product(hidden_halves[1], down_w.result, NT, bf16),
+        {},
+    )
     layer_own = (r_one + rms_norm(m_sum, mlp_post)).astype(bf16)
-    layer_out = lax.all_gather(layer_own, "tensor", axis=0, tiled=True)[None]
 
     incoming = lax.dynamic_slice_in_dim(out_grad[0], t * sub, sub, 0).astype(f32)
     d_msum, dg_mlp_post = norm_back(m_sum, mlp_post, incoming)
-    dm = gather16(d_msum.astype(bf16))
-    d_hidden = nn(dm, w_down)
-    unused, gelu_pull = jax.vjp(
-        lambda gate_in, up_in: jax.nn.gelu(gate_in, approximate=True) * up_in, gate_pre, up_pre
-    )
-    d_gate, d_up = gelu_pull(d_hidden)
-    d_gu = jnp.concatenate([d_gate.astype(bf16), d_up.astype(bf16)], axis=1)
-    dh_two = scatter16(nt(d_gu[:split], w_gu), nt(d_gu[split:], w_gu))
-    dw_down = tn(dm, hidden)
-    dw_gu = tn(h_two, d_gu)
-
+    def scattered(grad):
+        return lax.psum_scatter(grad, "fsdp", scatter_dimension=0, tiled=True)
+
+    class Unit:
+        def __init__(self, grad):
+            self.sum = Move(grad, scattered)
+            self.sum.result = scattered(grad)
+
+        def paired(self):
+            self.over = [Move(self.sum.result, swap_x)]
+            return self.over
+
+        def parts(self):
+            (move,) = self.over
+            return move.value, move.result
+
+    class Late:
+        def __init__(self, places):
+            self.places = places
+
+        def __contains__(self, place):
+            return place in self.places
+
+        def __getitem__(self, place):
+            return self.places[place]()
+
+    def product(pair):
+        return sum_over_rows([pair], bf16)
+
+    dm = gather8(d_msum.astype(bf16), {})
+    down_work = Move((dm, hidden), product)
+    (dm,) = step([dm], begin=[down_work])
+    (dm,) = step([dm], end=[down_work])
+    down_unit = Unit(down_work.result)
+    d_gate, d_up = gated_back(dm, down_w.result, gate, up)
+    gate_work, up_work = Move((h_two, d_gate), product), Move((h_two, d_up), product)
+    d_halves = list(zip(halves(d_gate), halves(d_up)))
+    weights = (gate_w.result, up_w.result)
+    dh_two = scatter8(
+        lambda got: rows_product(d_halves[0], weights, NT, f32, got),
+        lambda: rows_product(d_halves[1], weights, NT, bf16),
+        {1: ([gate_work], ()), 2: ([up_work], [gate_work])},
+    )
+    gate_unit = Unit(gate_work.result)
     dr_add, dg_mlp_pre = norm_back(r_one, mlp_pre, dh_two)
     d_resid = incoming + dr_add
     d_asum, dg_post = norm_back(a_sum, post_gain, d_resid)
 
-    da = gather8(d_asum.astype(bf16))
-    d_mixed_rows = nn(da, w_out).astype(bf16)
-    d_mixed = to_sequence(d_mixed_rows)
-    dw_out = tn(da, o_rows)
+    (da,) = step([d_asum.astype(bf16)], end=[up_work, down_unit.sum])
+    up_unit = Unit(up_work.result)
+    da = gather8(da, {})
+    d_mixed = to_sequence(rows_product(da, w_out, NN, bf16))
+    out_work = Move((da, o_rows), lambda pair: sum_over_rows([pair]))
     delta = jnp.sum(d_mixed.astype(f32) * mixed.astype(f32), axis=-1)
     steps = rows // block
+    layer_y = Move(layer_own, swap_y)
+    d_mixed, delta = step([d_mixed, delta], begin=down_unit.paired() + [layer_y, out_work])
     d_query, dkv_all = attend_back(
         info,
         q_cast,
@@ -480,76 +646,104 @@
         doc_row.reshape(steps, 1, block),
         block,
     )
+    (dkv_all,) = step([dkv_all], end=down_unit.over + [out_work])
+    q_rows = to_exchange(rotate(d_query * q_scale, cos_tab, -sine_tab).astype(bf16))
+
+    def qkv_grad(rows_in):
+        parts = rows_in.reshape(2, 2, 2, sub, HD)
+        near = parts[:, :, 0].reshape(rows, HD)
+        far = parts[:, :, 1].reshape(rows, HD)
+        return sum_over_rows([(h_own, near), (h_far, far)]).reshape(zs, depth, HD)
+
+    def sends(grad):
+        moves = [
+            z_move(lax.dynamic_index_in_dim(grad, z ^ j, 0, False).astype(bf16), j)
+            for j in range(1, zs)
+        ]
+        return lax.dynamic_index_in_dim(grad, z, 0, False), moves
+
+    def received(pair_of):
+        near, moves = pair_of
+        for move in moves:
+            near = near + move.result.astype(f32)
+        return near.astype(bf16)
+
     kept, given = dkv_all[0], dkv_all[1]
-    summed = [kept[i].astype(f32) + swap_x(given[i]).astype(f32) for i in range(zs)]
-    acc = summed[1] if zs > 1 else summed[0]
-    for i in list(range(2, zs)) + [0]:
-        acc = send(acc, turn) + summed[i]
-    dq_cast = rotate(d_query * q_scale, cos_tab, -sine_tab).astype(bf16)
+    order = list(range(1, zs)) + [0]
+    acc = kept[order[0]].astype(f32) + send(given[order[0]], swap_x)
+    for n, i in enumerate(order[1:]):
+        moved, far = acc.astype(bf16), given[i]
+        if n == 0:
+            dw_query = sends(qkv_grad(q_rows))
+            query_work = [
+                Move(part, lambda part: rows_product(part, w_qkv[:, :HD], NT, f32))
+                for part in halves(q_rows)
+            ]
+            moved, far = step([moved, far], begin=query_work, end=[layer_y, gate_unit.sum])
+        if n == 1:
+            moved, far = step([moved, far], begin=dw_query[1], end=query_work)
+        acc = kept[i].astype(f32) + swap_x(far).astype(f32) + turn(moved).astype(f32)
     dkv_cast = rotate(acc, kv_cos, -kv_sine).astype(bf16)
-    d_proj = to_exchange(jnp.concatenate([dq_cast, dkv_cast], axis=-1))
-    dh_one = scatter8(nt(d_proj, w_qkv))
-    dw_qkv = tn(h_one, d_proj)
+    kv_rows = to_exchange(dkv_cast)
+    (kv_rows,) = step([kv_rows], begin=gate_unit.paired(), end=dw_query[1])
+    kv_halves = halves(kv_rows)
+    kv_work = Move(kv_rows, qkv_grad)
+    out_back = sends(out_work.result.reshape(zs, depth, HD))
+    layer_pair = jnp.stack([layer_own, layer_y.result])
+    layer_core = Move(layer_pair, swap_core)
+    kv_back = []
+
+    def begin_kv():
+        kv_back.extend(sends(kv_work.result))
+        return kv_back[1] + up_unit.paired(), [kv_work, up_unit.sum] + gate_unit.over
+
+    w_kv = w_qkv[:, HD:]
+    dh_one = scatter8(
+        lambda got: rows_product(kv_halves[0], w_kv, NT, f32, query_work[0].result, got),
+        lambda: rows_product(kv_halves[1], w_kv, NT, bf16, query_work[1].result),
+        Late(
+            {
+                1: lambda: ([kv_work], ()),
+                2: begin_kv,
+            }
+        ),
+    )
     dx_add, dg_pre = norm_back(x_own, pre_gain, dh_one)
     grad_own = (d_resid + dx_add).astype(bf16)
-    grad_own = jnp.stack([grad_own, swap_y(grad_own)])
-    grad_own = jnp.stack([grad_own, swap_core(grad_own)], axis=1).reshape(1, ts, sub, width)
-    input_grad = in_order(grad_own).reshape(1, rows, width).astype(f32)
-
-    def give_back(grad):
-        both = 2 * depth
-        kept = lax.dynamic_slice_in_dim(grad, pair * both, both, 0)
-        for s in range(1, zs // 2):
-            part = lax.dynamic_slice_in_dim(grad, (pair ^ s) * both, both, 0)
-            kept = kept + swap(part.astype(bf16), "fsdp", 2 * s).astype(f32)
-        mine = lax.dynamic_slice_in_dim(kept, b * depth, depth, 0)
-        theirs = swap_z(lax.dynamic_slice_in_dim(kept, (1 - b) * depth, depth, 0).astype(bf16))
-        far = swap_x(jnp.stack([mine.astype(bf16), theirs]))
-        return mine, theirs.astype(f32), far[0].astype(f32), far[1].astype(f32)
-
-    def side_by_side(parts):
-        mine, theirs, far_mine, far_theirs = parts
-        even = b == 0
-        near = jnp.where(
-            even, jnp.concatenate([mine, theirs], 1), jnp.concatenate([theirs, mine], 1)
+    (grad_own,) = step([grad_own], begin=[layer_core] + out_back[1])
+    grad_pair = jnp.stack([grad_own, swap_y(grad_own)])
+    (grad_pair,) = step([grad_pair], end=kv_back[1])
+    qkv_x = Move(jnp.concatenate([received(dw_query), received(kv_back)], 1), swap_x)
+    (grad_pair,) = step([grad_pair], begin=[qkv_x])
+    out_x = Move(received(out_back), swap_x)
+    out_x.result = swap_x(out_x.value)
+    grad_all = jnp.stack([grad_pair, swap_core(grad_pair)], axis=1).reshape(1, ts, sub, width)
+    input_grad = in_order(grad_all).reshape(1, rows, width).astype(f32)
+    layer_all = jnp.stack([layer_pair, layer_core.result], axis=1).reshape(1, ts, sub, width)
+    layer_out = in_order(layer_all).reshape(1, rows, width)
+
+    gain_grads = jnp.stack([dg_pre, dg_post, dg_mlp_pre, dg_mlp_post])
+    for mover in (swap_y, swap_core, swap_x):
+        gain_grads = gain_grads + mover(gain_grads)
+    bits = 1
+    while bits < zs:
+        gain_grads = gain_grads + swap(gain_grads, "fsdp", bits)
+        bits *= 2
+    gain_grads = lax.dynamic_slice_in_dim(gain_grads, z * depth, depth, 1)
+
+    def two(even, left, right):
+        return jnp.where(
+            even, jnp.concatenate([left, right], 1), jnp.concatenate([right, left], 1)
         )
-        far = jnp.where(
-            even,
-            jnp.concatenate([far_mine, far_theirs], 1),
-            jnp.concatenate([far_theirs, far_mine], 1),
-        )
-        return jnp.where(
-            first, jnp.concatenate([near, far], 1), jnp.concatenate([far, near], 1)
-        )
-
-    g_down = side_by_side(give_back(dw_down)).T
-    gu_parts = give_back(dw_gu)
-    g_gate = side_by_side([part[:, :quarter] for part in gu_parts])
-    g_up = side_by_side([part[:, quarter:] for part in gu_parts])
-
-    def heads(near, far):
-        return jnp.where(
-            first, jnp.concatenate([near, far], 1), jnp.concatenate([far, near], 1)
-        )
-
-    near_out = lax.psum_scatter(dw_out.astype(bf16), "fsdp", scatter_dimension=0, tiled=True)
-    g_out = heads(near_out.astype(f32), swap_x(near_out).astype(f32)).T
-
-    def part_of(grad, i):
-        return lax.dynamic_slice_in_dim(grad, (z - i) % zs * depth, depth, 0)
-
-    acc = part_of(dw_qkv, 1)
-    for i in list(range(2, zs)) + [0]:
-        acc = send(acc, turn) + part_of(dw_qkv, i)
-    far = swap_x(acc.astype(bf16)).astype(f32)
-    g_query = heads(acc[:, :HD], far[:, :HD])
-    g_key = jnp.where(first, acc[:, HD:], far[:, HD:])
-    g_value = jnp.where(first, far[:, HD:], acc[:, HD:])
-
-    gain_grads = lax.psum(
-        jnp.stack([dg_pre, dg_post, dg_mlp_pre, dg_mlp_post]), ("seq", "fsdp", "tensor")
-    )
-    gain_grads = lax.dynamic_slice_in_dim(gain_grads, z * depth, depth, 1)
+
+    g_down = two(first, *down_unit.parts()).T.astype(f32)
+    g_gate = two(first, *gate_unit.parts()).astype(f32)
+    g_up = two(first, *up_unit.parts()).astype(f32)
+    near, far = qkv_x.value, qkv_x.result
+    g_query = two(first, near[:, :HD], far[:, :HD]).astype(f32)
+    g_key = jnp.where(first, near[:, HD:], far[:, HD:]).astype(f32)
+    g_value = jnp.where(first, far[:, HD:], near[:, HD:]).astype(f32)
+    g_out = two(first, out_x.value, out_x.result).T.astype(f32)
     return (
         layer_out,
         input_grad,

time: 1280 us -> 1090 us (0.85)
  Pallas kernels: 32.4 us -> 213 us
  waiting for transfers between devices: 675 us -> 523 us
  matrix products: 134 us -> 0 us
  blocking collectives: 39.7 us -> 0 us
  other arithmetic: 118 us -> 94.7 us
  local copies, waits for them, and re-layouts: 112 us -> 94.7 us
    ppermute x84 -> x71, waiting for transfers between devices: 545 us -> 293 us  [swap(): lax.ppermute(value, axis, [(i, i ^ bit) for i in range(lax.axis_size(axis...]
    pallas_call x0 -> x21, Pallas kernels: none -> 181 us  [tiled(): pl.pallas_call(body, grid=(rows // tile,), in_specs=in_specs, out_specs=[...]
    dot_general x14 -> x0, matrix products: 134 us -> none  [dot(): lax.dot_general(left, right, (dims, ((), ())), preferred_element_type=f32)]
    ppermute x12 -> x9, waiting for transfers between devices: 109 us -> 184 us  [turn(): lax.ppermute(value, 'fsdp', [(i, (i + 1) % size) for i in range(size)])]
    ppermute x84 -> x71, starting transfers between devices: 130 us -> 78.6 us  [swap(): lax.ppermute(value, axis, [(i, i ^ bit) for i in range(lax.axis_size(axis...]
    all_gather x2 -> x3, waiting for transfers between devices: 0.02 us -> 46.1 us  [gathered(): return lax.all_gather(part, 'fsdp', axis=0, tiled=True)]
    ppermute x12 -> x9, starting transfers between devices: 19.4 us -> 63.1 us  [turn(): lax.ppermute(value, 'fsdp', [(i, (i + 1) % size) for i in range(size)])]
    psum x1 -> x0, blocking collectives: 39.7 us -> none  [shards(): lax.psum(jnp.stack([dg_pre, dg_post, dg_mlp_pre, dg_mlp_post]), ('seq', '...]
  transfers between devices with their start and end apart: 99 -> 86, of which waited for: 61 -> 58; matrix products, arithmetic and copies ran while one was open for 16% -> 13% of each run, Pallas kernels for 3% -> 17%
where the time goes in v2:
time: 1090 us; the launch traced here: 1080 us
  waiting for transfers between devices  523 us (48%)
  Pallas kernels  213 us (20%)
  starting transfers between devices  142 us (13%)
  local copies, waits for them, and re-layouts  94.7 us (9%)
  other arithmetic  94.7 us (9%)
  between operations  16 us (1%)
    ppermute x71, waiting for transfers between devices, swap(): lax.ppermute(value, axis, [(i, i ^ bit) for i in range(lax.axis_size(axis...  293 us
    ppermute x9, waiting for transfers between devices, turn(): lax.ppermute(value, 'fsdp', [(i, (i + 1) % size) for i in range(size)])  184 us
    pallas_call x21, Pallas kernels, tiled(): pl.pallas_call(body, grid=(rows // tile,), in_specs=in_specs, out_specs=[...  181 us
    ppermute x71, starting transfers between devices, swap(): lax.ppermute(value, axis, [(i, i ^ bit) for i in range(lax.axis_size(axis...  78.6 us
    ppermute x9, starting transfers between devices, turn(): lax.ppermute(value, 'fsdp', [(i, (i + 1) % size) for i in range(size)])  63.1 us
    all_gather x3, waiting for transfers between devices, gathered(): return lax.all_gather(part, 'fsdp', axis=0, tiled=True)  46.1 us
    unnamed x158, local copies, waits for them, and re-layouts  29.1 us
  transfers between devices with their start and end apart: 86, of which 58 were waited for; matrix products, arithmetic and copies ran while one was open for 13% of the time, Pallas kernels for 17%

profile of v2, /device:TPU:0, one launch (start us, length us, event | category | flops | bytes accessed | tf_op | source)
XLA Modules:
  0.0 1083.8 jit_solution(13512046225873084247)
XLA Ops:
  22.4 15.5 %collective-permute-done = bf16[592,512]{1,0:T(8,128)(2,1)} collective-permute-done((bf16[592,512]{1,0:T(8,128)(2,1)S(1)}, bf16[592,512]{1,0:T(8,128)(2,1)}, u32[]{:S(2)}, u32[]{:S(2)}) %collective-permute-start) | collective-permute-done | bytes 606240 | tf_op jit(solution)/shard_map/ppermute | solution.py:38
  39.1 15.2 %collective-permute-done.1 = bf16[592,512]{1,0:T(8,128)(2,1)} collective-permute-done((bf16[592,512]{1,0:T(8,128)(2,1)}, bf16[592,512]{1,0:T(8,128)(2,1)}, u32[]{:S(2)}, u32[]{:S(2)}) %collective-permute-start.1) | collective-permute-done | bytes 606240 | tf_op jit(solution)/shard_map/ppermute | solution.py:38
  57.8 12.6 %collective-permute-done.3 = bf16[592,512]{1,0:T(8,128)(2,1)} collective-permute-done((bf16[592,512]{1,0:T(8,128)(2,1)}, bf16[592,512]{1,0:T(8,128)(2,1)}, u32[]{:S(2)}, u32[]{:S(2)}) %collective-permute-start.3) | collective-permute-done | bytes 606240 | tf_op jit(solution)/shard_map/ppermute | solution.py:38
  79.3 5.5 shard_map.237
  88.4 5.2 shard_map.238
  99.5 33.6 %collective-permute-done.5 = bf16[2,640,256]{2,1,0:T(8,128)(2,1)} collective-permute-done((bf16[2,640,256]{2,1,0:T(8,128)(2,1)}, bf16[2,640,256]{2,1,0:T(8,128)(2,1)}, u32[]{:S(2)}, u32[]{:S(2)}) %collective-permute-start.5) | collective-permute-done | bytes 655392 | tf_op jit(solution)/shard_map/ppermute | solution.py:38
  133.1 11.4 %collective-permute-start.6 = (bf16[2,640,256]{2,1,0:T(8,128)(2,1)}, bf16[2,640,256]{2,1,0:T(8,128)(2,1)}, u32[]{:S(2)}, u32[]{:S(2)}) collective-permute-start(bf16[2,640,256]{2,1,0:T(8,128)(2,1)} %collective-permute-done.5), channel_id=1, source_target_pairs={{0,4},{4,8},{8,12},{12,0},{1,5},{5,9},{9,13},{13,1},{2,6},{6,10},{... | collective-permute-start | bytes 1966088 | tf_op jit(solution)/shard_map/ppermute | solution.py:38
  150.1 26.6 %collective-permute-done.6 = bf16[2,640,256]{2,1,0:T(8,128)(2,1)} collective-permute-done((bf16[2,640,256]{2,1,0:T(8,128)(2,1)}, bf16[2,640,256]{2,1,0:T(8,128)(2,1)}, u32[]{:S(2)}, u32[]{:S(2)}) %collective-permute-start.6) | collective-permute-done | bytes 655392 | tf_op jit(solution)/shard_map/ppermute | solution.py:38
  176.8 11.8 %collective-permute-start.7 = (bf16[2,640,256]{2,1,0:T(8,128)(2,1)}, bf16[2,640,256]{2,1,0:T(8,128)(2,1)}, u32[]{:S(2)}, u32[]{:S(2)}) collective-permute-start(bf16[2,640,256]{2,1,0:T(8,128)(2,1)} %collective-permute-done.6), channel_id=1, source_target_pairs={{0,4},{4,8},{8,12},{12,0},{1,5},{5,9},{9,13},{13,1},{2,6},{6,10},{... | collective-permute-start | bytes 1966088 | tf_op jit(solution)/shard_map/ppermute | solution.py:38
  196.8 15.3 %collective-permute-done.7 = bf16[2,640,256]{2,1,0:T(8,128)(2,1)} collective-permute-done((bf16[2,640,256]{2,1,0:T(8,128)(2,1)}, bf16[2,640,256]{2,1,0:T(8,128)(2,1)}, u32[]{:S(2)}, u32[]{:S(2)}) %collective-permute-start.7) | collective-permute-done | bytes 655392 | tf_op jit(solution)/shard_map/ppermute | solution.py:38
  223.6 11.7 %collective-permute-done.11 = bf16[2,640,256]{2,1,0:T(8,128)(2,1)S(1)} collective-permute-done((bf16[2,640,256]{2,1,0:T(8,128)(2,1)}, bf16[2,640,256]{2,1,0:T(8,128)(2,1)S(1)}, u32[]{:S(2)}, u32[]{:S(2)}) %collective-permute-start.11) | collective-permute-done | bytes 655392 | tf_op jit(solution)/shard_map/ppermute | solution.py:21
  240.3 11.2 %shard_map.239 = (bf16[2,640,256]{2,1,0:T(8,128)(2,1)S(1)}, f32[2,640,1]{2,1,0:T(8,128)S(1)}) custom-call(s32[4]{0:T(128)S(1)} %pad_add_fusion.info, bf16[2,640,256]{2,1,0:T(8,128)(2,1)S(1)} %fusion.31.q_ref, bf16[2,4,2,640,256]{4,3,2,1,0:T(8,128)(2,1)} %bitcast.27.kv_ref, s32[640,1]{1,0:T(8,128)S(1)} %copy.47.col_ref, s32[1,640]{1,0:T(1,128)S(1)} %get-tuple-element.361.row_ref), custom_call_target="tpu_custom_call" | custom-call | flops 500000000 | bytes 1000000 | tf_op jit(solution)/shard_map/pallas_call | solution.py:249
  257.0 5.6 collective-permute-done.15.refs_2_
  274.9 15.4 %collective-permute-done.16 = bf16[2,160,1152]{2,1,0:T(8,128)(2,1)S(1)} collective-permute-done((bf16[2,160,1152]{2,1,0:T(8,128)(2,1)S(1)}, bf16[2,160,1152]{2,1,0:T(8,128)(2,1)S(1)}, u32[]{:S(2)}, u32[]{:S(2)}) %collective-permute-start.16) | collective-permute-done | bytes 737312 | tf_op jit(solution)/shard_map/ppermute | solution.py:21
  300.6 6.2 collective-permute-done.18
  314.0 12.7 %all-gather.6.cloned.1.call-done.up_w.refs_3_ = bf16[2304,1152]{1,0:T(8,128)(2,1)} async-done(((bf16[576,1152]{1,0:T(8,128)(2,1)}), bf16[2304,1152]{1,0:T(8,128)(2,1)}) %all-gather.6.cloned.1.call-update) | async-done | bytes 5308432 | tf_op jit(solution)/shard_map/all_gather | solution.py:494
  329.7 7.6 collective-permute-done.20
  341.7 15.2 %collective-permute-done.22 = bf16[2,160,1152]{2,1,0:T(8,128)(2,1)S(1)} collective-permute-done((bf16[2,160,1152]{2,1,0:T(8,128)(2,1)S(1)}, bf16[2,160,1152]{2,1,0:T(8,128)(2,1)S(1)}, u32[]{:S(2)}, u32[]{:S(2)}) %collective-permute-start.22) | collective-permute-done | bytes 737312 | tf_op jit(solution)/shard_map/ppermute | solution.py:21
  358.8 5.4 collective-permute-done.24
  367.6 22.4 %shard_map.242 = (f32[1280,1152]{1,0:T(8,128)}, f32[1280,1152]{1,0:T(8,128)}, bf16[1280,1152]{1,0:T(8,128)(2,1)}) custom-call(bf16[1280,2304]{1,0:T(8,128)(2,1)} %bitcast.372, bf16[2304,1152]{1,0:T(8,128)(2,1)} %all-gather.4.cloned.1.call-done.gate_w.refs_2_, bf16[2304,1152]{1,0:T(8,128)(2,1)} %all-gather.6.cloned.1.call-done.up_w.refs_3_), custom_call_target="tpu_custom_call" | custom-call | flops 500000000 | bytes 1000000 | tf_op jit(solution)/shard_map/pallas_call | solution.py:319
  393.1 33.4 %all-gather.8.cloned.1.call-done.refs_1_.w_ref = bf16[2304,1152]{1,0:T(8,128)(2,1)} async-done(((bf16[576,1152]{1,0:T(8,128)(2,1)}), bf16[2304,1152]{1,0:T(8,128)(2,1)}) %all-gather.8.cloned.1.call-update) | async-done | bytes 5308432 | tf_op jit(solution)/shard_map/all_gather | solution.py:494
  426.5 8.0 shard_map.243
  434.5 5.6 collective-permute-done.25.refs_2_
  441.7 8.8 shard_map.244
  456.7 15.6 %collective-permute-done.26 = bf16[2,160,1152]{2,1,0:T(8,128)(2,1)S(1)} collective-permute-done((bf16[2,160,1152]{2,1,0:T(8,128)(2,1)S(1)}, bf16[2,160,1152]{2,1,0:T(8,128)(2,1)S(1)}, u32[]{:S(2)}, u32[]{:S(2)}) %collective-permute-start.26) | collective-permute-done | bytes 737312 | tf_op jit(solution)/shard_map/ppermute | solution.py:21
  478.7 7.7 collective-permute-done.28
  494.5 6.5 collective-permute-done.30
  504.6 12.5 %collective-permute-done.32 = bf16[2,160,1152]{2,1,0:T(8,128)(2,1)S(1)} collective-permute-done((bf16[2,160,1152]{2,1,0:T(8,128)(2,1)S(1)}, bf16[2,160,1152]{2,1,0:T(8,128)(2,1)S(1)}, u32[]{:S(2)}, u32[]{:S(2)}) %collective-permute-start.32) | collective-permute-done | bytes 737312 | tf_op jit(solution)/shard_map/ppermute | solution.py:21
  518.3 5.4 collective-permute-done.34
  527.0 12.6 %shard_map.245 = bf16[2304,1152]{1,0:T(8,128)(2,1)} custom-call(bf16[1280,2304]{1,0:T(8,128)(2,1)} %bitcast.375, bf16[1280,1152]{1,0:T(8,128)(2,1)} %get-tuple-element.171.refs_1_), custom_call_target="tpu_custom_call" | custom-call | flops 500000000 | bytes 1000000 | tf_op jit(solution)/shard_map/pallas_call | solution.py:319
  539.6 17.1 %shard_map.246 = (bf16[1280,1152]{1,0:T(8,128)(2,1)}, bf16[1280,1152]{1,0:T(8,128)(2,1)}) custom-call(bf16[1280,2304]{1,0:T(8,128)(2,1)} %bitcast.376, bf16[2304,1152]{1,0:T(8,128)(2,1)} %all-gather.8.cloned.1.call-done.refs_1_.w_ref, f32[1280,1152]{1,0:T(8,128)} %get-tuple-element.173.gate_ref, f32[1280,1152]{1,0:T(8,128)} %get-tuple-element.174.up_ref), custom_call_target="tpu_custom_call" | custom-call | flops 500000000 | bytes 1000000 | tf_op jit(solution)/shard_map/pallas_call | solution.py:319
  561.3 13.4 %shard_map.247 = bf16[640,2304]{1,0:T(8,128)(2,1)} custom-call(bf16[640,1152]{1,0:T(8,128)(2,1)S(1)} %get-tuple-element.287.refs_0_, bf16[640,1152]{1,0:T(8,128)(2,1)} %get-tuple-element.285.refs_1_, bf16[2304,1152]{1,0:T(8,128)(2,1)} %all-gather.4.cloned.1.call-done.gate_w.refs_2_, bf16[2304,1152]{1,0:T(8,128)(2,1)} %all-gather.6.cloned.1.call-done.up_w.refs_3_), custom_call_target="tpu_custom_call" | custom-call | flops 500000000 | bytes 1000000 | tf_op jit(solution)/shard_map/pallas_call | solution.py:319
  574.7 5.5 collective-permute-done.35.refs_4_
  581.9 14.3 %shard_map.248 = f32[640,2304]{1,0:T(8,128)} custom-call(bf16[640,1152]{1,0:T(8,128)(2,1)S(1)} %get-tuple-element.288.refs_0_, bf16[640,1152]{1,0:T(8,128)(2,1)} %get-tuple-element.286.refs_1_, bf16[2304,1152]{1,0:T(8,128)(2,1)} %all-gather.4.cloned.1.call-done.gate_w.refs_2_, bf16[2304,1152]{1,0:T(8,128)(2,1)} %all-gather.6.cloned.1.call-done.up_w.refs_3_, ...), custom_call_target="tpu_custom_call" | custom-call | flops 500000000 | bytes 1000000 | tf_op jit(solution)/shard_map/pallas_call | solution.py:319
  603.1 12.1 %shard_map.249 = bf16[2304,1152]{1,0:T(8,128)(2,1)} custom-call(bf16[1280,2304]{1,0:T(8,128)(2,1)} %bitcast.373, bf16[1280,1152]{1,0:T(8,128)(2,1)} %get-tuple-element.180.refs_1_), custom_call_target="tpu_custom_call" | custom-call | flops 500000000 | bytes 1000000 | tf_op jit(solution)/shard_map/pallas_call | solution.py:319
  615.2 4.6 collective-permute-done.36
  626.9 12.3 %shard_map.250 = bf16[2304,1152]{1,0:T(8,128)(2,1)} custom-call(bf16[1280,2304]{1,0:T(8,128)(2,1)} %bitcast.374, bf16[1280,1152]{1,0:T(8,128)(2,1)} %get-tuple-element.184.refs_1_), custom_call_target="tpu_custom_call" | custom-call | flops 500000000 | bytes 1000000 | tf_op jit(solution)/shard_map/pallas_call | solution.py:319
  649.4 6.3 collective-permute-done.40
  659.0 13.7 %collective-permute-done.42 = bf16[2,160,1152]{2,1,0:T(8,128)(2,1)S(1)} collective-permute-done((bf16[2,160,1152]{2,1,0:T(8,128)(2,1)S(1)}, bf16[2,160,1152]{2,1,0:T(8,128)(2,1)S(1)}, u32[]{:S(2)}, u32[]{:S(2)}) %collective-permute-start.42) | collective-permute-done | bytes 737312 | tf_op jit(solution)/shard_map/ppermute | solution.py:21
  674.8 4.6 collective-permute-done.44
  682.9 4.6 shard_map.251
  693.1 6.8 shard_map.253
  699.9 21.3 %shard_map.252 = (f32[2,640,256]{2,1,0:T(8,128)}, bf16[2,4,2,640,256]{4,3,2,1,0:T(8,128)(2,1)}) custom-call(s32[4]{0:T(128)} %copy-done.9, bf16[2,640,256]{2,1,0:T(8,128)(2,1)} %copy-done.2, bf16[2,640,256]{2,1,0:T(8,128)(2,1)} %bitcast.412, f32[4,1,320]{2,1,0:T(1,128)} %reshape.607.lse_ref, f32[4,1,320]{2,1,0:T(1,128)} %reshape.580.delta_ref, ...), custom_call_target="tpu_custom_call" | custom-call | flops 500000000 | bytes 1000000 | tf_op jit(solution)/shard_map/pallas_call | solution.py:280
  730.4 11.6 %collective-permute-done.46 = bf16[2,640,256]{2,1,0:T(8,128)(2,1)S(1)} collective-permute-done((bf16[2,640,256]{2,1,0:T(8,128)(2,1)S(1)}, bf16[2,640,256]{2,1,0:T(8,128)(2,1)S(1)}, u32[]{:S(2)}, u32[]{:S(2)}) %collective-permute-start.46) | collective-permute-done | bytes 655392 | tf_op jit(solution)/shard_map/ppermute | solution.py:21
  751.0 6.9 shard_map.254
  765.7 16.6 %collective-permute-done.50 = bf16[2,640,256]{2,1,0:T(8,128)(2,1)S(1)} collective-permute-done((bf16[2,640,256]{2,1,0:T(8,128)(2,1)}, bf16[2,640,256]{2,1,0:T(8,128)(2,1)S(1)}, u32[]{:S(2)}, u32[]{:S(2)}) %collective-permute-start.50) | collective-permute-done | bytes 655392 | tf_op jit(solution)/shard_map/ppermute | solution.py:38
  784.4 19.2 %collective-permute-start.52 = (bf16[2,640,256]{2,1,0:T(8,128)(2,1)S(1)}, bf16[2,640,256]{2,1,0:T(8,128)(2,1)S(1)}, u32[]{:S(2)}, u32[]{:S(2)}) collective-permute-start(bf16[2,640,256]{2,1,0:T(8,128)(2,1)S(1)} %fusion.33), channel_id=1, source_target_pairs={{0,4},{4,8},{8,12},{12,0},{1,5},{5,9},{9,13},{13,1},{2,6},{6,10},{... | collective-permute-start | bytes 1966088 | tf_op jit(solution)/shard_map/ppermute | solution.py:38
  804.1 30.6 %collective-permute-done.52 = bf16[2,640,256]{2,1,0:T(8,128)(2,1)S(1)} collective-permute-done((bf16[2,640,256]{2,1,0:T(8,128)(2,1)S(1)}, bf16[2,640,256]{2,1,0:T(8,128)(2,1)S(1)}, u32[]{:S(2)}, u32[]{:S(2)}) %collective-permute-start.52) | collective-permute-done | bytes 655392 | tf_op jit(solution)/shard_map/ppermute | solution.py:38
  836.0 14.7 %collective-permute-start.53 = (bf16[2,640,256]{2,1,0:T(8,128)(2,1)S(1)}, bf16[2,640,256]{2,1,0:T(8,128)(2,1)S(1)}, u32[]{:S(2)}, u32[]{:S(2)}) collective-permute-start(bf16[2,640,256]{2,1,0:T(8,128)(2,1)S(1)} %fusion.35), channel_id=1, source_target_pairs={{0,4},{4,8},{8,12},{12,0},{1,5},{5,9},{9,13},{13,1},{2,6},{6,10},{... | collective-permute-start | bytes 1966088 | tf_op jit(solution)/shard_map/ppermute | solution.py:38
  855.5 17.5 %collective-permute-done.53 = bf16[2,640,256]{2,1,0:T(8,128)(2,1)S(1)} collective-permute-done((bf16[2,640,256]{2,1,0:T(8,128)(2,1)S(1)}, bf16[2,640,256]{2,1,0:T(8,128)(2,1)S(1)}, u32[]{:S(2)}, u32[]{:S(2)}) %collective-permute-start.53) | collective-permute-done | bytes 655392 | tf_op jit(solution)/shard_map/ppermute | solution.py:38
  882.1 8.1 collective-permute-done.56
  894.9 5.6 collective-permute-done.57.refs_3_
  900.5 5.7 shard_map.258
  916.7 7.6 shard_map.259
  932.2 24.3 %collective-permute-done.60 = bf16[576,1152]{1,0:T(8,128)(2,1)} collective-permute-done((bf16[576,1152]{1,0:T(8,128)(2,1)}, bf16[576,1152]{1,0:T(8,128)(2,1)}, u32[]{:S(2)}, u32[]{:S(2)}) %collective-permute-start.60) | collective-permute-done | bytes 1327136 | tf_op jit(solution)/shard_map/ppermute | solution.py:21
  958.0 5.2 convert_bitcast_fusion
  966.4 6.3 collective-permute-done.62
  983.0 5.6 collective-permute-start.72
  994.3 5.3 fusion
  999.6 19.3 %collective-permute-done.73 = f32[4,2304]{1,0:T(4,128)S(1)} collective-permute-done((f32[4,2304]{1,0:T(4,128)S(1)}, f32[4,2304]{1,0:T(4,128)S(1)}, u32[]{:S(2)}, u32[]{:S(2)}) %collective-permute-start.73) | collective-permute-done | bytes 36896 | tf_op jit(solution)/shard_map/ppermute | solution.py:21
  1025.9 7.5 collective-permute-done.65
  1034.0 9.9 collective-permute-done.66
  1045.8 11.5 %collective-permute-done.78 = bf16[576,256]{1,0:T(8,128)(2,1)S(1)} collective-permute-done((bf16[576,256]{1,0:T(8,128)(2,1)S(1)}, bf16[576,256]{1,0:T(8,128)(2,1)S(1)}, u32[]{:S(2)}, u32[]{:S(2)}) %collective-permute-start.78) | collective-permute-done | bytes 294944 | tf_op jit(solution)/shard_map/ppermute | solution.py:21
  1061.1 5.6 collective-permute-done.74
  (498 shorter events, 304.3 us)
Async XLA Ops:
  7.2 229.0 %all-gather.4.cloned.1.call-start = ((), (), s32[]{:S(2)}) async-start(), calls=%async_computation.3 | async-start | bytes 6635520 | tf_op jit(solution)/shard_map/all_gather | solution.py:494
  17.8 36.5 %collective-permute-start.2 = (bf16[2,160,2304]{2,1,0:T(8,128)(2,1)}, bf16[2,160,2304]{2,1,0:T(8,128)(2,1)}, u32[]{:S(2)}, u32[]{:S(2)}) collective-permute-start(bf16[2,160,2304]{2,1,0:T(8,128)(2,1)} %slice_bitcast_fusion.8), channel_id=1, source_target_pairs={{0,16},{16,0},{1,17},{17,1},{2,18},{18,2},{3,19},{19,3},{4,20},{20... | collective-permute-start | bytes 4423688 | tf_op jit(solution)/shard_map/ppermute | solution.py:21
  20.8 17.1 %collective-permute-start = (bf16[592,512]{1,0:T(8,128)(2,1)S(1)}, bf16[592,512]{1,0:T(8,128)(2,1)}, u32[]{:S(2)}, u32[]{:S(2)}) collective-permute-start(bf16[592,512]{1,0:T(8,128)(2,1)S(1)} %pad_maximum_fusion.27), channel_id=1, source_target_pairs={{0,4},{4,8},{8,12},{12,0},{1,5},{5,9},{9,13},{13,1},{2,6},{6,10},{... | collective-permute-start | bytes 1818632 | tf_op jit(solution)/shard_map/ppermute | solution.py:38
  37.9 16.4 %collective-permute-start.1 = (bf16[592,512]{1,0:T(8,128)(2,1)}, bf16[592,512]{1,0:T(8,128)(2,1)}, u32[]{:S(2)}, u32[]{:S(2)}) collective-permute-start(bf16[592,512]{1,0:T(8,128)(2,1)} %collective-permute-done), channel_id=1, source_target_pairs={{0,4},{4,8},{8,12},{12,0},{1,5},{5,9},{9,13},{13,1},{2,6},{6,10},{... | collective-permute-start | bytes 1818632 | tf_op jit(solution)/shard_map/ppermute | solution.py:38
  54.3 16.1 %collective-permute-start.3 = (bf16[592,512]{1,0:T(8,128)(2,1)}, bf16[592,512]{1,0:T(8,128)(2,1)}, u32[]{:S(2)}, u32[]{:S(2)}) collective-permute-start(bf16[592,512]{1,0:T(8,128)(2,1)} %collective-permute-done.1), channel_id=1, source_target_pairs={{0,4},{4,8},{8,12},{12,0},{1,5},{5,9},{9,13},{13,1},{2,6},{6,10},{... | collective-permute-start | bytes 1818632 | tf_op jit(solution)/shard_map/ppermute | solution.py:38
  71.5 255.2 %all-gather.6.cloned.1.call-start = ((), (), s32[]{:S(2)}) async-start(), calls=%async_computation.4 | async-start | bytes 6635520 | tf_op jit(solution)/shard_map/all_gather | solution.py:494
  99.5 33.6 %collective-permute-start.5 = (bf16[2,640,256]{2,1,0:T(8,128)(2,1)}, bf16[2,640,256]{2,1,0:T(8,128)(2,1)}, u32[]{:S(2)}, u32[]{:S(2)}) collective-permute-start(bf16[2,640,256]{2,1,0:T(8,128)(2,1)} %pad_maximum_fusion.22), channel_id=1, source_target_pairs={{0,4},{4,8},{8,12},{12,0},{1,5},{5,9},{9,13},{13,1},{2,6},{6,10},{... | collective-permute-start | bytes 1966088 | tf_op jit(solution)/shard_map/ppermute | solution.py:38
  133.1 43.6 %collective-permute-start.6 = (bf16[2,640,256]{2,1,0:T(8,128)(2,1)}, bf16[2,640,256]{2,1,0:T(8,128)(2,1)}, u32[]{:S(2)}, u32[]{:S(2)}) collective-permute-start(bf16[2,640,256]{2,1,0:T(8,128)(2,1)} %collective-permute-done.5), channel_id=1, source_target_pairs={{0,4},{4,8},{8,12},{12,0},{1,5},{5,9},{9,13},{13,1},{2,6},{6,10},{... | collective-permute-start | bytes 1966088 | tf_op jit(solution)/shard_map/ppermute | solution.py:38
  148.6 66.5 %collective-permute-start.8 = (bf16[2,640,256]{2,1,0:T(8,128)(2,1)}, bf16[2,640,256]{2,1,0:T(8,128)(2,1)}, u32[]{:S(2)}, u32[]{:S(2)}) collective-permute-start(bf16[2,640,256]{2,1,0:T(8,128)(2,1)} %pad_maximum_fusion.22), channel_id=1, source_target_pairs={{0,16},{16,0},{1,17},{17,1},{2,18},{18,2},{3,19},{19,3},{4,20},{20... | collective-permute-start | bytes 1966088 | tf_op jit(solution)/shard_map/ppermute | solution.py:21
  176.8 35.3 %collective-permute-start.7 = (bf16[2,640,256]{2,1,0:T(8,128)(2,1)}, bf16[2,640,256]{2,1,0:T(8,128)(2,1)}, u32[]{:S(2)}, u32[]{:S(2)}) collective-permute-start(bf16[2,640,256]{2,1,0:T(8,128)(2,1)} %collective-permute-done.6), channel_id=1, source_target_pairs={{0,4},{4,8},{8,12},{12,0},{1,5},{5,9},{9,13},{13,1},{2,6},{6,10},{... | collective-permute-start | bytes 1966088 | tf_op jit(solution)/shard_map/ppermute | solution.py:38
  190.8 27.8 %collective-permute-start.9 = (bf16[2,640,256]{2,1,0:T(8,128)(2,1)}, bf16[2,640,256]{2,1,0:T(8,128)(2,1)}, u32[]{:S(2)}, u32[]{:S(2)}) collective-permute-start(bf16[2,640,256]{2,1,0:T(8,128)(2,1)} %collective-permute-done.5), channel_id=1, source_target_pairs={{0,16},{16,0},{1,17},{17,1},{2,18},{18,2},{3,19},{19,3},{4,20},{20... | collective-permute-start | bytes 1966088 | tf_op jit(solution)/shard_map/ppermute | solution.py:21
  194.7 28.0 %collective-permute-start.10 = (bf16[2,640,256]{2,1,0:T(8,128)(2,1)}, bf16[2,640,256]{2,1,0:T(8,128)(2,1)S(1)}, u32[]{:S(2)}, u32[]{:S(2)}) collective-permute-start(bf16[2,640,256]{2,1,0:T(8,128)(2,1)} %collective-permute-done.6), channel_id=1, source_target_pairs={{0,16},{16,0},{1,17},{17,1},{2,18},{18,2},{3,19},{19,3},{4,20},{20... | collective-permute-start | bytes 1966088 | tf_op jit(solution)/shard_map/ppermute | solution.py:21
  212.1 24.1 %collective-permute-start.12 = (bf16[576,256]{1,0:T(8,128)(2,1)}, bf16[576,256]{1,0:T(8,128)(2,1)S(1)}, u32[]{:S(2)}, u32[]{:S(2)}) collective-permute-start(bf16[576,256]{1,0:T(8,128)(2,1)} %get-tuple-element.144), channel_id=1, source_target_pairs={{0,4},{4,0},{8,12},{12,8},{1,5},{5,1},{9,13},{13,9},{2,6},{6,2},{1... | collective-permute-start | bytes 884744 | tf_op jit(solution)/shard_map/ppermute | solution.py:21
  212.1 24.1 %collective-permute-start.13 = (bf16[576,256]{1,0:T(8,128)(2,1)}, bf16[576,256]{1,0:T(8,128)(2,1)S(1)}, u32[]{:S(2)}, u32[]{:S(2)}) collective-permute-start(bf16[576,256]{1,0:T(8,128)(2,1)} %get-tuple-element.144), channel_id=1, source_target_pairs={{0,8},{4,12},{8,0},{12,4},{1,9},{5,13},{9,1},{13,5},{2,10},{6,14},... | collective-permute-start | bytes 884744 | tf_op jit(solution)/shard_map/ppermute | solution.py:21
  212.9 213.6 %all-gather.8.cloned.1.call-start = ((), (), s32[]{:S(2)}) async-start(), calls=%async_computation.5 | async-start | bytes 6635520 | tf_op jit(solution)/shard_map/all_gather | solution.py:494
  215.1 20.2 %collective-permute-start.11 = (bf16[2,640,256]{2,1,0:T(8,128)(2,1)}, bf16[2,640,256]{2,1,0:T(8,128)(2,1)S(1)}, u32[]{:S(2)}, u32[]{:S(2)}) collective-permute-start(bf16[2,640,256]{2,1,0:T(8,128)(2,1)} %collective-permute-done.7), channel_id=1, source_target_pairs={{0,16},{16,0},{1,17},{17,1},{2,18},{18,2},{3,19},{19,3},{4,20},{20... | collective-permute-start | bytes 1966088 | tf_op jit(solution)/shard_map/ppermute | solution.py:21
  236.2 17.5 %collective-permute-start.14 = (bf16[576,256]{1,0:T(8,128)(2,1)}, bf16[576,256]{1,0:T(8,128)(2,1)S(1)}, u32[]{:S(2)}, u32[]{:S(2)}) collective-permute-start(bf16[576,256]{1,0:T(8,128)(2,1)} %get-tuple-element.144), channel_id=1, source_target_pairs={{0,12},{4,8},{8,4},{12,0},{1,13},{5,9},{9,5},{13,1},{2,14},{6,10},... | collective-permute-start | bytes 884744 | tf_op jit(solution)/shard_map/ppermute | solution.py:21
  271.7 18.6 %collective-permute-start.16 = (bf16[2,160,1152]{2,1,0:T(8,128)(2,1)S(1)}, bf16[2,160,1152]{2,1,0:T(8,128)(2,1)S(1)}, u32[]{:S(2)}, u32[]{:S(2)}) collective-permute-start(bf16[2,160,1152]{2,1,0:T(8,128)(2,1)S(1)} %slice_bitcast_fusion.24), channel_id=1, source_target_pairs={{0,16},{16,0},{1,17},{17,1},{2,18},{18,2},{3,19},{19,3},{4,20},{20... | collective-permute-start | bytes 2211848 | tf_op jit(solution)/shard_map/ppermute | solution.py:21
  273.4 18.3 %collective-permute-start.17 = (bf16[2,160,1152]{2,1,0:T(8,128)(2,1)S(1)}, bf16[2,160,1152]{2,1,0:T(8,128)(2,1)S(1)}, u32[]{:S(2)}, u32[]{:S(2)}) collective-permute-start(bf16[2,160,1152]{2,1,0:T(8,128)(2,1)S(1)} %slice_bitcast_fusion.23), channel_id=1, source_target_pairs={{0,2},{1,3},{2,0},{3,1},{4,6},{5,7},{6,4},{7,5},{8,10},{9,11},{10,... | collective-permute-start | bytes 2211848 | tf_op jit(solution)/shard_map/ppermute | solution.py:21
  299.8 346.9 %reduce-scatter.4.cloned.1.call-start = ((), (), s32[]{:S(2)}) async-start(), calls=%async_computation.6 | async-start | bytes 6635520 | tf_op jit(solution)/shard_map/reduce_scatter | solution.py:582
  326.8 10.5 collective-permute-start.20
  339.5 17.4 %collective-permute-start.22 = (bf16[2,160,1152]{2,1,0:T(8,128)(2,1)S(1)}, bf16[2,160,1152]{2,1,0:T(8,128)(2,1)S(1)}, u32[]{:S(2)}, u32[]{:S(2)}) collective-permute-start(bf16[2,160,1152]{2,1,0:T(8,128)(2,1)S(1)} %pad_maximum_fusion.16), channel_id=1, source_target_pairs={{0,2},{1,3},{2,0},{3,1},{4,6},{5,7},{6,4},{7,5},{8,10},{9,11},{10,... | collective-permute-start | bytes 2211848 | tf_op jit(solution)/shard_map/ppermute | solution.py:21
  341.1 17.0 %collective-permute-start.23 = (bf16[2,160,1152]{2,1,0:T(8,128)(2,1)S(1)}, bf16[2,160,1152]{2,1,0:T(8,128)(2,1)S(1)}, u32[]{:S(2)}, u32[]{:S(2)}) collective-permute-start(bf16[2,160,1152]{2,1,0:T(8,128)(2,1)S(1)} %pad_maximum_fusion.17), channel_id=1, source_target_pairs={{0,16},{16,0},{1,17},{17,1},{2,18},{18,2},{3,19},{19,3},{4,20},{20... | collective-permute-start | bytes 2211848 | tf_op jit(solution)/shard_map/ppermute | solution.py:21
  453.7 18.6 %collective-permute-start.26 = (bf16[2,160,1152]{2,1,0:T(8,128)(2,1)S(1)}, bf16[2,160,1152]{2,1,0:T(8,128)(2,1)S(1)}, u32[]{:S(2)}, u32[]{:S(2)}) collective-permute-start(bf16[2,160,1152]{2,1,0:T(8,128)(2,1)S(1)} %slice_bitcast_fusion.20), channel_id=1, source_target_pairs={{0,16},{16,0},{1,17},{17,1},{2,18},{18,2},{3,19},{19,3},{4,20},{20... | collective-permute-start | bytes 2211848 | tf_op jit(solution)/shard_map/ppermute | solution.py:21
  455.3 18.2 %collective-permute-start.27 = (bf16[2,160,1152]{2,1,0:T(8,128)(2,1)S(1)}, bf16[2,160,1152]{2,1,0:T(8,128)(2,1)S(1)}, u32[]{:S(2)}, u32[]{:S(2)}) collective-permute-start(bf16[2,160,1152]{2,1,0:T(8,128)(2,1)S(1)} %slice_bitcast_fusion.19), channel_id=1, source_target_pairs={{0,2},{1,3},{2,0},{3,1},{4,6},{5,7},{6,4},{7,5},{8,10},{9,11},{10,... | collective-permute-start | bytes 2211848 | tf_op jit(solution)/shard_map/ppermute | solution.py:21
  501.7 15.4 %collective-permute-start.32 = (bf16[2,160,1152]{2,1,0:T(8,128)(2,1)S(1)}, bf16[2,160,1152]{2,1,0:T(8,128)(2,1)S(1)}, u32[]{:S(2)}, u32[]{:S(2)}) collective-permute-start(bf16[2,160,1152]{2,1,0:T(8,128)(2,1)S(1)} %pad_maximum_fusion.18), channel_id=1, source_target_pairs={{0,2},{1,3},{2,0},{3,1},{4,6},{5,7},{6,4},{7,5},{8,10},{9,11},{10,... | collective-permute-start | bytes 2211848 | tf_op jit(solution)/shard_map/ppermute | solution.py:21
  503.2 14.7 %collective-permute-start.33 = (bf16[2,160,1152]{2,1,0:T(8,128)(2,1)S(1)}, bf16[2,160,1152]{2,1,0:T(8,128)(2,1)S(1)}, u32[]{:S(2)}, u32[]{:S(2)}) collective-permute-start(bf16[2,160,1152]{2,1,0:T(8,128)(2,1)S(1)} %pad_maximum_fusion.19), channel_id=1, source_target_pairs={{0,16},{16,0},{1,17},{17,1},{2,18},{18,2},{3,19},{19,3},{4,20},{20... | collective-permute-start | bytes 2211848 | tf_op jit(solution)/shard_map/ppermute | solution.py:21
  539.6 204.5 %reduce-scatter.6.cloned.1.call-start = ((), (), s32[]{:S(2)}) async-start(), calls=%async_computation.7 | async-start | bytes 6635520 | tf_op jit(solution)/shard_map/reduce_scatter | solution.py:582
  601.0 18.8 %collective-permute-start.36 = (bf16[2,160,1152]{2,1,0:T(8,128)(2,1)}, bf16[2,160,1152]{2,1,0:T(8,128)(2,1)}, u32[]{:S(2)}, u32[]{:S(2)}) collective-permute-start(bf16[2,160,1152]{2,1,0:T(8,128)(2,1)} %slice_bitcast_fusion.16), channel_id=1, source_target_pairs={{0,16},{16,0},{1,17},{17,1},{2,18},{18,2},{3,19},{19,3},{4,20},{20... | collective-permute-start | bytes 2211848 | tf_op jit(solution)/shard_map/ppermute | solution.py:21
  602.2 18.6 %collective-permute-start.37 = (bf16[2,160,1152]{2,1,0:T(8,128)(2,1)}, bf16[2,160,1152]{2,1,0:T(8,128)(2,1)}, u32[]{:S(2)}, u32[]{:S(2)}) collective-permute-start(bf16[2,160,1152]{2,1,0:T(8,128)(2,1)} %slice_bitcast_fusion.15), channel_id=1, source_target_pairs={{0,2},{1,3},{2,0},{3,1},{4,6},{5,7},{6,4},{7,5},{8,10},{9,11},{10,... | collective-permute-start | bytes 2211848 | tf_op jit(solution)/shard_map/ppermute | solution.py:21
  625.3 13.9 %collective-permute-start.38 = (bf16[160,1152]{1,0:T(8,128)(2,1)}, bf16[160,1152]{1,0:T(8,128)(2,1)}, u32[]{:S(2)}, u32[]{:S(2)}) collective-permute-start(bf16[160,1152]{1,0:T(8,128)(2,1)} %fusion.94), channel_id=1, source_target_pairs={{0,2},{1,3},{2,0},{3,1},{4,6},{5,7},{6,4},{7,5},{8,10},{9,11},{10,... | collective-permute-start | bytes 1105928 | tf_op jit(solution)/shard_map/ppermute | solution.py:21
  626.1 330.4 %reduce-scatter.8.cloned.1.call-start = ((), (), s32[]{:S(2)}) async-start(), calls=%async_computation.8 | async-start | bytes 6635520 | tf_op jit(solution)/shard_map/reduce_scatter | solution.py:582
  626.2 14.4 %collective-permute-start.39 = (bf16[160,1152]{1,0:T(8,128)(2,1)}, bf16[160,1152]{1,0:T(8,128)(2,1)}, u32[]{:S(2)}, u32[]{:S(2)}) collective-permute-start(bf16[160,1152]{1,0:T(8,128)(2,1)} %fusion.95), channel_id=1, source_target_pairs={{0,16},{16,0},{1,17},{17,1},{2,18},{18,2},{3,19},{19,3},{4,20},{20... | collective-permute-start | bytes 1105928 | tf_op jit(solution)/shard_map/ppermute | solution.py:21
  657.0 15.7 %collective-permute-start.42 = (bf16[2,160,1152]{2,1,0:T(8,128)(2,1)S(1)}, bf16[2,160,1152]{2,1,0:T(8,128)(2,1)S(1)}, u32[]{:S(2)}, u32[]{:S(2)}) collective-permute-start(bf16[2,160,1152]{2,1,0:T(8,128)(2,1)S(1)} %pad_maximum_fusion.20), channel_id=1, source_target_pairs={{0,2},{1,3},{2,0},{3,1},{4,6},{5,7},{6,4},{7,5},{8,10},{9,11},{10,... | collective-permute-start | bytes 2211848 | tf_op jit(solution)/shard_map/ppermute | solution.py:21
  658.2 15.5 %collective-permute-start.43 = (bf16[2,160,1152]{2,1,0:T(8,128)(2,1)S(1)}, bf16[2,160,1152]{2,1,0:T(8,128)(2,1)S(1)}, u32[]{:S(2)}, u32[]{:S(2)}) collective-permute-start(bf16[2,160,1152]{2,1,0:T(8,128)(2,1)S(1)} %pad_maximum_fusion.21), channel_id=1, source_target_pairs={{0,16},{16,0},{1,17},{17,1},{2,18},{18,2},{3,19},{19,3},{4,20},{20... | collective-permute-start | bytes 2211848 | tf_op jit(solution)/shard_map/ppermute | solution.py:21
  688.9 33.7 %collective-permute-start.45 = (bf16[576,1152]{1,0:T(8,128)(2,1)}, bf16[576,1152]{1,0:T(8,128)(2,1)}, u32[]{:S(2)}, u32[]{:S(2)}) collective-permute-start(bf16[576,1152]{1,0:T(8,128)(2,1)} %reduce-scatter.4.cloned.1.call-done), channel_id=1, source_target_pairs={{0,16},{16,0},{1,17},{17,1},{2,18},{18,2},{3,19},{19,3},{4,20},{20... | collective-permute-start | bytes 3981320 | tf_op jit(solution)/shard_map/ppermute | solution.py:21
  692.5 51.7 %collective-permute-start.47 = (bf16[160,2304]{1,0:T(8,128)(2,1)S(1)}, bf16[160,2304]{1,0:T(8,128)(2,1)}, u32[]{:S(2)}, u32[]{:S(2)}) collective-permute-start(bf16[160,2304]{1,0:T(8,128)(2,1)S(1)} %copy-done.46), channel_id=1, source_target_pairs={{0,2},{1,3},{2,0},{3,1},{4,6},{5,7},{6,4},{7,5},{8,10},{9,11},{10,... | collective-permute-start | bytes 2211848 | tf_op jit(solution)/shard_map/ppermute | solution.py:21
  725.7 16.2 %collective-permute-start.46 = (bf16[2,640,256]{2,1,0:T(8,128)(2,1)S(1)}, bf16[2,640,256]{2,1,0:T(8,128)(2,1)S(1)}, u32[]{:S(2)}, u32[]{:S(2)}) collective-permute-start(bf16[2,640,256]{2,1,0:T(8,128)(2,1)S(1)} %get-tuple-element.275), channel_id=1, source_target_pairs={{0,16},{16,0},{1,17},{17,1},{2,18},{18,2},{3,19},{19,3},{4,20},{20... | collective-permute-start | bytes 1966088 | tf_op jit(solution)/shard_map/ppermute | solution.py:21
  744.1 21.6 %collective-permute-start.49 = (bf16[2,640,256]{2,1,0:T(8,128)(2,1)}, bf16[2,640,256]{2,1,0:T(8,128)(2,1)S(1)}, u32[]{:S(2)}, u32[]{:S(2)}) collective-permute-start(bf16[2,640,256]{2,1,0:T(8,128)(2,1)} %get-tuple-element.204), channel_id=1, source_target_pairs={{0,16},{16,0},{1,17},{17,1},{2,18},{18,2},{3,19},{19,3},{4,20},{20... | collective-permute-start | bytes 1966088 | tf_op jit(solution)/shard_map/ppermute | solution.py:21
  745.5 36.8 %collective-permute-start.50 = (bf16[2,640,256]{2,1,0:T(8,128)(2,1)}, bf16[2,640,256]{2,1,0:T(8,128)(2,1)S(1)}, u32[]{:S(2)}, u32[]{:S(2)}) collective-permute-start(bf16[2,640,256]{2,1,0:T(8,128)(2,1)} %fusion.37), channel_id=1, source_target_pairs={{0,4},{4,8},{8,12},{12,0},{1,5},{5,9},{9,13},{13,1},{2,6},{6,10},{... | collective-permute-start | bytes 1966088 | tf_op jit(solution)/shard_map/ppermute | solution.py:38
  783.6 20.4 %collective-permute-start.51 = (bf16[2,640,256]{2,1,0:T(8,128)(2,1)S(1)}, bf16[2,640,256]{2,1,0:T(8,128)(2,1)S(1)}, u32[]{:S(2)}, u32[]{:S(2)}) collective-permute-start(bf16[2,640,256]{2,1,0:T(8,128)(2,1)S(1)} %copy-done.49), channel_id=1, source_target_pairs={{0,16},{16,0},{1,17},{17,1},{2,18},{18,2},{3,19},{19,3},{4,20},{20... | collective-permute-start | bytes 1966088 | tf_op jit(solution)/shard_map/ppermute | solution.py:21
  784.4 50.2 %collective-permute-start.52 = (bf16[2,640,256]{2,1,0:T(8,128)(2,1)S(1)}, bf16[2,640,256]{2,1,0:T(8,128)(2,1)S(1)}, u32[]{:S(2)}, u32[]{:S(2)}) collective-permute-start(bf16[2,640,256]{2,1,0:T(8,128)(2,1)S(1)} %fusion.33), channel_id=1, source_target_pairs={{0,4},{4,8},{8,12},{12,0},{1,5},{5,9},{9,13},{13,1},{2,6},{6,10},{... | collective-permute-start | bytes 1966088 | tf_op jit(solution)/shard_map/ppermute | solution.py:38
  803.7 51.9 %collective-permute-start.48 = (bf16[2,640,256]{2,1,0:T(8,128)(2,1)S(1)}, bf16[2,640,256]{2,1,0:T(8,128)(2,1)S(1)}, u32[]{:S(2)}, u32[]{:S(2)}) collective-permute-start(bf16[2,640,256]{2,1,0:T(8,128)(2,1)S(1)} %copy-done.48), channel_id=1, source_target_pairs={{0,16},{16,0},{1,17},{17,1},{2,18},{18,2},{3,19},{19,3},{4,20},{20... | collective-permute-start | bytes 1966088 | tf_op jit(solution)/shard_map/ppermute | solution.py:21
  836.0 37.0 %collective-permute-start.53 = (bf16[2,640,256]{2,1,0:T(8,128)(2,1)S(1)}, bf16[2,640,256]{2,1,0:T(8,128)(2,1)S(1)}, u32[]{:S(2)}, u32[]{:S(2)}) collective-permute-start(bf16[2,640,256]{2,1,0:T(8,128)(2,1)S(1)} %fusion.35), channel_id=1, source_target_pairs={{0,4},{4,8},{8,12},{12,0},{1,5},{5,9},{9,13},{13,1},{2,6},{6,10},{... | collective-permute-start | bytes 1966088 | tf_op jit(solution)/shard_map/ppermute | solution.py:38
  850.7 30.9 %collective-permute-start.54 = (bf16[576,256]{1,0:T(8,128)(2,1)S(1)}, bf16[576,256]{1,0:T(8,128)(2,1)S(1)}, u32[]{:S(2)}, u32[]{:S(2)}) collective-permute-start(bf16[576,256]{1,0:T(8,128)(2,1)S(1)} %get-tuple-element.213), channel_id=1, source_target_pairs={{0,4},{4,0},{8,12},{12,8},{1,5},{5,1},{9,13},{13,9},{2,6},{6,2},{1... | collective-permute-start | bytes 884744 | tf_op jit(solution)/shard_map/ppermute | solution.py:21
  853.2 28.9 %collective-permute-start.55 = (bf16[576,256]{1,0:T(8,128)(2,1)S(1)}, bf16[576,256]{1,0:T(8,128)(2,1)S(1)}, u32[]{:S(2)}, u32[]{:S(2)}) collective-permute-start(bf16[576,256]{1,0:T(8,128)(2,1)S(1)} %get-tuple-element.214), channel_id=1, source_target_pairs={{0,8},{4,12},{8,0},{12,4},{1,9},{5,13},{9,1},{13,5},{2,10},{6,14},... | collective-permute-start | bytes 884744 | tf_op jit(solution)/shard_map/ppermute | solution.py:21
  853.4 36.8 %collective-permute-start.56 = (bf16[576,256]{1,0:T(8,128)(2,1)S(1)}, bf16[576,256]{1,0:T(8,128)(2,1)S(1)}, u32[]{:S(2)}, u32[]{:S(2)}) collective-permute-start(bf16[576,256]{1,0:T(8,128)(2,1)S(1)} %get-tuple-element.215), channel_id=1, source_target_pairs={{0,12},{4,8},{8,4},{12,0},{1,13},{5,9},{9,5},{13,1},{2,14},{6,10},... | collective-permute-start | bytes 884744 | tf_op jit(solution)/shard_map/ppermute | solution.py:21
  909.4 19.4 %collective-permute-start.58 = (bf16[2,160,1152]{2,1,0:T(8,128)(2,1)S(1)}, bf16[2,160,1152]{2,1,0:T(8,128)(2,1)S(1)}, u32[]{:S(2)}, u32[]{:S(2)}) collective-permute-start(bf16[2,160,1152]{2,1,0:T(8,128)(2,1)S(1)} %slice_bitcast_fusion.12), channel_id=1, source_target_pairs={{0,16},{16,0},{1,17},{17,1},{2,18},{18,2},{3,19},{19,3},{4,20},{20... | collective-permute-start | bytes 2211848 | tf_op jit(solution)/shard_map/ppermute | solution.py:21
  910.9 18.4 %collective-permute-start.59 = (bf16[2,160,1152]{2,1,0:T(8,128)(2,1)S(1)}, bf16[2,160,1152]{2,1,0:T(8,128)(2,1)}, u32[]{:S(2)}, u32[]{:S(2)}) collective-permute-start(bf16[2,160,1152]{2,1,0:T(8,128)(2,1)S(1)} %slice_bitcast_fusion.11), channel_id=1, source_target_pairs={{0,2},{1,3},{2,0},{3,1},{4,6},{5,7},{6,4},{7,5},{8,10},{9,11},{10,... | collective-permute-start | bytes 2211848 | tf_op jit(solution)/shard_map/ppermute | solution.py:21
  916.1 40.4 %collective-permute-start.60 = (bf16[576,1152]{1,0:T(8,128)(2,1)}, bf16[576,1152]{1,0:T(8,128)(2,1)}, u32[]{:S(2)}, u32[]{:S(2)}) collective-permute-start(bf16[576,1152]{1,0:T(8,128)(2,1)} %reduce-scatter.6.cloned.1.call-done), channel_id=1, source_target_pairs={{0,16},{16,0},{1,17},{17,1},{2,18},{18,2},{3,19},{19,3},{4,20},{20... | collective-permute-start | bytes 3981320 | tf_op jit(solution)/shard_map/ppermute | solution.py:21
  983.0 11.2 %collective-permute-start.72 = (f32[4,2304]{1,0:T(4,128)S(1)}, f32[4,2304]{1,0:T(4,128)S(1)}, u32[]{:S(2)}, u32[]{:S(2)}) collective-permute-start(f32[4,2304]{1,0:T(4,128)S(1)} %add.422), channel_id=1, source_target_pairs={{0,4},{4,0},{8,12},{12,8},{1,5},{5,1},{9,13},{13,9},{2,6},{6,2},{1... | collective-permute-start | bytes 110600 | tf_op jit(solution)/shard_map/ppermute | solution.py:21
  989.1 32.0 %collective-permute-start.75 = (bf16[576,256]{1,0:T(8,128)(2,1)S(1)}, bf16[576,256]{1,0:T(8,128)(2,1)S(1)}, u32[]{:S(2)}, u32[]{:S(2)}) collective-permute-start(bf16[576,256]{1,0:T(8,128)(2,1)S(1)} %copy-done.56), channel_id=1, source_target_pairs={{0,4},{4,0},{8,12},{12,8},{1,5},{5,1},{9,13},{13,9},{2,6},{6,2},{1... | collective-permute-start | bytes 884744 | tf_op jit(solution)/shard_map/ppermute | solution.py:21
  989.5 31.6 %collective-permute-start.76 = (bf16[576,256]{1,0:T(8,128)(2,1)S(1)}, bf16[576,256]{1,0:T(8,128)(2,1)S(1)}, u32[]{:S(2)}, u32[]{:S(2)}) collective-permute-start(bf16[576,256]{1,0:T(8,128)(2,1)S(1)} %copy-done.55), channel_id=1, source_target_pairs={{0,8},{4,12},{8,0},{12,4},{1,9},{5,13},{9,1},{13,5},{2,10},{6,14},... | collective-permute-start | bytes 884744 | tf_op jit(solution)/shard_map/ppermute | solution.py:21
  991.2 31.9 %collective-permute-start.77 = (bf16[576,256]{1,0:T(8,128)(2,1)S(1)}, bf16[576,256]{1,0:T(8,128)(2,1)S(1)}, u32[]{:S(2)}, u32[]{:S(2)}) collective-permute-start(bf16[576,256]{1,0:T(8,128)(2,1)S(1)} %copy-done.54), channel_id=1, source_target_pairs={{0,12},{4,8},{8,4},{12,0},{1,13},{5,9},{9,5},{13,1},{2,14},{6,10},... | collective-permute-start | bytes 884744 | tf_op jit(solution)/shard_map/ppermute | solution.py:21
  993.6 32.0 %collective-permute-start.64 = (bf16[160,2304]{1,0:T(8,128)(2,1)S(1)}, bf16[160,2304]{1,0:T(8,128)(2,1)S(1)}, u32[]{:S(2)}, u32[]{:S(2)}) collective-permute-start(bf16[160,2304]{1,0:T(8,128)(2,1)S(1)} %fusion.19), channel_id=1, source_target_pairs={{0,2},{1,3},{2,0},{3,1},{4,6},{5,7},{6,4},{7,5},{8,10},{9,11},{10,... | collective-permute-start | bytes 2211848 | tf_op jit(solution)/shard_map/ppermute | solution.py:21
  994.2 24.7 %collective-permute-start.73 = (f32[4,2304]{1,0:T(4,128)S(1)}, f32[4,2304]{1,0:T(4,128)S(1)}, u32[]{:S(2)}, u32[]{:S(2)}) collective-permute-start(f32[4,2304]{1,0:T(4,128)S(1)} %add.423), channel_id=1, source_target_pairs={{0,8},{4,12},{8,0},{12,4},{1,9},{5,13},{9,1},{13,5},{2,10},{6,14},... | collective-permute-start | bytes 110600 | tf_op jit(solution)/shard_map/ppermute | solution.py:21
  1018.9 39.6 %collective-permute-start.79 = (bf16[576,1152]{1,0:T(8,128)(2,1)S(1)}, bf16[576,1152]{1,0:T(8,128)(2,1)S(1)}, u32[]{:S(2)}, u32[]{:S(2)}) collective-permute-start(bf16[576,1152]{1,0:T(8,128)(2,1)S(1)} %copy-done.45), channel_id=1, source_target_pairs={{0,16},{16,0},{1,17},{17,1},{2,18},{18,2},{3,19},{19,3},{4,20},{20... | collective-permute-start | bytes 3981320 | tf_op jit(solution)/shard_map/ppermute | solution.py:21
  1021.1 12.3 %collective-permute-start.65 = (bf16[576,256]{1,0:T(8,128)(2,1)S(1)}, bf16[576,256]{1,0:T(8,128)(2,1)S(1)}, u32[]{:S(2)}, u32[]{:S(2)}) collective-permute-start(bf16[576,256]{1,0:T(8,128)(2,1)S(1)} %copy-done.53), channel_id=1, source_target_pairs={{0,4},{4,0},{8,12},{12,8},{1,5},{5,1},{9,13},{13,9},{2,6},{6,2},{1... | collective-permute-start | bytes 884744 | tf_op jit(solution)/shard_map/ppermute | solution.py:21
  1021.1 22.8 %collective-permute-start.66 = (bf16[576,256]{1,0:T(8,128)(2,1)S(1)}, bf16[576,256]{1,0:T(8,128)(2,1)S(1)}, u32[]{:S(2)}, u32[]{:S(2)}) collective-permute-start(bf16[576,256]{1,0:T(8,128)(2,1)S(1)} %copy-done.52), channel_id=1, source_target_pairs={{0,8},{4,12},{8,0},{12,4},{1,9},{5,13},{9,1},{13,5},{2,10},{6,14},... | collective-permute-start | bytes 884744 | tf_op jit(solution)/shard_map/ppermute | solution.py:21
  1023.1 20.8 %collective-permute-start.67 = (bf16[576,256]{1,0:T(8,128)(2,1)S(1)}, bf16[576,256]{1,0:T(8,128)(2,1)S(1)}, u32[]{:S(2)}, u32[]{:S(2)}) collective-permute-start(bf16[576,256]{1,0:T(8,128)(2,1)S(1)} %get-tuple-element.231), channel_id=1, source_target_pairs={{0,12},{4,8},{8,4},{12,0},{1,13},{5,9},{9,5},{13,1},{2,14},{6,10},... | collective-permute-start | bytes 884744 | tf_op jit(solution)/shard_map/ppermute | solution.py:21
  1025.6 43.5 %collective-permute-start.63 = (bf16[2,160,2304]{2,1,0:T(8,128)(2,1)S(1)}, bf16[2,160,2304]{2,1,0:T(8,128)(2,1)S(1)}, u32[]{:S(2)}, u32[]{:S(2)}) collective-permute-start(bf16[2,160,2304]{2,1,0:T(8,128)(2,1)S(1)} %get-tuple-element.227), channel_id=1, source_target_pairs={{0,1},{1,0},{2,3},{3,2},{4,5},{5,4},{6,7},{7,6},{8,9},{9,8},{10,11... | collective-permute-start | bytes 4423688 | tf_op jit(solution)/shard_map/ppermute | solution.py:21
  1033.4 23.9 %collective-permute-start.78 = (bf16[576,256]{1,0:T(8,128)(2,1)S(1)}, bf16[576,256]{1,0:T(8,128)(2,1)S(1)}, u32[]{:S(2)}, u32[]{:S(2)}) collective-permute-start(bf16[576,256]{1,0:T(8,128)(2,1)S(1)} %fusion.83), channel_id=1, source_target_pairs={{0,16},{16,0},{1,17},{17,1},{2,18},{18,2},{3,19},{19,3},{4,20},{20... | collective-permute-start | bytes 884744 | tf_op jit(solution)/shard_map/ppermute | solution.py:21
  1045.2 21.6 %collective-permute-start.74 = (bf16[576,512]{1,0:T(8,128)(2,1)S(1)}, bf16[576,512]{1,0:T(8,128)(2,1)S(1)}, u32[]{:S(2)}, u32[]{:S(2)}) collective-permute-start(bf16[576,512]{1,0:T(8,128)(2,1)S(1)} %pad_maximum_fusion.28), channel_id=1, source_target_pairs={{0,16},{16,0},{1,17},{17,1},{2,18},{18,2},{3,19},{19,3},{4,20},{20... | collective-permute-start | bytes 1769480 | tf_op jit(solution)/shard_map/ppermute | solution.py:21
  1045.8 23.6 %collective-permute-start.68 = (bf16[2,160,2304]{2,1,0:T(8,128)(2,1)S(1)}, bf16[2,160,2304]{2,1,0:T(8,128)(2,1)S(1)}, u32[]{:S(2)}, u32[]{:S(2)}) collective-permute-start(bf16[2,160,2304]{2,1,0:T(8,128)(2,1)S(1)} %pad_maximum_fusion.15), channel_id=1, source_target_pairs={{0,1},{1,0},{2,3},{3,2},{4,5},{5,4},{6,7},{7,6},{8,9},{9,8},{10,11... | collective-permute-start | bytes 4423688 | tf_op jit(solution)/shard_map/ppermute | solution.py:21
  (94 other events, 807.8 us)
Sparse Core Ops, SparseCore 0:
  71.7 130.9 all-gather.3
  213.1 113.6 all-gather.5
  328.3 98.1 all-gather.7
  539.7 92.2 reduce-scatter.3
  634.9 95.3 reduce-scatter.5
  733.0 146.5 reduce-scatter.7

commit v3 on v2

--- a/solution.py
+++ b/solution.py
@@ -64,9 +64,9 @@
     a, b = jnp.stack([a, swap_x(a)]), jnp.stack([b, swap_y(b)])
     a, b = at(plan, 1, [a, b])
     a, b = jnp.stack([a, swap_y(a)]), jnp.stack([b, swap_x(b)], axis=1)
-    chip = jnp.concatenate([a, b], axis=-1)
+    chip = jnp.concatenate([a, b], axis=-1).reshape(4 * own.shape[0], -1)
     (chip,) = at(plan, 2, [chip])
-    return jnp.stack([chip, swap_core(chip)]).reshape(8 * own.shape[0], -1)
+    return chip, swap_core(chip)
 
 
 def send(part, mover):
@@ -80,9 +80,9 @@
     cut = width // 2
     part = part.reshape(2, 2, rows, width)
     a, b = part[..., :cut], part[..., cut:]
-    give_a, give_b = at(plan, 1, [a[:, 1].astype(bf16), b[1].astype(bf16)])
-    a = a[:, 0] + swap_x(give_a).astype(f32)
-    b = b[0] + swap_y(give_b).astype(f32)
+    give_a, give_b = at(plan, 1, [a[:, 1], b[1]])
+    a = a[:, 0].astype(f32) + swap_x(give_a).astype(f32)
+    b = b[0].astype(f32) + swap_y(give_b).astype(f32)
     give_a, give_b = at(plan, 2, [a[1].astype(bf16), b[1].astype(bf16)])
     a = a[0] + swap_y(give_a).astype(f32)
     b = b[0] + swap_x(give_b).astype(f32)
@@ -467,6 +467,15 @@
     def z_move(value, bits):
         return Move(value, functools.partial(swap, axis="fsdp", bit=bits))
 
+    def gathered(part):
+        return lax.all_gather(part, "fsdp", axis=0, tiled=True)
+
+    gate_w, up_w = (
+        Move(lax.dynamic_slice_in_dim(weight, x * units, units, 1), gathered)
+        for weight in (gate_weight, up_weight)
+    )
+    down_w = Move(lax.dynamic_slice_in_dim(down_weight, x * units, units, 0).T, gathered)
+    down_w.result = gathered(down_w.value)
     w_own = jnp.concatenate(
         [
             lax.dynamic_slice_in_dim(query_weight, x * HD, HD, 1),
@@ -485,20 +494,14 @@
     far_move = Move(to_far, swap_x)
     far_move.result = swap_x(to_far)
     for i in range(1, zs):
-        (block,) = step([ring[-1]], end=[far_move] if i == zs - 1 else [])
+        final = i == zs - 1
+        (block,) = step(
+            [ring[-1]], begin=[gate_w] if i == 2 else [], end=[far_move] if final else []
+        )
         ring.append(turn(block))
     far_x = far_move.result
     far_x = jnp.concatenate([far_x, swap_core(far_x)]).reshape(rows, width)
 
-    def gathered(part):
-        return lax.all_gather(part, "fsdp", axis=0, tiled=True)
-
-    gate_w, up_w = (
-        Move(lax.dynamic_slice_in_dim(weight, x * units, units, 1), gathered)
-        for weight in (gate_weight, up_weight)
-    )
-    down_w = Move(lax.dynamic_slice_in_dim(down_weight, x * units, units, 0).T, gathered)
-    down_w.result = gathered(down_w.value)
     w_out_own = lax.dynamic_slice_in_dim(out_weight, x * HD, HD, 0).T
     out_moves = {j: z_move(w_out_own, j) for j in range(1, zs)}
     def assemble(own, moves):
@@ -519,7 +522,6 @@
         w_qkv = lax.dynamic_update_slice_in_dim(w_qkv, part[:depth], place * depth, 0)
         part = part[depth:].reshape(-1)[: 4 * depth].reshape(1, 4, depth)
         all_gains = lax.dynamic_update_slice_in_dim(all_gains, part, place, 0)
-    (w_qkv,) = step([w_qkv], begin=[gate_w])
     all_gains = all_gains.transpose(1, 0, 2).reshape(4, width).astype(f32)
     pre_gain, post_gain, mlp_pre, mlp_post = (all_gains[i] for i in range(4))
     h_own, own_part = norm_product(own_x.reshape(rows, width), pre_gain, w_qkv)
@@ -559,7 +561,7 @@
     o_rows = to_exchange(mixed)
     o_halves = halves(o_rows)
     a_sum = scatter8(
-        lambda got: rows_product(o_halves[0], w_out, NT, f32, got),
+        lambda got: rows_product(o_halves[0], w_out, NT, bf16, got),
         lambda: rows_product(o_halves[1], w_out, NT, bf16),
         {},
     )
@@ -567,11 +569,13 @@
     x_own = lax.dynamic_slice_in_dim(layer_in[0], t * sub, sub, 0).astype(f32)
     r_one = x_own + rms_norm(a_sum, post_gain)
     h_two = gather8(rms_norm(r_one, mlp_pre).astype(bf16), {0: ((), [up_w])})
-    gate, up, hidden = gated_product(h_two, gate_w.result, up_w.result)
-    hidden_halves = halves(hidden)
+    gate, up, hidden = zip(
+        *(gated_product(part, gate_w.result, up_w.result) for part in h_two)
+    )
+    hidden = step(hidden)
     m_sum = scatter8(
-        lambda got: rows_product(hidden_halves[0], down_w.result, NT, f32, got),
-        lambda: rows_product(hidden_halves[1], down_w.result, NT, bf16),
+        lambda got: rows_product(hidden[0], down_w.result, NT, bf16, got),
+        lambda: rows_product(hidden[1], down_w.result, NT, bf16),
         {},
     )
     layer_own = (r_one + rms_norm(m_sum, mlp_post)).astype(bf16)
@@ -582,9 +586,10 @@
         return lax.psum_scatter(grad, "fsdp", scatter_dimension=0, tiled=True)
 
     class Unit:
-        def __init__(self, grad):
+        def __init__(self, grad, held=False):
             self.sum = Move(grad, scattered)
-            self.sum.result = scattered(grad)
+            if not held:
+                self.sum.result = scattered(grad)
 
         def paired(self):
             self.over = [Move(self.sum.result, swap_x)]
@@ -604,21 +609,22 @@
         def __getitem__(self, place):
             return self.places[place]()
 
-    def product(pair):
-        return sum_over_rows([pair], bf16)
+    def product(given):
+        return sum_over_rows(list(zip(*given)), bf16)
 
     dm = gather8(d_msum.astype(bf16), {})
     down_work = Move((dm, hidden), product)
-    (dm,) = step([dm], begin=[down_work])
-    (dm,) = step([dm], end=[down_work])
+    dm = step(dm, begin=[down_work])
+    dm = step(dm, end=[down_work])
     down_unit = Unit(down_work.result)
-    d_gate, d_up = gated_back(dm, down_w.result, gate, up)
+    d_gate, d_up = zip(
+        *(gated_back(part, down_w.result, *have) for part, *have in zip(dm, gate, up))
+    )
     gate_work, up_work = Move((h_two, d_gate), product), Move((h_two, d_up), product)
-    d_halves = list(zip(halves(d_gate), halves(d_up)))
     weights = (gate_w.result, up_w.result)
     dh_two = scatter8(
-        lambda got: rows_product(d_halves[0], weights, NT, f32, got),
-        lambda: rows_product(d_halves[1], weights, NT, bf16),
+        lambda got: rows_product((d_gate[0], d_up[0]), weights, NT, bf16, got),
+        lambda: rows_product((d_gate[1], d_up[1]), weights, NT, bf16),
         {1: ([gate_work], ()), 2: ([up_work], [gate_work])},
     )
     gate_unit = Unit(gate_work.result)
@@ -627,14 +633,35 @@
     d_asum, dg_post = norm_back(a_sum, post_gain, d_resid)
 
     (da,) = step([d_asum.astype(bf16)], end=[up_work, down_unit.sum])
-    up_unit = Unit(up_work.result)
+    up_unit = Unit(up_work.result, held=True)
     da = gather8(da, {})
-    d_mixed = to_sequence(rows_product(da, w_out, NN, bf16))
-    out_work = Move((da, o_rows), lambda pair: sum_over_rows([pair]))
+    def qkv_grad(rows_in, kind=f32):
+        parts = rows_in.reshape(2, 2, 2, sub, HD)
+        near = parts[:, :, 0].reshape(rows, HD)
+        far = parts[:, :, 1].reshape(rows, HD)
+        return sum_over_rows([(h_own, near), (h_far, far)], kind)
+
+    def sends(grad):
+        moves = [
+            z_move(lax.dynamic_index_in_dim(grad, z ^ j, 0, False).astype(bf16), j)
+            for j in range(1, zs)
+        ]
+        return lax.dynamic_index_in_dim(grad, z, 0, False), moves
+
+    def received(pair_of):
+        near, moves = pair_of
+        for move in moves:
+            near = near + move.result.astype(f32)
+        return near.astype(bf16)
+
+    d_mixed = to_sequence(jnp.concatenate([rows_product(part, w_out, NN, bf16) for part in da]))
+    out_work = Move((da, o_halves), product)
+    da = step(da, begin=[out_work])
     delta = jnp.sum(d_mixed.astype(f32) * mixed.astype(f32), axis=-1)
     steps = rows // block
     layer_y = Move(layer_own, swap_y)
-    d_mixed, delta = step([d_mixed, delta], begin=down_unit.paired() + [layer_y, out_work])
+    d_mixed, delta = step([d_mixed, delta], end=[out_work])
+    d_mixed, delta = step([d_mixed, delta], begin=down_unit.paired() + [layer_y])
     d_query, dkv_all = attend_back(
         info,
         q_cast,
@@ -646,89 +673,73 @@
         doc_row.reshape(steps, 1, block),
         block,
     )
-    (dkv_all,) = step([dkv_all], end=down_unit.over + [out_work])
+    (dkv_all,) = step([dkv_all], end=down_unit.over)
     q_rows = to_exchange(rotate(d_query * q_scale, cos_tab, -sine_tab).astype(bf16))
 
-    def qkv_grad(rows_in):
-        parts = rows_in.reshape(2, 2, 2, sub, HD)
-        near = parts[:, :, 0].reshape(rows, HD)
-        far = parts[:, :, 1].reshape(rows, HD)
-        return sum_over_rows([(h_own, near), (h_far, far)]).reshape(zs, depth, HD)
-
-    def sends(grad):
-        moves = [
-            z_move(lax.dynamic_index_in_dim(grad, z ^ j, 0, False).astype(bf16), j)
-            for j in range(1, zs)
-        ]
-        return lax.dynamic_index_in_dim(grad, z, 0, False), moves
-
-    def received(pair_of):
-        near, moves = pair_of
-        for move in moves:
-            near = near + move.result.astype(f32)
-        return near.astype(bf16)
-
+    q_work = Move(q_rows, lambda part: qkv_grad(part, bf16))
+    (dkv_all,) = step([dkv_all], begin=[q_work])
     kept, given = dkv_all[0], dkv_all[1]
     order = list(range(1, zs)) + [0]
     acc = kept[order[0]].astype(f32) + send(given[order[0]], swap_x)
     for n, i in enumerate(order[1:]):
         moved, far = acc.astype(bf16), given[i]
         if n == 0:
-            dw_query = sends(qkv_grad(q_rows))
             query_work = [
                 Move(part, lambda part: rows_product(part, w_qkv[:, :HD], NT, f32))
                 for part in halves(q_rows)
             ]
-            moved, far = step([moved, far], begin=query_work, end=[layer_y, gate_unit.sum])
+            (far,) = step([far], end=[q_work])
+            other_unit = Unit(
+                jnp.concatenate([out_work.result, q_work.result], axis=1), held=True
+            )
+            moved, far = step(
+                [moved, far],
+                begin=query_work + [other_unit.sum],
+                end=[layer_y, gate_unit.sum],
+            )
         if n == 1:
-            moved, far = step([moved, far], begin=dw_query[1], end=query_work)
+            moved, far = step(
+                [moved, far], begin=gate_unit.paired() + [up_unit.sum], end=query_work
+            )
+        if n == len(order) - 2:
+            moved, far = step([moved, far], end=gate_unit.over)
         acc = kept[i].astype(f32) + swap_x(far).astype(f32) + turn(moved).astype(f32)
     dkv_cast = rotate(acc, kv_cos, -kv_sine).astype(bf16)
     kv_rows = to_exchange(dkv_cast)
-    (kv_rows,) = step([kv_rows], begin=gate_unit.paired(), end=dw_query[1])
+    kv_work = Move(kv_rows, qkv_grad)
+    (kv_rows,) = step([kv_rows], begin=[kv_work], end=[other_unit.sum])
+    (kv_rows,) = step([kv_rows], begin=other_unit.paired(), end=[kv_work])
     kv_halves = halves(kv_rows)
-    kv_work = Move(kv_rows, qkv_grad)
-    out_back = sends(out_work.result.reshape(zs, depth, HD))
+    kv_back = sends(kv_work.result.reshape(zs, depth, HD))
     layer_pair = jnp.stack([layer_own, layer_y.result])
     layer_core = Move(layer_pair, swap_core)
-    kv_back = []
-
-    def begin_kv():
-        kv_back.extend(sends(kv_work.result))
-        return kv_back[1] + up_unit.paired(), [kv_work, up_unit.sum] + gate_unit.over
-
     w_kv = w_qkv[:, HD:]
     dh_one = scatter8(
-        lambda got: rows_product(kv_halves[0], w_kv, NT, f32, query_work[0].result, got),
+        lambda got: rows_product(kv_halves[0], w_kv, NT, bf16, query_work[0].result, got),
         lambda: rows_product(kv_halves[1], w_kv, NT, bf16, query_work[1].result),
-        Late(
-            {
-                1: lambda: ([kv_work], ()),
-                2: begin_kv,
-            }
-        ),
+        {1: (kv_back[1], other_unit.over)},
     )
     dx_add, dg_pre = norm_back(x_own, pre_gain, dh_one)
     grad_own = (d_resid + dx_add).astype(bf16)
-    (grad_own,) = step([grad_own], begin=[layer_core] + out_back[1])
+    (grad_own,) = step([grad_own], end=kv_back[1] + [up_unit.sum])
+    grad_own, dg_pre = step([grad_own, dg_pre], begin=up_unit.paired())
     grad_pair = jnp.stack([grad_own, swap_y(grad_own)])
-    (grad_pair,) = step([grad_pair], end=kv_back[1])
-    qkv_x = Move(jnp.concatenate([received(dw_query), received(kv_back)], 1), swap_x)
-    (grad_pair,) = step([grad_pair], begin=[qkv_x])
-    out_x = Move(received(out_back), swap_x)
-    out_x.result = swap_x(out_x.value)
+    kv_x = Move(received(kv_back), swap_x)
+    (grad_pair,) = step([grad_pair], begin=[kv_x, layer_core])
+    last_moves = up_unit.over + [kv_x]
     grad_all = jnp.stack([grad_pair, swap_core(grad_pair)], axis=1).reshape(1, ts, sub, width)
+    (grad_all,) = step([grad_all], end=last_moves)
     input_grad = in_order(grad_all).reshape(1, rows, width).astype(f32)
     layer_all = jnp.stack([layer_pair, layer_core.result], axis=1).reshape(1, ts, sub, width)
     layer_out = in_order(layer_all).reshape(1, rows, width)
 
     gain_grads = jnp.stack([dg_pre, dg_post, dg_mlp_pre, dg_mlp_post])
-    for mover in (swap_y, swap_core, swap_x):
-        gain_grads = gain_grads + mover(gain_grads)
     bits = 1
     while bits < zs:
         gain_grads = gain_grads + swap(gain_grads, "fsdp", bits)
         bits *= 2
+    for mover in (swap_y, swap_core, swap_x):
+        gain_grads = gain_grads + mover(gain_grads)
     gain_grads = lax.dynamic_slice_in_dim(gain_grads, z * depth, depth, 1)
 
     def two(even, left, right):
@@ -739,11 +750,12 @@
     g_down = two(first, *down_unit.parts()).T.astype(f32)
     g_gate = two(first, *gate_unit.parts()).astype(f32)
     g_up = two(first, *up_unit.parts()).astype(f32)
-    near, far = qkv_x.value, qkv_x.result
-    g_query = two(first, near[:, :HD], far[:, :HD]).astype(f32)
-    g_key = jnp.where(first, near[:, HD:], far[:, HD:]).astype(f32)
-    g_value = jnp.where(first, far[:, HD:], near[:, HD:]).astype(f32)
-    g_out = two(first, out_x.value, out_x.result).T.astype(f32)
+    near, far = other_unit.parts()
+    g_out = two(first, near[:, :HD], far[:, :HD]).T.astype(f32)
+    g_query = two(first, near[:, HD:], far[:, HD:]).astype(f32)
+    near, far = kv_x.value, kv_x.result
+    g_key = jnp.where(first, near, far).astype(f32)
+    g_value = jnp.where(first, far, near).astype(f32)
     return (
         layer_out,
         input_grad,

time: 1090 us -> 1020 us (0.936)
  starting transfers between devices: 142 us -> 103 us
  waiting for transfers between devices: 523 us -> 496 us
  other arithmetic: 94.7 us -> 75.3 us
    ppermute x9, starting transfers between devices: 63.1 us -> 28.5 us  [turn(): lax.ppermute(value, 'fsdp', [(i, (i + 1) % size) for i in range(size)])]
    ppermute x9, waiting for transfers between devices: 184 us -> 156 us  [turn(): lax.ppermute(value, 'fsdp', [(i, (i + 1) % size) for i in range(size)])]
    unnamed x158 -> x144, local copies, waits for them, and re-layouts: 29.1 us -> 40.9 us
    pallas_call x21 -> x24, Pallas kernels: 181 us -> 187 us  [tiled(): pl.pallas_call(body, grid=(rows // tile,), in_specs=in_specs, out_specs=[...]
    ppermute x71 -> x65, starting transfers between devices: 78.6 us -> 74 us  [swap(): lax.ppermute(value, axis, [(i, i ^ bit) for i in range(lax.axis_size(axis...]
    ppermute x71 -> x65, waiting for transfers between devices: 293 us -> 290 us  [swap(): lax.ppermute(value, axis, [(i, i ^ bit) for i in range(lax.axis_size(axis...]
  transfers between devices with their start and end apart: 86 -> 81, of which waited for: 58 -> 56; matrix products, arithmetic and copies ran while one was open for 13% -> 11% of each run, Pallas kernels for 17% -> 19%
where the time goes in v3:
time: 1020 us; the launch traced here: 1010 us
  waiting for transfers between devices  496 us (49%)
  Pallas kernels  220 us (22%)
  starting transfers between devices  103 us (10%)
  local copies, waits for them, and re-layouts  96.4 us (9%)
  other arithmetic  75.3 us (7%)
  between operations  15.8 us (2%)
    ppermute x65, waiting for transfers between devices, swap(): lax.ppermute(value, axis, [(i, i ^ bit) for i in range(lax.axis_size(axis...  290 us
    pallas_call x24, Pallas kernels, tiled(): pl.pallas_call(body, grid=(rows // tile,), in_specs=in_specs, out_specs=[...  187 us
    ppermute x9, waiting for transfers between devices, turn(): lax.ppermute(value, 'fsdp', [(i, (i + 1) % size) for i in range(size)])  156 us
    ppermute x65, starting transfers between devices, swap(): lax.ppermute(value, axis, [(i, i ^ bit) for i in range(lax.axis_size(axis...  74 us
    all_gather x3, waiting for transfers between devices, gathered(): return lax.all_gather(part, 'fsdp', axis=0, tiled=True)  50.9 us
    unnamed x144, local copies, waits for them, and re-layouts  40.9 us
    ppermute x9, starting transfers between devices, turn(): lax.ppermute(value, 'fsdp', [(i, (i + 1) % size) for i in range(size)])  28.5 us
    pallas_call x1, Pallas kernels, attend_back(): pl.pallas_call(functools.partial(backward_kernel, zs, rows, block), grid_...  21.4 us
  transfers between devices with their start and end apart: 81, of which 56 were waited for; matrix products, arithmetic and copies ran while one was open for 11% of the time, Pallas kernels for 19%

profile of v3, /device:TPU:0, one launch (start us, length us, event | category | flops | bytes accessed | tf_op | source)
XLA Modules:
  0.0 1007.2 jit_solution(10183490367151260789)
XLA Ops:
  22.1 14.6 %collective-permute-done = bf16[592,512]{1,0:T(8,128)(2,1)} collective-permute-done((bf16[592,512]{1,0:T(8,128)(2,1)S(1)}, bf16[592,512]{1,0:T(8,128)(2,1)}, u32[]{:S(2)}, u32[]{:S(2)}) %collective-permute-start) | collective-permute-done | bytes 606240 | tf_op jit(solution)/shard_map/ppermute | solution.py:38
  46.7 23.6 %collective-permute-done.1 = bf16[592,512]{1,0:T(8,128)(2,1)} collective-permute-done((bf16[592,512]{1,0:T(8,128)(2,1)}, bf16[592,512]{1,0:T(8,128)(2,1)}, u32[]{:S(2)}, u32[]{:S(2)}) %collective-permute-start.1) | collective-permute-done | bytes 606240 | tf_op jit(solution)/shard_map/ppermute | solution.py:38
  70.5 7.3 collective-permute-start.3
  81.6 25.6 %collective-permute-done.3 = bf16[592,512]{1,0:T(8,128)(2,1)} collective-permute-done((bf16[592,512]{1,0:T(8,128)(2,1)}, bf16[592,512]{1,0:T(8,128)(2,1)}, u32[]{:S(2)}, u32[]{:S(2)}) %collective-permute-start.3) | collective-permute-done | bytes 606240 | tf_op jit(solution)/shard_map/ppermute | solution.py:38
  110.1 5.2 shard_map.237
  117.2 5.2 shard_map.238
  123.5 3.8 fusion.67
  128.2 12.2 %collective-permute-start.5 = (bf16[2,640,256]{2,1,0:T(8,128)(2,1)}, bf16[2,640,256]{2,1,0:T(8,128)(2,1)}, u32[]{:S(2)}, u32[]{:S(2)}) collective-permute-start(bf16[2,640,256]{2,1,0:T(8,128)(2,1)} %pad_maximum_fusion.20), channel_id=1, source_target_pairs={{0,4},{4,8},{8,12},{12,0},{1,5},{5,9},{9,13},{13,1},{2,6},{6,10},{... | collective-permute-start | bytes 1966088 | tf_op jit(solution)/shard_map/ppermute | solution.py:38
  140.4 29.1 %collective-permute-done.5 = bf16[2,640,256]{2,1,0:T(8,128)(2,1)} collective-permute-done((bf16[2,640,256]{2,1,0:T(8,128)(2,1)}, bf16[2,640,256]{2,1,0:T(8,128)(2,1)}, u32[]{:S(2)}, u32[]{:S(2)}) %collective-permute-start.5) | collective-permute-done | bytes 655392 | tf_op jit(solution)/shard_map/ppermute | solution.py:38
  173.6 11.8 %collective-permute-done.6 = bf16[2,640,256]{2,1,0:T(8,128)(2,1)} collective-permute-done((bf16[2,640,256]{2,1,0:T(8,128)(2,1)}, bf16[2,640,256]{2,1,0:T(8,128)(2,1)}, u32[]{:S(2)}, u32[]{:S(2)}) %collective-permute-start.6) | collective-permute-done | bytes 655392 | tf_op jit(solution)/shard_map/ppermute | solution.py:38
  193.7 9.9 collective-permute-done.7
  211.7 7.9 collective-permute-done.10
  220.5 10.0 collective-permute-done.11
  235.3 11.2 %shard_map.239 = (bf16[2,640,256]{2,1,0:T(8,128)(2,1)S(1)}, f32[2,640,1]{2,1,0:T(8,128)S(1)}) custom-call(s32[4]{0:T(128)S(1)} %pad_add_fusion.info, bf16[2,640,256]{2,1,0:T(8,128)(2,1)S(1)} %fusion.23.q_ref, bf16[2,4,2,640,256]{4,3,2,1,0:T(8,128)(2,1)} %bitcast.27.kv_ref, s32[640,1]{1,0:T(8,128)S(1)} %copy.75.col_ref, s32[1,640]{1,0:T(1,128)S(1)} %get-tuple-element.407.row_ref), custom_call_target="tpu_custom_call" | custom-call | flops 500000000 | bytes 1000000 | tf_op jit(solution)/shard_map/pallas_call | solution.py:249
  251.0 5.6 collective-permute-done.15.refs_2_
  267.2 16.0 %collective-permute-done.16 = bf16[2,160,1152]{2,1,0:T(8,128)(2,1)S(1)} collective-permute-done((bf16[2,160,1152]{2,1,0:T(8,128)(2,1)S(1)}, bf16[2,160,1152]{2,1,0:T(8,128)(2,1)S(1)}, u32[]{:S(2)}, u32[]{:S(2)}) %collective-permute-start.16) | collective-permute-done | bytes 737312 | tf_op jit(solution)/shard_map/ppermute | solution.py:21
  290.2 7.3 collective-permute-done.18
  302.8 14.5 %all-gather.6.cloned.1.call-done.up_w.refs_3_ = bf16[2304,1152]{1,0:T(8,128)(2,1)} async-done(((bf16[576,1152]{1,0:T(8,128)(2,1)}), bf16[2304,1152]{1,0:T(8,128)(2,1)}) %all-gather.6.cloned.1.call-update) | async-done | bytes 5308432 | tf_op jit(solution)/shard_map/all_gather | solution.py:471
  320.2 7.8 collective-permute-done.20
  332.2 14.6 %collective-permute-done.22 = bf16[2,160,1152]{2,1,0:T(8,128)(2,1)S(1)} collective-permute-done((bf16[2,160,1152]{2,1,0:T(8,128)(2,1)S(1)}, bf16[2,160,1152]{2,1,0:T(8,128)(2,1)S(1)}, u32[]{:S(2)}, u32[]{:S(2)}) %collective-permute-start.22) | collective-permute-done | bytes 737312 | tf_op jit(solution)/shard_map/ppermute | solution.py:21
  350.2 13.7 %shard_map.242 = (f32[640,1152]{1,0:T(8,128)}, f32[640,1152]{1,0:T(8,128)}, bf16[640,1152]{1,0:T(8,128)(2,1)S(1)}) custom-call(bf16[640,2304]{1,0:T(8,128)(2,1)} %bitcast.346, bf16[2304,1152]{1,0:T(8,128)(2,1)} %all-gather.4.cloned.1.call-done.gate_w.refs_2_, bf16[2304,1152]{1,0:T(8,128)(2,1)} %all-gather.6.cloned.1.call-done.up_w.refs_3_), custom_call_target="tpu_custom_call" | custom-call | flops 500000000 | bytes 1000000 | tf_op jit(solution)/shard_map/pallas_call | solution.py:319
  365.5 13.7 %shard_map.243 = (f32[640,1152]{1,0:T(8,128)}, f32[640,1152]{1,0:T(8,128)}, bf16[640,1152]{1,0:T(8,128)(2,1)S(1)}) custom-call(bf16[640,2304]{1,0:T(8,128)(2,1)} %copy-done.17, bf16[2304,1152]{1,0:T(8,128)(2,1)} %all-gather.4.cloned.1.call-done.gate_w.refs_2_, bf16[2304,1152]{1,0:T(8,128)(2,1)} %all-gather.6.cloned.1.call-done.up_w.refs_3_), custom_call_target="tpu_custom_call" | custom-call | flops 500000000 | bytes 1000000 | tf_op jit(solution)/shard_map/pallas_call | solution.py:319
  380.4 36.4 %all-gather.8.cloned.1.call-done.refs_1_.w_ref = bf16[2304,1152]{1,0:T(8,128)(2,1)} async-done(((bf16[576,1152]{1,0:T(8,128)(2,1)}), bf16[2304,1152]{1,0:T(8,128)(2,1)}) %all-gather.8.cloned.1.call-update) | async-done | bytes 5308432 | tf_op jit(solution)/shard_map/all_gather | solution.py:471
  418.2 7.8 shard_map.244
  426.1 5.6 collective-permute-done.25.refs_2_
  433.3 8.3 shard_map.245
  447.1 15.6 %collective-permute-done.26 = bf16[2,160,1152]{2,1,0:T(8,128)(2,1)S(1)} collective-permute-done((bf16[2,160,1152]{2,1,0:T(8,128)(2,1)S(1)}, bf16[2,160,1152]{2,1,0:T(8,128)(2,1)S(1)}, u32[]{:S(2)}, u32[]{:S(2)}) %collective-permute-start.26) | collective-permute-done | bytes 737312 | tf_op jit(solution)/shard_map/ppermute | solution.py:21
  468.4 7.6 collective-permute-done.28
  486.2 6.4 collective-permute-done.30
  496.3 12.4 %collective-permute-done.32 = bf16[2,160,1152]{2,1,0:T(8,128)(2,1)S(1)} collective-permute-done((bf16[2,160,1152]{2,1,0:T(8,128)(2,1)S(1)}, bf16[2,160,1152]{2,1,0:T(8,128)(2,1)S(1)}, u32[]{:S(2)}, u32[]{:S(2)}) %collective-permute-start.32) | collective-permute-done | bytes 737312 | tf_op jit(solution)/shard_map/ppermute | solution.py:21
  510.2 5.4 collective-permute-done.34.refs_1_.dm_ref
  517.2 13.0 %shard_map.246 = bf16[2304,1152]{1,0:T(8,128)(2,1)} custom-call(bf16[640,2304]{1,0:T(8,128)(2,1)} %bitcast.350, bf16[640,2304]{1,0:T(8,128)(2,1)} %copy-done.30, bf16[640,1152]{1,0:T(8,128)(2,1)S(1)} %get-tuple-element.204.refs_0_.refs_2_, bf16[640,1152]{1,0:T(8,128)(2,1)} %copy-done.2), custom_call_target="tpu_custom_call" | custom-call | flops 500000000 | bytes 1000000 | tf_op jit(solution)/shard_map/pallas_call | solution.py:319
  530.2 10.3 %shard_map.248 = (bf16[640,1152]{1,0:T(8,128)(2,1)S(1)}, bf16[640,1152]{1,0:T(8,128)(2,1)}) custom-call(bf16[640,2304]{1,0:T(8,128)(2,1)} %copy-done.30, bf16[2304,1152]{1,0:T(8,128)(2,1)} %all-gather.8.cloned.1.call-done.refs_1_.w_ref, f32[640,1152]{1,0:T(8,128)} %get-tuple-element.212.gate_ref, f32[640,1152]{1,0:T(8,128)} %get-tuple-element.213.up_ref), custom_call_target="tpu_custom_call" | custom-call | flops 500000000 | bytes 1000000 | tf_op jit(solution)/shard_map/pallas_call | solution.py:319
  540.6 14.0 %shard_map.249 = bf16[640,2304]{1,0:T(8,128)(2,1)} custom-call(bf16[640,1152]{1,0:T(8,128)(2,1)S(1)} %get-tuple-element.221.refs_0_.refs_3_, bf16[640,1152]{1,0:T(8,128)(2,1)} %get-tuple-element.227.refs_1_.refs_3_, bf16[2304,1152]{1,0:T(8,128)(2,1)} %all-gather.4.cloned.1.call-done.gate_w.refs_2_, bf16[2304,1152]{1,0:T(8,128)(2,1)} %all-gather.6.cloned.1.call-done.up_w.refs_3_), custom_call_target="tpu_custom_call" | custom-call | flops 500000000 | bytes 1000000 | tf_op jit(solution)/shard_map/pallas_call | solution.py:319
  554.7 10.2 %shard_map.247 = (bf16[640,1152]{1,0:T(8,128)(2,1)S(1)}, bf16[640,1152]{1,0:T(8,128)(2,1)}) custom-call(bf16[640,2304]{1,0:T(8,128)(2,1)} %bitcast.351, bf16[2304,1152]{1,0:T(8,128)(2,1)} %all-gather.8.cloned.1.call-done.refs_1_.w_ref, f32[640,1152]{1,0:T(8,128)} %get-tuple-element.207.gate_ref, f32[640,1152]{1,0:T(8,128)} %get-tuple-element.208.up_ref), custom_call_target="tpu_custom_call" | custom-call | flops 500000000 | bytes 1000000 | tf_op jit(solution)/shard_map/pallas_call | solution.py:319
  566.4 13.9 %shard_map.250 = bf16[640,2304]{1,0:T(8,128)(2,1)} custom-call(bf16[640,1152]{1,0:T(8,128)(2,1)S(1)} %get-tuple-element.220.refs_0_.refs_2_, bf16[640,1152]{1,0:T(8,128)(2,1)} %get-tuple-element.226.refs_1_.refs_2_, bf16[2304,1152]{1,0:T(8,128)(2,1)} %all-gather.4.cloned.1.call-done.gate_w.refs_2_, ...), custom_call_target="tpu_custom_call" | custom-call | flops 500000000 | bytes 1000000 | tf_op jit(solution)/shard_map/pallas_call | solution.py:319
  585.6 12.8 %shard_map.251 = bf16[2304,1152]{1,0:T(8,128)(2,1)} custom-call(bf16[640,2304]{1,0:T(8,128)(2,1)} %bitcast.347, bf16[640,2304]{1,0:T(8,128)(2,1)} %copy-done.17, bf16[640,1152]{1,0:T(8,128)(2,1)S(1)} %get-tuple-element.220.refs_0_.refs_2_, bf16[640,1152]{1,0:T(8,128)(2,1)} %copy-done.6), custom_call_target="tpu_custom_call" | custom-call | flops 500000000 | bytes 1000000 | tf_op jit(solution)/shard_map/pallas_call | solution.py:319
  598.4 4.4 collective-permute-done.36
  609.6 13.2 %shard_map.252 = bf16[2304,1152]{1,0:T(8,128)(2,1)} custom-call(bf16[640,2304]{1,0:T(8,128)(2,1)} %bitcast.348, bf16[640,2304]{1,0:T(8,128)(2,1)} %copy-done.17, bf16[640,1152]{1,0:T(8,128)(2,1)S(1)} %copy-done.4, bf16[640,1152]{1,0:T(8,128)(2,1)} %get-tuple-element.227.refs_1_.refs_3_), custom_call_target="tpu_custom_call" | custom-call | flops 500000000 | bytes 1000000 | tf_op jit(solution)/shard_map/pallas_call | solution.py:319
  632.7 7.6 collective-permute-done.40
  643.3 14.6 %collective-permute-done.42 = bf16[2,160,1152]{2,1,0:T(8,128)(2,1)S(1)} collective-permute-done((bf16[2,160,1152]{2,1,0:T(8,128)(2,1)S(1)}, bf16[2,160,1152]{2,1,0:T(8,128)(2,1)S(1)}, u32[]{:S(2)}, u32[]{:S(2)}) %collective-permute-start.42) | collective-permute-done | bytes 737312 | tf_op jit(solution)/shard_map/ppermute | solution.py:21
  668.9 5.8 shard_map.255
  680.3 21.4 %shard_map.256 = (f32[2,640,256]{2,1,0:T(8,128)}, bf16[2,4,2,640,256]{4,3,2,1,0:T(8,128)(2,1)}) custom-call(s32[4]{0:T(128)} %copy-done.12, bf16[2,640,256]{2,1,0:T(8,128)(2,1)} %copy-done.5, bf16[2,640,256]{2,1,0:T(8,128)(2,1)} %bitcast.380, f32[4,1,320]{2,1,0:T(1,128)} %reshape.610.lse_ref, f32[4,1,320]{2,1,0:T(1,128)} %reshape.576.delta_ref, ...), custom_call_target="tpu_custom_call" | custom-call | flops 500000000 | bytes 1000000 | tf_op jit(solution)/shard_map/pallas_call | solution.py:280
  711.1 5.8 shard_map.257
  718.5 8.0 collective-permute-done.46
  744.6 24.2 %collective-permute-done.49 = bf16[2,640,256]{2,1,0:T(8,128)(2,1)S(1)} collective-permute-done((bf16[2,640,256]{2,1,0:T(8,128)(2,1)}, bf16[2,640,256]{2,1,0:T(8,128)(2,1)S(1)}, u32[]{:S(2)}, u32[]{:S(2)}) %collective-permute-start.49) | collective-permute-done | bytes 655392 | tf_op jit(solution)/shard_map/ppermute | solution.py:38
  775.4 34.7 %collective-permute-done.50 = bf16[2,640,256]{2,1,0:T(8,128)(2,1)S(1)} collective-permute-done((bf16[2,640,256]{2,1,0:T(8,128)(2,1)S(1)}, bf16[2,640,256]{2,1,0:T(8,128)(2,1)S(1)}, u32[]{:S(2)}, u32[]{:S(2)}) %collective-permute-start.50) | collective-permute-done | bytes 655392 | tf_op jit(solution)/shard_map/ppermute | solution.py:21
  813.9 9.5 collective-permute-done.53
  823.4 16.6 %collective-permute-done.54 = bf16[2,640,256]{2,1,0:T(8,128)(2,1)} collective-permute-done((bf16[2,640,256]{2,1,0:T(8,128)(2,1)S(1)}, bf16[2,640,256]{2,1,0:T(8,128)(2,1)}, u32[]{:S(2)}, u32[]{:S(2)}) %collective-permute-start.54) | collective-permute-done | bytes 655392 | tf_op jit(solution)/shard_map/ppermute | solution.py:38
  844.8 6.9 shard_map.260
  851.9 4.6 shard_map.261
  862.3 5.3 shard_map.262
  870.0 4.8 collective-permute-done.56
  876.5 5.2 convert_bitcast_fusion
  884.3 8.8 collective-permute-done.57
  901.3 10.1 collective-permute-start.62
  911.8 8.2 collective-permute-done.60
  922.0 8.2 collective-permute-done.61
  930.2 4.7 collective-permute-done.62
  935.0 7.5 collective-permute-done.63
  942.6 6.4 collective-permute-start.69
  952.2 14.8 %collective-permute-done.64 = bf16[160,2304]{1,0:T(8,128)(2,1)S(1)} collective-permute-done((bf16[160,2304]{1,0:T(8,128)(2,1)S(1)}, bf16[160,2304]{1,0:T(8,128)(2,1)S(1)}, u32[]{:S(2)}, u32[]{:S(2)}) %collective-permute-start.64) | collective-permute-done | bytes 737312 | tf_op jit(solution)/shard_map/ppermute | solution.py:21
  976.2 5.0 collective-permute-done.73
  983.5 5.7 collective-permute-done.68
  (463 shorter events, 268.7 us)
Async XLA Ops:
  7.2 224.2 %all-gather.4.cloned.1.call-start = ((), (), s32[]{:S(2)}) async-start(), calls=%async_computation.4 | async-start | bytes 6635520 | tf_op jit(solution)/shard_map/all_gather | solution.py:471
  17.8 18.9 %collective-permute-start = (bf16[592,512]{1,0:T(8,128)(2,1)S(1)}, bf16[592,512]{1,0:T(8,128)(2,1)}, u32[]{:S(2)}, u32[]{:S(2)}) collective-permute-start(bf16[592,512]{1,0:T(8,128)(2,1)S(1)} %pad_maximum_fusion.26), channel_id=1, source_target_pairs={{0,4},{4,8},{8,12},{12,0},{1,5},{5,9},{9,13},{13,1},{2,6},{6,10},{... | collective-permute-start | bytes 1818632 | tf_op jit(solution)/shard_map/ppermute | solution.py:38
  36.7 280.5 %all-gather.6.cloned.1.call-start = ((), (), s32[]{:S(2)}) async-start(), calls=%async_computation.5 | async-start | bytes 6635520 | tf_op jit(solution)/shard_map/all_gather | solution.py:471
  36.8 33.8 %collective-permute-start.2 = (bf16[2,160,2304]{2,1,0:T(8,128)(2,1)}, bf16[2,160,2304]{2,1,0:T(8,128)(2,1)S(1)}, u32[]{:S(2)}, u32[]{:S(2)}) collective-permute-start(bf16[2,160,2304]{2,1,0:T(8,128)(2,1)} %slice_bitcast_fusion), channel_id=1, source_target_pairs={{0,16},{16,0},{1,17},{17,1},{2,18},{18,2},{3,19},{19,3},{4,20},{20... | collective-permute-start | bytes 4423688 | tf_op jit(solution)/shard_map/ppermute | solution.py:21
  42.3 28.0 %collective-permute-start.1 = (bf16[592,512]{1,0:T(8,128)(2,1)}, bf16[592,512]{1,0:T(8,128)(2,1)}, u32[]{:S(2)}, u32[]{:S(2)}) collective-permute-start(bf16[592,512]{1,0:T(8,128)(2,1)} %collective-permute-done), channel_id=1, source_target_pairs={{0,4},{4,8},{8,12},{12,0},{1,5},{5,9},{9,13},{13,1},{2,6},{6,10},{... | collective-permute-start | bytes 1818632 | tf_op jit(solution)/shard_map/ppermute | solution.py:38
  70.5 36.6 %collective-permute-start.3 = (bf16[592,512]{1,0:T(8,128)(2,1)}, bf16[592,512]{1,0:T(8,128)(2,1)}, u32[]{:S(2)}, u32[]{:S(2)}) collective-permute-start(bf16[592,512]{1,0:T(8,128)(2,1)} %collective-permute-done.1), channel_id=1, source_target_pairs={{0,4},{4,8},{8,12},{12,0},{1,5},{5,9},{9,13},{13,1},{2,6},{6,10},{... | collective-permute-start | bytes 1818632 | tf_op jit(solution)/shard_map/ppermute | solution.py:38
  77.8 37.5 %collective-permute-start.4 = (bf16[2,160,2304]{2,1,0:T(8,128)(2,1)S(1)}, bf16[2,160,2304]{2,1,0:T(8,128)(2,1)S(1)}, u32[]{:S(2)}, u32[]{:S(2)}) collective-permute-start(bf16[2,160,2304]{2,1,0:T(8,128)(2,1)S(1)} %collective-permute-done.2), channel_id=1, source_target_pairs={{0,1},{1,0},{2,3},{3,2},{4,5},{5,4},{6,7},{7,6},{8,9},{9,8},{10,11... | collective-permute-start | bytes 4423688 | tf_op jit(solution)/shard_map/ppermute | solution.py:21
  128.2 41.3 %collective-permute-start.5 = (bf16[2,640,256]{2,1,0:T(8,128)(2,1)}, bf16[2,640,256]{2,1,0:T(8,128)(2,1)}, u32[]{:S(2)}, u32[]{:S(2)}) collective-permute-start(bf16[2,640,256]{2,1,0:T(8,128)(2,1)} %pad_maximum_fusion.20), channel_id=1, source_target_pairs={{0,4},{4,8},{8,12},{12,0},{1,5},{5,9},{9,13},{13,1},{2,6},{6,10},{... | collective-permute-start | bytes 1966088 | tf_op jit(solution)/shard_map/ppermute | solution.py:38
  169.5 15.9 %collective-permute-start.6 = (bf16[2,640,256]{2,1,0:T(8,128)(2,1)}, bf16[2,640,256]{2,1,0:T(8,128)(2,1)}, u32[]{:S(2)}, u32[]{:S(2)}) collective-permute-start(bf16[2,640,256]{2,1,0:T(8,128)(2,1)} %collective-permute-done.5), channel_id=1, source_target_pairs={{0,4},{4,8},{8,12},{12,0},{1,5},{5,9},{9,13},{13,1},{2,6},{6,10},{... | collective-permute-start | bytes 1966088 | tf_op jit(solution)/shard_map/ppermute | solution.py:38
  173.6 32.6 %collective-permute-start.8 = (bf16[2,640,256]{2,1,0:T(8,128)(2,1)}, bf16[2,640,256]{2,1,0:T(8,128)(2,1)}, u32[]{:S(2)}, u32[]{:S(2)}) collective-permute-start(bf16[2,640,256]{2,1,0:T(8,128)(2,1)} %pad_maximum_fusion.20), channel_id=1, source_target_pairs={{0,16},{16,0},{1,17},{17,1},{2,18},{18,2},{3,19},{19,3},{4,20},{20... | collective-permute-start | bytes 1966088 | tf_op jit(solution)/shard_map/ppermute | solution.py:21
  185.4 18.2 %collective-permute-start.7 = (bf16[2,640,256]{2,1,0:T(8,128)(2,1)}, bf16[2,640,256]{2,1,0:T(8,128)(2,1)}, u32[]{:S(2)}, u32[]{:S(2)}) collective-permute-start(bf16[2,640,256]{2,1,0:T(8,128)(2,1)} %collective-permute-done.6), channel_id=1, source_target_pairs={{0,4},{4,8},{8,12},{12,0},{1,5},{5,9},{9,13},{13,1},{2,6},{6,10},{... | collective-permute-start | bytes 1966088 | tf_op jit(solution)/shard_map/ppermute | solution.py:38
  187.7 22.1 %collective-permute-start.9 = (bf16[2,640,256]{2,1,0:T(8,128)(2,1)}, bf16[2,640,256]{2,1,0:T(8,128)(2,1)}, u32[]{:S(2)}, u32[]{:S(2)}) collective-permute-start(bf16[2,640,256]{2,1,0:T(8,128)(2,1)} %collective-permute-done.5), channel_id=1, source_target_pairs={{0,16},{16,0},{1,17},{17,1},{2,18},{18,2},{3,19},{19,3},{4,20},{20... | collective-permute-start | bytes 1966088 | tf_op jit(solution)/shard_map/ppermute | solution.py:21
  190.5 29.1 %collective-permute-start.10 = (bf16[2,640,256]{2,1,0:T(8,128)(2,1)}, bf16[2,640,256]{2,1,0:T(8,128)(2,1)S(1)}, u32[]{:S(2)}, u32[]{:S(2)}) collective-permute-start(bf16[2,640,256]{2,1,0:T(8,128)(2,1)} %collective-permute-done.6), channel_id=1, source_target_pairs={{0,16},{16,0},{1,17},{17,1},{2,18},{18,2},{3,19},{19,3},{4,20},{20... | collective-permute-start | bytes 1966088 | tf_op jit(solution)/shard_map/ppermute | solution.py:21
  203.6 27.7 %collective-permute-start.12 = (bf16[576,256]{1,0:T(8,128)(2,1)}, bf16[576,256]{1,0:T(8,128)(2,1)S(1)}, u32[]{:S(2)}, u32[]{:S(2)}) collective-permute-start(bf16[576,256]{1,0:T(8,128)(2,1)} %get-tuple-element.172), channel_id=1, source_target_pairs={{0,4},{4,0},{8,12},{12,8},{1,5},{5,1},{9,13},{13,9},{2,6},{6,2},{1... | collective-permute-start | bytes 884744 | tf_op jit(solution)/shard_map/ppermute | solution.py:21
  203.6 27.7 %collective-permute-start.13 = (bf16[576,256]{1,0:T(8,128)(2,1)}, bf16[576,256]{1,0:T(8,128)(2,1)S(1)}, u32[]{:S(2)}, u32[]{:S(2)}) collective-permute-start(bf16[576,256]{1,0:T(8,128)(2,1)} %get-tuple-element.172), channel_id=1, source_target_pairs={{0,8},{4,12},{8,0},{12,4},{1,9},{5,13},{9,1},{13,5},{2,10},{6,14},... | collective-permute-start | bytes 884744 | tf_op jit(solution)/shard_map/ppermute | solution.py:21
  203.7 213.1 %all-gather.8.cloned.1.call-start = ((), (), s32[]{:S(2)}) async-start(), calls=%async_computation.6 | async-start | bytes 6635520 | tf_op jit(solution)/shard_map/all_gather | solution.py:471
  206.2 24.2 %collective-permute-start.11 = (bf16[2,640,256]{2,1,0:T(8,128)(2,1)}, bf16[2,640,256]{2,1,0:T(8,128)(2,1)S(1)}, u32[]{:S(2)}, u32[]{:S(2)}) collective-permute-start(bf16[2,640,256]{2,1,0:T(8,128)(2,1)} %collective-permute-done.7), channel_id=1, source_target_pairs={{0,16},{16,0},{1,17},{17,1},{2,18},{18,2},{3,19},{19,3},{4,20},{20... | collective-permute-start | bytes 1966088 | tf_op jit(solution)/shard_map/ppermute | solution.py:21
  231.4 17.0 %collective-permute-start.14 = (bf16[576,256]{1,0:T(8,128)(2,1)}, bf16[576,256]{1,0:T(8,128)(2,1)S(1)}, u32[]{:S(2)}, u32[]{:S(2)}) collective-permute-start(bf16[576,256]{1,0:T(8,128)(2,1)} %get-tuple-element.172), channel_id=1, source_target_pairs={{0,12},{4,8},{8,4},{12,0},{1,13},{5,9},{9,5},{13,1},{2,14},{6,10},... | collective-permute-start | bytes 884744 | tf_op jit(solution)/shard_map/ppermute | solution.py:21
  264.3 18.9 %collective-permute-start.16 = (bf16[2,160,1152]{2,1,0:T(8,128)(2,1)S(1)}, bf16[2,160,1152]{2,1,0:T(8,128)(2,1)S(1)}, u32[]{:S(2)}, u32[]{:S(2)}) collective-permute-start(bf16[2,160,1152]{2,1,0:T(8,128)(2,1)S(1)} %slice_bitcast_fusion.23), channel_id=1, source_target_pairs={{0,16},{16,0},{1,17},{17,1},{2,18},{18,2},{3,19},{19,3},{4,20},{20... | collective-permute-start | bytes 2211848 | tf_op jit(solution)/shard_map/ppermute | solution.py:21
  266.4 18.3 %collective-permute-start.17 = (bf16[2,160,1152]{2,1,0:T(8,128)(2,1)S(1)}, bf16[2,160,1152]{2,1,0:T(8,128)(2,1)S(1)}, u32[]{:S(2)}, u32[]{:S(2)}) collective-permute-start(bf16[2,160,1152]{2,1,0:T(8,128)(2,1)S(1)} %slice_bitcast_fusion.22), channel_id=1, source_target_pairs={{0,2},{1,3},{2,0},{3,1},{4,6},{5,7},{6,4},{7,5},{8,10},{9,11},{10,... | collective-permute-start | bytes 2211848 | tf_op jit(solution)/shard_map/ppermute | solution.py:21
  287.6 9.9 collective-permute-start.18
  289.6 340.7 %reduce-scatter.5.cloned.1.call-start = ((), (), s32[]{:S(2)}) async-start(), calls=%async_computation.7 | async-start | bytes 6635520 | tf_op jit(solution)/shard_map/reduce_scatter | solution.py:586
  317.2 10.7 %collective-permute-start.20 = (bf16[160,1152]{1,0:T(8,128)(2,1)}, bf16[160,1152]{1,0:T(8,128)(2,1)S(1)}, u32[]{:S(2)}, u32[]{:S(2)}) collective-permute-start(bf16[160,1152]{1,0:T(8,128)(2,1)} %get-tuple-element.182), channel_id=1, source_target_pairs={{0,16},{16,0},{1,17},{17,1},{2,18},{18,2},{3,19},{19,3},{4,20},{20... | collective-permute-start | bytes 1105928 | tf_op jit(solution)/shard_map/ppermute | solution.py:21
  318.7 10.4 %collective-permute-start.21 = (bf16[160,1152]{1,0:T(8,128)(2,1)}, bf16[160,1152]{1,0:T(8,128)(2,1)S(1)}, u32[]{:S(2)}, u32[]{:S(2)}) collective-permute-start(bf16[160,1152]{1,0:T(8,128)(2,1)} %get-tuple-element.183), channel_id=1, source_target_pairs={{0,2},{1,3},{2,0},{3,1},{4,6},{5,7},{6,4},{7,5},{8,10},{9,11},{10,... | collective-permute-start | bytes 1105928 | tf_op jit(solution)/shard_map/ppermute | solution.py:21
  329.2 17.5 %collective-permute-start.22 = (bf16[2,160,1152]{2,1,0:T(8,128)(2,1)S(1)}, bf16[2,160,1152]{2,1,0:T(8,128)(2,1)S(1)}, u32[]{:S(2)}, u32[]{:S(2)}) collective-permute-start(bf16[2,160,1152]{2,1,0:T(8,128)(2,1)S(1)} %pad_maximum_fusion.14), channel_id=1, source_target_pairs={{0,2},{1,3},{2,0},{3,1},{4,6},{5,7},{6,4},{7,5},{8,10},{9,11},{10,... | collective-permute-start | bytes 2211848 | tf_op jit(solution)/shard_map/ppermute | solution.py:21
  330.8 17.2 %collective-permute-start.23 = (bf16[2,160,1152]{2,1,0:T(8,128)(2,1)S(1)}, bf16[2,160,1152]{2,1,0:T(8,128)(2,1)S(1)}, u32[]{:S(2)}, u32[]{:S(2)}) collective-permute-start(bf16[2,160,1152]{2,1,0:T(8,128)(2,1)S(1)} %pad_maximum_fusion.15), channel_id=1, source_target_pairs={{0,16},{16,0},{1,17},{17,1},{2,18},{18,2},{3,19},{19,3},{4,20},{20... | collective-permute-start | bytes 2211848 | tf_op jit(solution)/shard_map/ppermute | solution.py:21
  348.6 15.3 %collective-permute-start.24 = (bf16[640,2304]{1,0:T(8,128)(2,1)S(1)}, bf16[640,2304]{1,0:T(8,128)(2,1)S(1)}, u32[]{:S(2)}, u32[]{:S(2)}) collective-permute-start(bf16[640,2304]{1,0:T(8,128)(2,1)S(1)} %bitcast.345), channel_id=1, source_target_pairs={{0,1},{1,0},{2,3},{3,2},{4,5},{5,4},{6,7},{7,6},{8,9},{9,8},{10,11... | collective-permute-start | bytes 8847368 | tf_op jit(solution)/shard_map/ppermute | solution.py:21
  444.1 18.6 %collective-permute-start.26 = (bf16[2,160,1152]{2,1,0:T(8,128)(2,1)S(1)}, bf16[2,160,1152]{2,1,0:T(8,128)(2,1)S(1)}, u32[]{:S(2)}, u32[]{:S(2)}) collective-permute-start(bf16[2,160,1152]{2,1,0:T(8,128)(2,1)S(1)} %slice_bitcast_fusion.17), channel_id=1, source_target_pairs={{0,16},{16,0},{1,17},{17,1},{2,18},{18,2},{3,19},{19,3},{4,20},{20... | collective-permute-start | bytes 2211848 | tf_op jit(solution)/shard_map/ppermute | solution.py:21
  445.7 18.2 %collective-permute-start.27 = (bf16[2,160,1152]{2,1,0:T(8,128)(2,1)S(1)}, bf16[2,160,1152]{2,1,0:T(8,128)(2,1)S(1)}, u32[]{:S(2)}, u32[]{:S(2)}) collective-permute-start(bf16[2,160,1152]{2,1,0:T(8,128)(2,1)S(1)} %slice_bitcast_fusion.16), channel_id=1, source_target_pairs={{0,2},{1,3},{2,0},{3,1},{4,6},{5,7},{6,4},{7,5},{8,10},{9,11},{10,... | collective-permute-start | bytes 2211848 | tf_op jit(solution)/shard_map/ppermute | solution.py:21
  493.3 15.4 %collective-permute-start.32 = (bf16[2,160,1152]{2,1,0:T(8,128)(2,1)S(1)}, bf16[2,160,1152]{2,1,0:T(8,128)(2,1)S(1)}, u32[]{:S(2)}, u32[]{:S(2)}) collective-permute-start(bf16[2,160,1152]{2,1,0:T(8,128)(2,1)S(1)} %pad_maximum_fusion.16), channel_id=1, source_target_pairs={{0,2},{1,3},{2,0},{3,1},{4,6},{5,7},{6,4},{7,5},{8,10},{9,11},{10,... | collective-permute-start | bytes 2211848 | tf_op jit(solution)/shard_map/ppermute | solution.py:21
  494.9 14.7 %collective-permute-start.33 = (bf16[2,160,1152]{2,1,0:T(8,128)(2,1)S(1)}, bf16[2,160,1152]{2,1,0:T(8,128)(2,1)S(1)}, u32[]{:S(2)}, u32[]{:S(2)}) collective-permute-start(bf16[2,160,1152]{2,1,0:T(8,128)(2,1)S(1)} %pad_maximum_fusion.17), channel_id=1, source_target_pairs={{0,16},{16,0},{1,17},{17,1},{2,18},{18,2},{3,19},{19,3},{4,20},{20... | collective-permute-start | bytes 2211848 | tf_op jit(solution)/shard_map/ppermute | solution.py:21
  530.2 198.6 %reduce-scatter.7.cloned.1.call-start = ((), (), s32[]{:S(2)}) async-start(), calls=%async_computation.8 | async-start | bytes 6635520 | tf_op jit(solution)/shard_map/reduce_scatter | solution.py:586
  554.6 10.2 %collective-permute-start.35 = (bf16[640,2304]{1,0:T(8,128)(2,1)}, bf16[640,2304]{1,0:T(8,128)(2,1)S(1)}, u32[]{:S(2)}, u32[]{:S(2)}) collective-permute-start(bf16[640,2304]{1,0:T(8,128)(2,1)} %shard_map.249), channel_id=1, source_target_pairs={{0,1},{1,0},{2,3},{3,2},{4,5},{5,4},{6,7},{7,6},{8,9},{9,8},{10,11... | collective-permute-start | bytes 8847368 | tf_op jit(solution)/shard_map/ppermute | solution.py:21
  583.6 19.1 %collective-permute-start.36 = (bf16[2,160,1152]{2,1,0:T(8,128)(2,1)}, bf16[2,160,1152]{2,1,0:T(8,128)(2,1)S(1)}, u32[]{:S(2)}, u32[]{:S(2)}) collective-permute-start(bf16[2,160,1152]{2,1,0:T(8,128)(2,1)} %slice_bitcast_fusion.11), channel_id=1, source_target_pairs={{0,16},{16,0},{1,17},{17,1},{2,18},{18,2},{3,19},{19,3},{4,20},{20... | collective-permute-start | bytes 2211848 | tf_op jit(solution)/shard_map/ppermute | solution.py:21
  584.9 18.7 %collective-permute-start.37 = (bf16[2,160,1152]{2,1,0:T(8,128)(2,1)S(1)}, bf16[2,160,1152]{2,1,0:T(8,128)(2,1)}, u32[]{:S(2)}, u32[]{:S(2)}) collective-permute-start(bf16[2,160,1152]{2,1,0:T(8,128)(2,1)S(1)} %slice_bitcast_fusion.10), channel_id=1, source_target_pairs={{0,2},{1,3},{2,0},{3,1},{4,6},{5,7},{6,4},{7,5},{8,10},{9,11},{10,... | collective-permute-start | bytes 2211848 | tf_op jit(solution)/shard_map/ppermute | solution.py:21
  607.7 15.2 %collective-permute-start.38 = (bf16[160,1152]{1,0:T(8,128)(2,1)}, bf16[160,1152]{1,0:T(8,128)(2,1)}, u32[]{:S(2)}, u32[]{:S(2)}) collective-permute-start(bf16[160,1152]{1,0:T(8,128)(2,1)} %fusion.80), channel_id=1, source_target_pairs={{0,2},{1,3},{2,0},{3,1},{4,6},{5,7},{6,4},{7,5},{8,10},{9,11},{10,... | collective-permute-start | bytes 1105928 | tf_op jit(solution)/shard_map/ppermute | solution.py:21
  608.3 16.0 %collective-permute-start.39 = (bf16[160,1152]{1,0:T(8,128)(2,1)}, bf16[160,1152]{1,0:T(8,128)(2,1)}, u32[]{:S(2)}, u32[]{:S(2)}) collective-permute-start(bf16[160,1152]{1,0:T(8,128)(2,1)} %fusion.81), channel_id=1, source_target_pairs={{0,16},{16,0},{1,17},{17,1},{2,18},{18,2},{3,19},{19,3},{4,20},{20... | collective-permute-start | bytes 1105928 | tf_op jit(solution)/shard_map/ppermute | solution.py:21
  609.6 235.2 %reduce-scatter.9.cloned.1.call-start = ((), (), s32[]{:S(2)}) async-start(), calls=%async_computation.9 | async-start | bytes 2949120 | tf_op jit(solution)/shard_map/reduce_scatter | solution.py:586
  630.4 9.9 collective-permute-start.40
  641.1 16.9 %collective-permute-start.42 = (bf16[2,160,1152]{2,1,0:T(8,128)(2,1)S(1)}, bf16[2,160,1152]{2,1,0:T(8,128)(2,1)S(1)}, u32[]{:S(2)}, u32[]{:S(2)}) collective-permute-start(bf16[2,160,1152]{2,1,0:T(8,128)(2,1)S(1)} %pad_maximum_fusion.18), channel_id=1, source_target_pairs={{0,2},{1,3},{2,0},{3,1},{4,6},{5,7},{6,4},{7,5},{8,10},{9,11},{10,... | collective-permute-start | bytes 2211848 | tf_op jit(solution)/shard_map/ppermute | solution.py:21
  642.4 16.3 %collective-permute-start.43 = (bf16[2,160,1152]{2,1,0:T(8,128)(2,1)S(1)}, bf16[2,160,1152]{2,1,0:T(8,128)(2,1)S(1)}, u32[]{:S(2)}, u32[]{:S(2)}) collective-permute-start(bf16[2,160,1152]{2,1,0:T(8,128)(2,1)S(1)} %pad_maximum_fusion.19), channel_id=1, source_target_pairs={{0,16},{16,0},{1,17},{17,1},{2,18},{18,2},{3,19},{19,3},{4,20},{20... | collective-permute-start | bytes 2211848 | tf_op jit(solution)/shard_map/ppermute | solution.py:21
  676.0 31.6 %collective-permute-start.45 = (bf16[576,1152]{1,0:T(8,128)(2,1)}, bf16[576,1152]{1,0:T(8,128)(2,1)}, u32[]{:S(2)}, u32[]{:S(2)}) collective-permute-start(bf16[576,1152]{1,0:T(8,128)(2,1)} %reduce-scatter.5.cloned.1.call-done), channel_id=1, source_target_pairs={{0,16},{16,0},{1,17},{17,1},{2,18},{18,2},{3,19},{19,3},{4,20},{20... | collective-permute-start | bytes 3981320 | tf_op jit(solution)/shard_map/ppermute | solution.py:21
  679.1 49.7 %collective-permute-start.47 = (bf16[160,2304]{1,0:T(8,128)(2,1)S(1)}, bf16[160,2304]{1,0:T(8,128)(2,1)}, u32[]{:S(2)}, u32[]{:S(2)}) collective-permute-start(bf16[160,2304]{1,0:T(8,128)(2,1)S(1)} %copy-done.54), channel_id=1, source_target_pairs={{0,2},{1,3},{2,0},{3,1},{4,6},{5,7},{6,4},{7,5},{8,10},{9,11},{10,... | collective-permute-start | bytes 2211848 | tf_op jit(solution)/shard_map/ppermute | solution.py:21
  710.0 16.5 %collective-permute-start.46 = (bf16[2,640,256]{2,1,0:T(8,128)(2,1)}, bf16[2,640,256]{2,1,0:T(8,128)(2,1)}, u32[]{:S(2)}, u32[]{:S(2)}) collective-permute-start(bf16[2,640,256]{2,1,0:T(8,128)(2,1)} %get-tuple-element.323), channel_id=1, source_target_pairs={{0,16},{16,0},{1,17},{17,1},{2,18},{18,2},{3,19},{19,3},{4,20},{20... | collective-permute-start | bytes 1966088 | tf_op jit(solution)/shard_map/ppermute | solution.py:21
  728.9 213.6 %reduce-scatter.11.cloned.1.call-start = ((), (), s32[]{:S(2)}) async-start(), calls=%async_computation.10 | async-start | bytes 6635520 | tf_op jit(solution)/shard_map/reduce_scatter | solution.py:586
  729.1 15.6 %collective-permute-start.48 = (bf16[2,640,256]{2,1,0:T(8,128)(2,1)}, bf16[2,640,256]{2,1,0:T(8,128)(2,1)S(1)}, u32[]{:S(2)}, u32[]{:S(2)}) collective-permute-start(bf16[2,640,256]{2,1,0:T(8,128)(2,1)} %get-tuple-element.258), channel_id=1, source_target_pairs={{0,16},{16,0},{1,17},{17,1},{2,18},{18,2},{3,19},{19,3},{4,20},{20... | collective-permute-start | bytes 1966088 | tf_op jit(solution)/shard_map/ppermute | solution.py:21
  730.2 38.7 %collective-permute-start.49 = (bf16[2,640,256]{2,1,0:T(8,128)(2,1)}, bf16[2,640,256]{2,1,0:T(8,128)(2,1)S(1)}, u32[]{:S(2)}, u32[]{:S(2)}) collective-permute-start(bf16[2,640,256]{2,1,0:T(8,128)(2,1)} %fusion.29), channel_id=1, source_target_pairs={{0,4},{4,8},{8,12},{12,0},{1,5},{5,9},{9,13},{13,1},{2,6},{6,10},{... | collective-permute-start | bytes 1966088 | tf_op jit(solution)/shard_map/ppermute | solution.py:38
  770.2 41.5 %collective-permute-start.52 = (bf16[576,1152]{1,0:T(8,128)(2,1)S(1)}, bf16[576,1152]{1,0:T(8,128)(2,1)S(1)}, u32[]{:S(2)}, u32[]{:S(2)}) collective-permute-start(bf16[576,1152]{1,0:T(8,128)(2,1)S(1)} %copy-done.49), channel_id=1, source_target_pairs={{0,16},{16,0},{1,17},{17,1},{2,18},{18,2},{3,19},{19,3},{4,20},{20... | collective-permute-start | bytes 3981320 | tf_op jit(solution)/shard_map/ppermute | solution.py:21
  770.9 39.3 %collective-permute-start.50 = (bf16[2,640,256]{2,1,0:T(8,128)(2,1)S(1)}, bf16[2,640,256]{2,1,0:T(8,128)(2,1)S(1)}, u32[]{:S(2)}, u32[]{:S(2)}) collective-permute-start(bf16[2,640,256]{2,1,0:T(8,128)(2,1)S(1)} %copy-done.57), channel_id=1, source_target_pairs={{0,16},{16,0},{1,17},{17,1},{2,18},{18,2},{3,19},{19,3},{4,20},{20... | collective-permute-start | bytes 1966088 | tf_op jit(solution)/shard_map/ppermute | solution.py:21
  772.3 38.1 %collective-permute-start.51 = (bf16[2,640,256]{2,1,0:T(8,128)(2,1)S(1)}, bf16[2,640,256]{2,1,0:T(8,128)(2,1)S(1)}, u32[]{:S(2)}, u32[]{:S(2)}) collective-permute-start(bf16[2,640,256]{2,1,0:T(8,128)(2,1)S(1)} %fusion.25), channel_id=1, source_target_pairs={{0,4},{4,8},{8,12},{12,0},{1,5},{5,9},{9,13},{13,1},{2,6},{6,10},{... | collective-permute-start | bytes 1966088 | tf_op jit(solution)/shard_map/ppermute | solution.py:38
  812.8 10.6 %collective-permute-start.53 = (bf16[2,640,256]{2,1,0:T(8,128)(2,1)S(1)}, bf16[2,640,256]{2,1,0:T(8,128)(2,1)S(1)}, u32[]{:S(2)}, u32[]{:S(2)}) collective-permute-start(bf16[2,640,256]{2,1,0:T(8,128)(2,1)S(1)} %get-tuple-element.267), channel_id=1, source_target_pairs={{0,16},{16,0},{1,17},{17,1},{2,18},{18,2},{3,19},{19,3},{4,20},{20... | collective-permute-start | bytes 1966088 | tf_op jit(solution)/shard_map/ppermute | solution.py:21
  813.9 26.2 %collective-permute-start.54 = (bf16[2,640,256]{2,1,0:T(8,128)(2,1)S(1)}, bf16[2,640,256]{2,1,0:T(8,128)(2,1)}, u32[]{:S(2)}, u32[]{:S(2)}) collective-permute-start(bf16[2,640,256]{2,1,0:T(8,128)(2,1)S(1)} %fusion.27), channel_id=1, source_target_pairs={{0,4},{4,8},{8,12},{12,0},{1,5},{5,9},{9,13},{13,1},{2,6},{6,10},{... | collective-permute-start | bytes 1966088 | tf_op jit(solution)/shard_map/ppermute | solution.py:38
  858.8 16.0 %collective-permute-start.56 = (bf16[576,512]{1,0:T(8,128)(2,1)S(1)}, bf16[576,512]{1,0:T(8,128)(2,1)S(1)}, u32[]{:S(2)}, u32[]{:S(2)}) collective-permute-start(bf16[576,512]{1,0:T(8,128)(2,1)S(1)} %copy-done.58), channel_id=1, source_target_pairs={{0,16},{16,0},{1,17},{17,1},{2,18},{18,2},{3,19},{19,3},{4,20},{20... | collective-permute-start | bytes 1769480 | tf_op jit(solution)/shard_map/ppermute | solution.py:21
  874.8 18.3 %collective-permute-start.57 = (bf16[2,160,1152]{2,1,0:T(8,128)(2,1)S(1)}, bf16[2,160,1152]{2,1,0:T(8,128)(2,1)S(1)}, u32[]{:S(2)}, u32[]{:S(2)}) collective-permute-start(bf16[2,160,1152]{2,1,0:T(8,128)(2,1)S(1)} %slice_bitcast_fusion.5), channel_id=1, source_target_pairs={{0,16},{16,0},{1,17},{17,1},{2,18},{18,2},{3,19},{19,3},{4,20},{20... | collective-permute-start | bytes 2211848 | tf_op jit(solution)/shard_map/ppermute | solution.py:21
  876.5 17.9 %collective-permute-start.58 = (bf16[2,160,1152]{2,1,0:T(8,128)(2,1)S(1)}, bf16[2,160,1152]{2,1,0:T(8,128)(2,1)S(1)}, u32[]{:S(2)}, u32[]{:S(2)}) collective-permute-start(bf16[2,160,1152]{2,1,0:T(8,128)(2,1)S(1)} %slice_bitcast_fusion.4), channel_id=1, source_target_pairs={{0,2},{1,3},{2,0},{3,1},{4,6},{5,7},{6,4},{7,5},{8,10},{9,11},{10,... | collective-permute-start | bytes 2211848 | tf_op jit(solution)/shard_map/ppermute | solution.py:21
  894.9 16.9 %collective-permute-start.59 = (bf16[160,1152]{1,0:T(8,128)(2,1)S(1)}, bf16[160,1152]{1,0:T(8,128)(2,1)S(1)}, u32[]{:S(2)}, u32[]{:S(2)}) collective-permute-start(bf16[160,1152]{1,0:T(8,128)(2,1)S(1)} %fusion.82), channel_id=1, source_target_pairs={{0,2},{1,3},{2,0},{3,1},{4,6},{5,7},{6,4},{7,5},{8,10},{9,11},{10,... | collective-permute-start | bytes 1105928 | tf_op jit(solution)/shard_map/ppermute | solution.py:21
  898.9 31.3 %collective-permute-start.61 = (bf16[576,256]{1,0:T(8,128)(2,1)S(1)}, bf16[576,256]{1,0:T(8,128)(2,1)S(1)}, u32[]{:S(2)}, u32[]{:S(2)}) collective-permute-start(bf16[576,256]{1,0:T(8,128)(2,1)S(1)} %get-tuple-element.282), channel_id=1, source_target_pairs={{0,4},{4,0},{8,12},{12,8},{1,5},{5,1},{9,13},{13,9},{2,6},{6,2},{1... | collective-permute-start | bytes 884744 | tf_op jit(solution)/shard_map/ppermute | solution.py:21
  901.3 33.7 %collective-permute-start.62 = (bf16[576,256]{1,0:T(8,128)(2,1)S(1)}, bf16[576,256]{1,0:T(8,128)(2,1)S(1)}, u32[]{:S(2)}, u32[]{:S(2)}) collective-permute-start(bf16[576,256]{1,0:T(8,128)(2,1)S(1)} %get-tuple-element.283), channel_id=1, source_target_pairs={{0,8},{4,12},{8,0},{12,4},{1,9},{5,13},{9,1},{13,5},{2,10},{6,14},... | collective-permute-start | bytes 884744 | tf_op jit(solution)/shard_map/ppermute | solution.py:21
  911.3 31.2 %collective-permute-start.63 = (bf16[576,256]{1,0:T(8,128)(2,1)S(1)}, bf16[576,256]{1,0:T(8,128)(2,1)}, u32[]{:S(2)}, u32[]{:S(2)}) collective-permute-start(bf16[576,256]{1,0:T(8,128)(2,1)S(1)} %get-tuple-element.284), channel_id=1, source_target_pairs={{0,12},{4,8},{8,4},{12,0},{1,13},{5,9},{9,5},{13,1},{2,14},{6,10},... | collective-permute-start | bytes 884744 | tf_op jit(solution)/shard_map/ppermute | solution.py:21
  949.0 18.0 %collective-permute-start.64 = (bf16[160,2304]{1,0:T(8,128)(2,1)S(1)}, bf16[160,2304]{1,0:T(8,128)(2,1)S(1)}, u32[]{:S(2)}, u32[]{:S(2)}) collective-permute-start(bf16[160,2304]{1,0:T(8,128)(2,1)S(1)} %fusion.19), channel_id=1, source_target_pairs={{0,2},{1,3},{2,0},{3,1},{4,6},{5,7},{6,4},{7,5},{8,10},{9,11},{10,... | collective-permute-start | bytes 2211848 | tf_op jit(solution)/shard_map/ppermute | solution.py:21
  949.8 39.4 %collective-permute-start.67 = (bf16[576,1152]{1,0:T(8,128)(2,1)}, bf16[576,1152]{1,0:T(8,128)(2,1)S(1)}, u32[]{:S(2)}, u32[]{:S(2)}) collective-permute-start(bf16[576,1152]{1,0:T(8,128)(2,1)} %reduce-scatter.11.cloned.1.call-done), channel_id=1, source_target_pairs={{0,16},{16,0},{1,17},{17,1},{2,18},{18,2},{3,19},{19,3},{4,20},{20... | collective-permute-start | bytes 3981320 | tf_op jit(solution)/shard_map/ppermute | solution.py:21
  951.9 15.3 %collective-permute-start.70 = (f32[4,2304]{1,0:T(4,128)S(1)}, f32[4,2304]{1,0:T(4,128)S(1)}, u32[]{:S(2)}, u32[]{:S(2)}) collective-permute-start(f32[4,2304]{1,0:T(4,128)S(1)} %fusion.100), channel_id=1, source_target_pairs={{0,8},{4,12},{8,0},{12,4},{1,9},{5,13},{9,1},{13,5},{2,10},{6,14},... | collective-permute-start | bytes 110600 | tf_op jit(solution)/shard_map/ppermute | solution.py:21
  967.1 15.9 %collective-permute-start.66 = (bf16[2,160,2304]{2,1,0:T(8,128)(2,1)S(1)}, bf16[2,160,2304]{2,1,0:T(8,128)(2,1)S(1)}, u32[]{:S(2)}, u32[]{:S(2)}) collective-permute-start(bf16[2,160,2304]{2,1,0:T(8,128)(2,1)S(1)} %pad_maximum_fusion.13), channel_id=1, source_target_pairs={{0,1},{1,0},{2,3},{3,2},{4,5},{5,4},{6,7},{7,6},{8,9},{9,8},{10,11... | collective-permute-start | bytes 4423688 | tf_op jit(solution)/shard_map/ppermute | solution.py:21
  968.4 22.0 %collective-permute-start.65 = (bf16[2,160,2304]{2,1,0:T(8,128)(2,1)S(1)}, bf16[2,160,2304]{2,1,0:T(8,128)(2,1)S(1)}, u32[]{:S(2)}, u32[]{:S(2)}) collective-permute-start(bf16[2,160,2304]{2,1,0:T(8,128)(2,1)S(1)} %copy-done.47), channel_id=1, source_target_pairs={{0,1},{1,0},{2,3},{3,2},{4,5},{5,4},{6,7},{7,6},{8,9},{9,8},{10,11... | collective-permute-start | bytes 4423688 | tf_op jit(solution)/shard_map/ppermute | solution.py:21
  (82 other events, 552.6 us)
Sparse Core Ops, SparseCore 0:
  36.8 135.3 all-gather.3
  203.8 113.3 all-gather.5
  319.4 97.4 all-gather.7
  530.3 92.2 reduce-scatter.4
  625.4 95.3 reduce-scatter.6
  729.0 80.0 reduce-scatter.8
  814.0 123.1 reduce-scatter.10

commit v4 on v3

--- a/solution.py
+++ b/solution.py
@@ -487,9 +487,10 @@
     gain_rows = -(-4 * depth // (32 * HD)) * 16
     gains = jnp.pad(gains, (0, gain_rows * 2 * HD - 4 * depth)).reshape(gain_rows, 2 * HD)
     w_own = jnp.concatenate([w_own, gains])
+    w_own, layer_in = lax.optimization_barrier((w_own, layer_in))
     own_x = in_order(layer_in.reshape(1, ts, sub, width))[0]
     own_x = own_x.reshape(2, 2, sub, width).transpose(1, 0, 2, 3)
-    w_own, to_far = lax.optimization_barrier((w_own, own_x[0]))
+    to_far = own_x[0]
     ring = [w_own]
     far_move = Move(to_far, swap_x)
     far_move.result = swap_x(to_far)

time: 1020 us -> 1010 us (level)
  waiting for transfers between devices: 496 us -> 434 us
  starting transfers between devices: 103 us -> 162 us
    ppermute x65, waiting for transfers between devices: 290 us -> 244 us  [swap(): lax.ppermute(value, axis, [(i, i ^ bit) for i in range(lax.axis_size(axis...]
    ppermute x9, starting transfers between devices: 28.5 us -> 71.6 us  [turn(): lax.ppermute(value, 'fsdp', [(i, (i + 1) % size) for i in range(size)])]
    ppermute x9, waiting for transfers between devices: 156 us -> 140 us  [turn(): lax.ppermute(value, 'fsdp', [(i, (i + 1) % size) for i in range(size)])]
    ppermute x65, starting transfers between devices: 74 us -> 89.3 us  [swap(): lax.ppermute(value, axis, [(i, i ^ bit) for i in range(lax.axis_size(axis...]
    unnamed x144 -> x150, local copies, waits for them, and re-layouts: 40.9 us -> 40.3 us
  transfers between devices with their start and end apart: 81 -> 81, of which waited for: 56 -> 54; matrix products, arithmetic and copies ran while one was open for 11% -> 11% of each run, Pallas kernels for 19% -> 19%
where the time goes in v4:
time: 1010 us; the launch traced here: 999 us
  waiting for transfers between devices  434 us (43%)
  Pallas kernels  220 us (22%)
  starting transfers between devices  162 us (16%)
  local copies, waits for them, and re-layouts  91 us (9%)
  other arithmetic  76.5 us (8%)
  between operations  15.8 us (2%)
    ppermute x65, waiting for transfers between devices, swap(): lax.ppermute(value, axis, [(i, i ^ bit) for i in range(lax.axis_size(axis...  244 us
    pallas_call x24, Pallas kernels, tiled(): pl.pallas_call(body, grid=(rows // tile,), in_specs=in_specs, out_specs=[...  187 us
    ppermute x9, waiting for transfers between devices, turn(): lax.ppermute(value, 'fsdp', [(i, (i + 1) % size) for i in range(size)])  140 us
    ppermute x65, starting transfers between devices, swap(): lax.ppermute(value, axis, [(i, i ^ bit) for i in range(lax.axis_size(axis...  89.3 us
    ppermute x9, starting transfers between devices, turn(): lax.ppermute(value, 'fsdp', [(i, (i + 1) % size) for i in range(size)])  71.6 us
    all_gather x3, waiting for transfers between devices, gathered(): return lax.all_gather(part, 'fsdp', axis=0, tiled=True)  50.3 us
    unnamed x150, local copies, waits for them, and re-layouts  40.3 us
    pallas_call x1, Pallas kernels, attend_back(): pl.pallas_call(functools.partial(backward_kernel, zs, rows, block), grid_...  21.4 us
  transfers between devices with their start and end apart: 81, of which 54 were waited for; matrix products, arithmetic and copies ran while one was open for 11% of the time, Pallas kernels for 19%

profile of v4, /device:TPU:0, one launch (start us, length us, event | category | flops | bytes accessed | tf_op | source)
XLA Modules:
  0.0 999.4 jit_solution(17803655983081519519)
XLA Ops:
  17.2 14.6 %collective-permute-done = bf16[592,512]{1,0:T(8,128)(2,1)} collective-permute-done((bf16[592,512]{1,0:T(8,128)(2,1)S(1)}, bf16[592,512]{1,0:T(8,128)(2,1)}, u32[]{:S(2)}, u32[]{:S(2)}) %collective-permute-start) | collective-permute-done | bytes 606240 | tf_op jit(solution)/shard_map/ppermute | solution.py:38
  43.5 25.1 %collective-permute-done.1 = bf16[592,512]{1,0:T(8,128)(2,1)S(1)} collective-permute-done((bf16[592,512]{1,0:T(8,128)(2,1)}, bf16[592,512]{1,0:T(8,128)(2,1)S(1)}, u32[]{:S(2)}, u32[]{:S(2)}) %collective-permute-start.1) | collective-permute-done | bytes 606240 | tf_op jit(solution)/shard_map/ppermute | solution.py:38
  69.3 7.8 collective-permute-start.3
  79.1 26.7 %collective-permute-done.3 = bf16[592,512]{1,0:T(8,128)(2,1)S(1)} collective-permute-done((bf16[592,512]{1,0:T(8,128)(2,1)S(1)}, bf16[592,512]{1,0:T(8,128)(2,1)S(1)}, u32[]{:S(2)}, u32[]{:S(2)}) %collective-permute-start.3) | collective-permute-done | bytes 606240 | tf_op jit(solution)/shard_map/ppermute | solution.py:38
  106.9 5.2 shard_map.237
  115.4 5.3 shard_map.238
  126.5 14.1 %collective-permute-start.5 = (bf16[2,640,256]{2,1,0:T(8,128)(2,1)}, bf16[2,640,256]{2,1,0:T(8,128)(2,1)}, u32[]{:S(2)}, u32[]{:S(2)}) collective-permute-start(bf16[2,640,256]{2,1,0:T(8,128)(2,1)} %pad_maximum_fusion.20), channel_id=1, source_target_pairs={{0,4},{4,8},{8,12},{12,0},{1,5},{5,9},{9,13},{13,1},{2,6},{6,10},{... | collective-permute-start | bytes 1966088 | tf_op jit(solution)/shard_map/ppermute | solution.py:38
  140.6 28.1 %collective-permute-done.5 = bf16[2,640,256]{2,1,0:T(8,128)(2,1)} collective-permute-done((bf16[2,640,256]{2,1,0:T(8,128)(2,1)}, bf16[2,640,256]{2,1,0:T(8,128)(2,1)}, u32[]{:S(2)}, u32[]{:S(2)}) %collective-permute-start.5) | collective-permute-done | bytes 655392 | tf_op jit(solution)/shard_map/ppermute | solution.py:38
  173.1 10.4 %collective-permute-done.6 = bf16[2,640,256]{2,1,0:T(8,128)(2,1)} collective-permute-done((bf16[2,640,256]{2,1,0:T(8,128)(2,1)}, bf16[2,640,256]{2,1,0:T(8,128)(2,1)}, u32[]{:S(2)}, u32[]{:S(2)}) %collective-permute-start.6) | collective-permute-done | bytes 655392 | tf_op jit(solution)/shard_map/ppermute | solution.py:38
  191.7 6.7 collective-permute-done.7
  208.0 9.6 collective-permute-done.10
  218.5 7.4 collective-permute-done.11
  231.0 11.2 %shard_map.239 = (bf16[2,640,256]{2,1,0:T(8,128)(2,1)S(1)}, f32[2,640,1]{2,1,0:T(8,128)S(1)}) custom-call(s32[4]{0:T(128)S(1)} %pad_add_fusion.info, bf16[2,640,256]{2,1,0:T(8,128)(2,1)S(1)} %fusion.23.q_ref, bf16[2,4,2,640,256]{4,3,2,1,0:T(8,128)(2,1)} %bitcast.27.kv_ref, s32[640,1]{1,0:T(8,128)S(1)} %copy.75.col_ref, s32[1,640]{1,0:T(1,128)S(1)} %get-tuple-element.407.row_ref), custom_call_target="tpu_custom_call" | custom-call | flops 500000000 | bytes 1000000 | tf_op jit(solution)/shard_map/pallas_call | solution.py:249
  245.7 5.6 collective-permute-done.15.refs_2_
  260.9 16.8 %collective-permute-done.16 = bf16[2,160,1152]{2,1,0:T(8,128)(2,1)S(1)} collective-permute-done((bf16[2,160,1152]{2,1,0:T(8,128)(2,1)S(1)}, bf16[2,160,1152]{2,1,0:T(8,128)(2,1)S(1)}, u32[]{:S(2)}, u32[]{:S(2)}) %collective-permute-start.16) | collective-permute-done | bytes 737312 | tf_op jit(solution)/shard_map/ppermute | solution.py:21
  285.4 5.5 collective-permute-done.18
  296.9 14.5 %all-gather.6.cloned.1.call-done.up_w.refs_3_ = bf16[2304,1152]{1,0:T(8,128)(2,1)} async-done(((bf16[576,1152]{1,0:T(8,128)(2,1)}), bf16[2304,1152]{1,0:T(8,128)(2,1)}) %all-gather.6.cloned.1.call-update) | async-done | bytes 5308432 | tf_op jit(solution)/shard_map/all_gather | solution.py:471
  314.3 7.8 collective-permute-done.20
  326.2 14.6 %collective-permute-done.22 = bf16[2,160,1152]{2,1,0:T(8,128)(2,1)S(1)} collective-permute-done((bf16[2,160,1152]{2,1,0:T(8,128)(2,1)S(1)}, bf16[2,160,1152]{2,1,0:T(8,128)(2,1)S(1)}, u32[]{:S(2)}, u32[]{:S(2)}) %collective-permute-start.22) | collective-permute-done | bytes 737312 | tf_op jit(solution)/shard_map/ppermute | solution.py:21
  344.3 13.7 %shard_map.242 = (f32[640,1152]{1,0:T(8,128)}, f32[640,1152]{1,0:T(8,128)}, bf16[640,1152]{1,0:T(8,128)(2,1)S(1)}) custom-call(bf16[640,2304]{1,0:T(8,128)(2,1)} %bitcast.346, bf16[2304,1152]{1,0:T(8,128)(2,1)} %all-gather.4.cloned.1.call-done.gate_w.refs_2_, bf16[2304,1152]{1,0:T(8,128)(2,1)} %all-gather.6.cloned.1.call-done.up_w.refs_3_), custom_call_target="tpu_custom_call" | custom-call | flops 500000000 | bytes 1000000 | tf_op jit(solution)/shard_map/pallas_call | solution.py:319
  359.6 13.7 %shard_map.243 = (f32[640,1152]{1,0:T(8,128)}, f32[640,1152]{1,0:T(8,128)}, bf16[640,1152]{1,0:T(8,128)(2,1)S(1)}) custom-call(bf16[640,2304]{1,0:T(8,128)(2,1)} %copy-done.17, bf16[2304,1152]{1,0:T(8,128)(2,1)} %all-gather.4.cloned.1.call-done.gate_w.refs_2_, bf16[2304,1152]{1,0:T(8,128)(2,1)} %all-gather.6.cloned.1.call-done.up_w.refs_3_), custom_call_target="tpu_custom_call" | custom-call | flops 500000000 | bytes 1000000 | tf_op jit(solution)/shard_map/pallas_call | solution.py:319
  374.5 35.8 %all-gather.8.cloned.1.call-done.refs_1_.w_ref = bf16[2304,1152]{1,0:T(8,128)(2,1)} async-done(((bf16[576,1152]{1,0:T(8,128)(2,1)}), bf16[2304,1152]{1,0:T(8,128)(2,1)}) %all-gather.8.cloned.1.call-update) | async-done | bytes 5308432 | tf_op jit(solution)/shard_map/all_gather | solution.py:471
  411.7 7.9 shard_map.244
  419.6 5.6 collective-permute-done.25.refs_2_
  426.8 8.3 shard_map.245
  440.6 15.6 %collective-permute-done.26 = bf16[2,160,1152]{2,1,0:T(8,128)(2,1)S(1)} collective-permute-done((bf16[2,160,1152]{2,1,0:T(8,128)(2,1)S(1)}, bf16[2,160,1152]{2,1,0:T(8,128)(2,1)S(1)}, u32[]{:S(2)}, u32[]{:S(2)}) %collective-permute-start.26) | collective-permute-done | bytes 737312 | tf_op jit(solution)/shard_map/ppermute | solution.py:21
  461.8 7.7 collective-permute-done.28
  479.7 6.5 collective-permute-done.30
  489.8 12.5 %collective-permute-done.32 = bf16[2,160,1152]{2,1,0:T(8,128)(2,1)S(1)} collective-permute-done((bf16[2,160,1152]{2,1,0:T(8,128)(2,1)S(1)}, bf16[2,160,1152]{2,1,0:T(8,128)(2,1)S(1)}, u32[]{:S(2)}, u32[]{:S(2)}) %collective-permute-start.32) | collective-permute-done | bytes 737312 | tf_op jit(solution)/shard_map/ppermute | solution.py:21
  503.7 5.4 collective-permute-done.34.refs_1_.dm_ref
  510.7 13.0 %shard_map.246 = bf16[2304,1152]{1,0:T(8,128)(2,1)} custom-call(bf16[640,2304]{1,0:T(8,128)(2,1)} %bitcast.350, bf16[640,2304]{1,0:T(8,128)(2,1)} %copy-done.30, bf16[640,1152]{1,0:T(8,128)(2,1)S(1)} %get-tuple-element.204.refs_0_.refs_2_, bf16[640,1152]{1,0:T(8,128)(2,1)} %copy-done.2), custom_call_target="tpu_custom_call" | custom-call | flops 500000000 | bytes 1000000 | tf_op jit(solution)/shard_map/pallas_call | solution.py:319
  523.8 10.3 %shard_map.248 = (bf16[640,1152]{1,0:T(8,128)(2,1)S(1)}, bf16[640,1152]{1,0:T(8,128)(2,1)}) custom-call(bf16[640,2304]{1,0:T(8,128)(2,1)} %copy-done.30, bf16[2304,1152]{1,0:T(8,128)(2,1)} %all-gather.8.cloned.1.call-done.refs_1_.w_ref, f32[640,1152]{1,0:T(8,128)} %get-tuple-element.212.gate_ref, f32[640,1152]{1,0:T(8,128)} %get-tuple-element.213.up_ref), custom_call_target="tpu_custom_call" | custom-call | flops 500000000 | bytes 1000000 | tf_op jit(solution)/shard_map/pallas_call | solution.py:319
  534.0 14.1 %shard_map.249 = bf16[640,2304]{1,0:T(8,128)(2,1)} custom-call(bf16[640,1152]{1,0:T(8,128)(2,1)S(1)} %get-tuple-element.221.refs_0_.refs_3_, bf16[640,1152]{1,0:T(8,128)(2,1)} %get-tuple-element.227.refs_1_.refs_3_, bf16[2304,1152]{1,0:T(8,128)(2,1)} %all-gather.4.cloned.1.call-done.gate_w.refs_2_, bf16[2304,1152]{1,0:T(8,128)(2,1)} %all-gather.6.cloned.1.call-done.up_w.refs_3_), custom_call_target="tpu_custom_call" | custom-call | flops 500000000 | bytes 1000000 | tf_op jit(solution)/shard_map/pallas_call | solution.py:319
  548.1 10.1 %shard_map.247 = (bf16[640,1152]{1,0:T(8,128)(2,1)S(1)}, bf16[640,1152]{1,0:T(8,128)(2,1)}) custom-call(bf16[640,2304]{1,0:T(8,128)(2,1)} %bitcast.351, bf16[2304,1152]{1,0:T(8,128)(2,1)} %all-gather.8.cloned.1.call-done.refs_1_.w_ref, f32[640,1152]{1,0:T(8,128)} %get-tuple-element.207.gate_ref, f32[640,1152]{1,0:T(8,128)} %get-tuple-element.208.up_ref), custom_call_target="tpu_custom_call" | custom-call | flops 500000000 | bytes 1000000 | tf_op jit(solution)/shard_map/pallas_call | solution.py:319
  559.9 13.9 %shard_map.250 = bf16[640,2304]{1,0:T(8,128)(2,1)} custom-call(bf16[640,1152]{1,0:T(8,128)(2,1)S(1)} %get-tuple-element.220.refs_0_.refs_2_, bf16[640,1152]{1,0:T(8,128)(2,1)} %get-tuple-element.226.refs_1_.refs_2_, bf16[2304,1152]{1,0:T(8,128)(2,1)} %all-gather.4.cloned.1.call-done.gate_w.refs_2_, ...), custom_call_target="tpu_custom_call" | custom-call | flops 500000000 | bytes 1000000 | tf_op jit(solution)/shard_map/pallas_call | solution.py:319
  579.1 12.8 %shard_map.251 = bf16[2304,1152]{1,0:T(8,128)(2,1)} custom-call(bf16[640,2304]{1,0:T(8,128)(2,1)} %bitcast.347, bf16[640,2304]{1,0:T(8,128)(2,1)} %copy-done.17, bf16[640,1152]{1,0:T(8,128)(2,1)S(1)} %get-tuple-element.220.refs_0_.refs_2_, bf16[640,1152]{1,0:T(8,128)(2,1)} %copy-done.6), custom_call_target="tpu_custom_call" | custom-call | flops 500000000 | bytes 1000000 | tf_op jit(solution)/shard_map/pallas_call | solution.py:319
  591.9 4.3 collective-permute-done.36
  603.1 13.2 %shard_map.252 = bf16[2304,1152]{1,0:T(8,128)(2,1)} custom-call(bf16[640,2304]{1,0:T(8,128)(2,1)} %bitcast.348, bf16[640,2304]{1,0:T(8,128)(2,1)} %copy-done.17, bf16[640,1152]{1,0:T(8,128)(2,1)S(1)} %copy-done.4, bf16[640,1152]{1,0:T(8,128)(2,1)} %get-tuple-element.227.refs_1_.refs_3_), custom_call_target="tpu_custom_call" | custom-call | flops 500000000 | bytes 1000000 | tf_op jit(solution)/shard_map/pallas_call | solution.py:319
  626.2 7.6 collective-permute-done.40
  636.8 14.6 %collective-permute-done.42 = bf16[2,160,1152]{2,1,0:T(8,128)(2,1)S(1)} collective-permute-done((bf16[2,160,1152]{2,1,0:T(8,128)(2,1)S(1)}, bf16[2,160,1152]{2,1,0:T(8,128)(2,1)S(1)}, u32[]{:S(2)}, u32[]{:S(2)}) %collective-permute-start.42) | collective-permute-done | bytes 737312 | tf_op jit(solution)/shard_map/ppermute | solution.py:21
  662.3 5.8 shard_map.255
  673.6 21.4 %shard_map.256 = (f32[2,640,256]{2,1,0:T(8,128)}, bf16[2,4,2,640,256]{4,3,2,1,0:T(8,128)(2,1)}) custom-call(s32[4]{0:T(128)} %copy-done.12, bf16[2,640,256]{2,1,0:T(8,128)(2,1)} %copy-done.5, bf16[2,640,256]{2,1,0:T(8,128)(2,1)} %bitcast.382, f32[4,1,320]{2,1,0:T(1,128)} %reshape.610.lse_ref, f32[4,1,320]{2,1,0:T(1,128)} %reshape.576.delta_ref, ...), custom_call_target="tpu_custom_call" | custom-call | flops 500000000 | bytes 1000000 | tf_op jit(solution)/shard_map/pallas_call | solution.py:280
  704.6 5.8 shard_map.257
  712.0 7.9 collective-permute-done.46
  738.1 14.3 %collective-permute-done.49 = bf16[2,640,256]{2,1,0:T(8,128)(2,1)S(1)} collective-permute-done((bf16[2,640,256]{2,1,0:T(8,128)(2,1)}, bf16[2,640,256]{2,1,0:T(8,128)(2,1)S(1)}, u32[]{:S(2)}, u32[]{:S(2)}) %collective-permute-start.49) | collective-permute-done | bytes 655392 | tf_op jit(solution)/shard_map/ppermute | solution.py:38
  755.8 25.6 %collective-permute-start.51 = (bf16[2,640,256]{2,1,0:T(8,128)(2,1)S(1)}, bf16[2,640,256]{2,1,0:T(8,128)(2,1)S(1)}, u32[]{:S(2)}, u32[]{:S(2)}) collective-permute-start(bf16[2,640,256]{2,1,0:T(8,128)(2,1)S(1)} %fusion.25), channel_id=1, source_target_pairs={{0,4},{4,8},{8,12},{12,0},{1,5},{5,9},{9,13},{13,1},{2,6},{6,10},{... | collective-permute-start | bytes 1966088 | tf_op jit(solution)/shard_map/ppermute | solution.py:38
  781.4 10.4 %collective-permute-done.50 = bf16[2,640,256]{2,1,0:T(8,128)(2,1)S(1)} collective-permute-done((bf16[2,640,256]{2,1,0:T(8,128)(2,1)S(1)}, bf16[2,640,256]{2,1,0:T(8,128)(2,1)S(1)}, u32[]{:S(2)}, u32[]{:S(2)}) %collective-permute-start.50) | collective-permute-done | bytes 655392 | tf_op jit(solution)/shard_map/ppermute | solution.py:21
  791.8 4.9 collective-permute-done.51
  800.3 18.0 %collective-permute-start.54 = (bf16[2,640,256]{2,1,0:T(8,128)(2,1)S(1)}, bf16[2,640,256]{2,1,0:T(8,128)(2,1)}, u32[]{:S(2)}, u32[]{:S(2)}) collective-permute-start(bf16[2,640,256]{2,1,0:T(8,128)(2,1)S(1)} %fusion.27), channel_id=1, source_target_pairs={{0,4},{4,8},{8,12},{12,0},{1,5},{5,9},{9,13},{13,1},{2,6},{6,10},{... | collective-permute-start | bytes 1966088 | tf_op jit(solution)/shard_map/ppermute | solution.py:38
  818.3 9.7 collective-permute-done.54
  832.7 6.9 shard_map.260
  839.7 4.5 shard_map.261
  850.1 5.4 shard_map.262
  857.9 4.8 collective-permute-done.56
  864.4 5.3 convert_bitcast_fusion
  872.3 8.7 collective-permute-done.57
  886.8 17.2 %collective-permute-start.61 = (bf16[576,256]{1,0:T(8,128)(2,1)S(1)}, bf16[576,256]{1,0:T(8,128)(2,1)S(1)}, u32[]{:S(2)}, u32[]{:S(2)}) collective-permute-start(bf16[576,256]{1,0:T(8,128)(2,1)S(1)} %get-tuple-element.282), channel_id=1, source_target_pairs={{0,4},{4,0},{8,12},{12,8},{1,5},{5,1},{9,13},{13,9},{2,6},{6,2},{1... | collective-permute-start | bytes 884744 | tf_op jit(solution)/shard_map/ppermute | solution.py:21
  908.0 8.1 collective-permute-done.60
  918.1 7.8 collective-permute-done.61
  925.9 8.8 collective-permute-done.63
  934.8 6.9 collective-permute-start.69
  947.7 11.5 %collective-permute-done.64 = bf16[160,2304]{1,0:T(8,128)(2,1)S(1)} collective-permute-done((bf16[160,2304]{1,0:T(8,128)(2,1)S(1)}, bf16[160,2304]{1,0:T(8,128)(2,1)S(1)}, u32[]{:S(2)}, u32[]{:S(2)}) %collective-permute-start.64) | collective-permute-done | bytes 737312 | tf_op jit(solution)/shard_map/ppermute | solution.py:21
  968.8 4.4 collective-permute-done.73
  976.1 5.3 collective-permute-done.68
  (469 shorter events, 271.0 us)
Async XLA Ops:
  7.2 219.6 %all-gather.4.cloned.1.call-start = ((), (), s32[]{:S(2)}) async-start(), calls=%async_computation.4 | async-start | bytes 6635520 | tf_op jit(solution)/shard_map/all_gather | solution.py:471
  12.9 18.9 %collective-permute-start = (bf16[592,512]{1,0:T(8,128)(2,1)S(1)}, bf16[592,512]{1,0:T(8,128)(2,1)}, u32[]{:S(2)}, u32[]{:S(2)}) collective-permute-start(bf16[592,512]{1,0:T(8,128)(2,1)S(1)} %pad_maximum_fusion.26), channel_id=1, source_target_pairs={{0,4},{4,8},{8,12},{12,0},{1,5},{5,9},{9,13},{13,1},{2,6},{6,10},{... | collective-permute-start | bytes 1818632 | tf_op jit(solution)/shard_map/ppermute | solution.py:38
  31.8 279.5 %all-gather.6.cloned.1.call-start = ((), (), s32[]{:S(2)}) async-start(), calls=%async_computation.5 | async-start | bytes 6635520 | tf_op jit(solution)/shard_map/all_gather | solution.py:471
  35.5 33.8 %collective-permute-start.2 = (bf16[2,160,2304]{2,1,0:T(8,128)(2,1)}, bf16[2,160,2304]{2,1,0:T(8,128)(2,1)}, u32[]{:S(2)}, u32[]{:S(2)}) collective-permute-start(bf16[2,160,2304]{2,1,0:T(8,128)(2,1)} %slice_bitcast_fusion), channel_id=1, source_target_pairs={{0,16},{16,0},{1,17},{17,1},{2,18},{18,2},{3,19},{19,3},{4,20},{20... | collective-permute-start | bytes 4423688 | tf_op jit(solution)/shard_map/ppermute | solution.py:21
  39.1 29.5 %collective-permute-start.1 = (bf16[592,512]{1,0:T(8,128)(2,1)}, bf16[592,512]{1,0:T(8,128)(2,1)S(1)}, u32[]{:S(2)}, u32[]{:S(2)}) collective-permute-start(bf16[592,512]{1,0:T(8,128)(2,1)} %collective-permute-done), channel_id=1, source_target_pairs={{0,4},{4,8},{8,12},{12,0},{1,5},{5,9},{9,13},{13,1},{2,6},{6,10},{... | collective-permute-start | bytes 1818632 | tf_op jit(solution)/shard_map/ppermute | solution.py:38
  69.3 36.5 %collective-permute-start.3 = (bf16[592,512]{1,0:T(8,128)(2,1)S(1)}, bf16[592,512]{1,0:T(8,128)(2,1)S(1)}, u32[]{:S(2)}, u32[]{:S(2)}) collective-permute-start(bf16[592,512]{1,0:T(8,128)(2,1)S(1)} %collective-permute-done.1), channel_id=1, source_target_pairs={{0,4},{4,8},{8,12},{12,0},{1,5},{5,9},{9,13},{13,1},{2,6},{6,10},{... | collective-permute-start | bytes 1818632 | tf_op jit(solution)/shard_map/ppermute | solution.py:38
  77.1 35.1 %collective-permute-start.4 = (bf16[2,160,2304]{2,1,0:T(8,128)(2,1)}, bf16[2,160,2304]{2,1,0:T(8,128)(2,1)S(1)}, u32[]{:S(2)}, u32[]{:S(2)}) collective-permute-start(bf16[2,160,2304]{2,1,0:T(8,128)(2,1)} %collective-permute-done.2), channel_id=1, source_target_pairs={{0,1},{1,0},{2,3},{3,2},{4,5},{5,4},{6,7},{7,6},{8,9},{9,8},{10,11... | collective-permute-start | bytes 4423688 | tf_op jit(solution)/shard_map/ppermute | solution.py:21
  126.5 42.3 %collective-permute-start.5 = (bf16[2,640,256]{2,1,0:T(8,128)(2,1)}, bf16[2,640,256]{2,1,0:T(8,128)(2,1)}, u32[]{:S(2)}, u32[]{:S(2)}) collective-permute-start(bf16[2,640,256]{2,1,0:T(8,128)(2,1)} %pad_maximum_fusion.20), channel_id=1, source_target_pairs={{0,4},{4,8},{8,12},{12,0},{1,5},{5,9},{9,13},{13,1},{2,6},{6,10},{... | collective-permute-start | bytes 1966088 | tf_op jit(solution)/shard_map/ppermute | solution.py:38
  168.8 14.7 %collective-permute-start.6 = (bf16[2,640,256]{2,1,0:T(8,128)(2,1)}, bf16[2,640,256]{2,1,0:T(8,128)(2,1)}, u32[]{:S(2)}, u32[]{:S(2)}) collective-permute-start(bf16[2,640,256]{2,1,0:T(8,128)(2,1)} %collective-permute-done.5), channel_id=1, source_target_pairs={{0,4},{4,8},{8,12},{12,0},{1,5},{5,9},{9,13},{13,1},{2,6},{6,10},{... | collective-permute-start | bytes 1966088 | tf_op jit(solution)/shard_map/ppermute | solution.py:38
  172.9 31.1 %collective-permute-start.8 = (bf16[2,640,256]{2,1,0:T(8,128)(2,1)}, bf16[2,640,256]{2,1,0:T(8,128)(2,1)}, u32[]{:S(2)}, u32[]{:S(2)}) collective-permute-start(bf16[2,640,256]{2,1,0:T(8,128)(2,1)} %pad_maximum_fusion.20), channel_id=1, source_target_pairs={{0,16},{16,0},{1,17},{17,1},{2,18},{18,2},{3,19},{19,3},{4,20},{20... | collective-permute-start | bytes 1966088 | tf_op jit(solution)/shard_map/ppermute | solution.py:21
  183.4 15.0 %collective-permute-start.7 = (bf16[2,640,256]{2,1,0:T(8,128)(2,1)}, bf16[2,640,256]{2,1,0:T(8,128)(2,1)}, u32[]{:S(2)}, u32[]{:S(2)}) collective-permute-start(bf16[2,640,256]{2,1,0:T(8,128)(2,1)} %collective-permute-done.6), channel_id=1, source_target_pairs={{0,4},{4,8},{8,12},{12,0},{1,5},{5,9},{9,13},{13,1},{2,6},{6,10},{... | collective-permute-start | bytes 1966088 | tf_op jit(solution)/shard_map/ppermute | solution.py:38
  185.7 20.3 %collective-permute-start.9 = (bf16[2,640,256]{2,1,0:T(8,128)(2,1)}, bf16[2,640,256]{2,1,0:T(8,128)(2,1)}, u32[]{:S(2)}, u32[]{:S(2)}) collective-permute-start(bf16[2,640,256]{2,1,0:T(8,128)(2,1)} %collective-permute-done.5), channel_id=1, source_target_pairs={{0,16},{16,0},{1,17},{17,1},{2,18},{18,2},{3,19},{19,3},{4,20},{20... | collective-permute-start | bytes 1966088 | tf_op jit(solution)/shard_map/ppermute | solution.py:21
  188.1 29.5 %collective-permute-start.10 = (bf16[2,640,256]{2,1,0:T(8,128)(2,1)}, bf16[2,640,256]{2,1,0:T(8,128)(2,1)S(1)}, u32[]{:S(2)}, u32[]{:S(2)}) collective-permute-start(bf16[2,640,256]{2,1,0:T(8,128)(2,1)} %collective-permute-done.6), channel_id=1, source_target_pairs={{0,16},{16,0},{1,17},{17,1},{2,18},{18,2},{3,19},{19,3},{4,20},{20... | collective-permute-start | bytes 1966088 | tf_op jit(solution)/shard_map/ppermute | solution.py:21
  198.4 28.3 %collective-permute-start.12 = (bf16[576,256]{1,0:T(8,128)(2,1)}, bf16[576,256]{1,0:T(8,128)(2,1)S(1)}, u32[]{:S(2)}, u32[]{:S(2)}) collective-permute-start(bf16[576,256]{1,0:T(8,128)(2,1)} %get-tuple-element.172), channel_id=1, source_target_pairs={{0,4},{4,0},{8,12},{12,8},{1,5},{5,1},{9,13},{13,9},{2,6},{6,2},{1... | collective-permute-start | bytes 884744 | tf_op jit(solution)/shard_map/ppermute | solution.py:21
  198.4 28.3 %collective-permute-start.13 = (bf16[576,256]{1,0:T(8,128)(2,1)}, bf16[576,256]{1,0:T(8,128)(2,1)S(1)}, u32[]{:S(2)}, u32[]{:S(2)}) collective-permute-start(bf16[576,256]{1,0:T(8,128)(2,1)} %get-tuple-element.172), channel_id=1, source_target_pairs={{0,8},{4,12},{8,0},{12,4},{1,9},{5,13},{9,1},{13,5},{2,10},{6,14},... | collective-permute-start | bytes 884744 | tf_op jit(solution)/shard_map/ppermute | solution.py:21
  201.5 208.9 %all-gather.8.cloned.1.call-start = ((), (), s32[]{:S(2)}) async-start(), calls=%async_computation.6 | async-start | bytes 6635520 | tf_op jit(solution)/shard_map/all_gather | solution.py:471
  204.0 21.8 %collective-permute-start.11 = (bf16[2,640,256]{2,1,0:T(8,128)(2,1)}, bf16[2,640,256]{2,1,0:T(8,128)(2,1)S(1)}, u32[]{:S(2)}, u32[]{:S(2)}) collective-permute-start(bf16[2,640,256]{2,1,0:T(8,128)(2,1)} %collective-permute-done.7), channel_id=1, source_target_pairs={{0,16},{16,0},{1,17},{17,1},{2,18},{18,2},{3,19},{19,3},{4,20},{20... | collective-permute-start | bytes 1966088 | tf_op jit(solution)/shard_map/ppermute | solution.py:21
  226.8 16.1 %collective-permute-start.14 = (bf16[576,256]{1,0:T(8,128)(2,1)}, bf16[576,256]{1,0:T(8,128)(2,1)S(1)}, u32[]{:S(2)}, u32[]{:S(2)}) collective-permute-start(bf16[576,256]{1,0:T(8,128)(2,1)} %get-tuple-element.172), channel_id=1, source_target_pairs={{0,12},{4,8},{8,4},{12,0},{1,13},{5,9},{9,5},{13,1},{2,14},{6,10},... | collective-permute-start | bytes 884744 | tf_op jit(solution)/shard_map/ppermute | solution.py:21
  259.1 18.6 %collective-permute-start.16 = (bf16[2,160,1152]{2,1,0:T(8,128)(2,1)S(1)}, bf16[2,160,1152]{2,1,0:T(8,128)(2,1)S(1)}, u32[]{:S(2)}, u32[]{:S(2)}) collective-permute-start(bf16[2,160,1152]{2,1,0:T(8,128)(2,1)S(1)} %slice_bitcast_fusion.23), channel_id=1, source_target_pairs={{0,16},{16,0},{1,17},{17,1},{2,18},{18,2},{3,19},{19,3},{4,20},{20... | collective-permute-start | bytes 2211848 | tf_op jit(solution)/shard_map/ppermute | solution.py:21
  259.3 18.4 %collective-permute-start.17 = (bf16[2,160,1152]{2,1,0:T(8,128)(2,1)S(1)}, bf16[2,160,1152]{2,1,0:T(8,128)(2,1)S(1)}, u32[]{:S(2)}, u32[]{:S(2)}) collective-permute-start(bf16[2,160,1152]{2,1,0:T(8,128)(2,1)S(1)} %slice_bitcast_fusion.22), channel_id=1, source_target_pairs={{0,2},{1,3},{2,0},{3,1},{4,6},{5,7},{6,4},{7,5},{8,10},{9,11},{10,... | collective-permute-start | bytes 2211848 | tf_op jit(solution)/shard_map/ppermute | solution.py:21
  280.7 10.2 %collective-permute-start.18 = (bf16[160,1152]{1,0:T(8,128)(2,1)}, bf16[160,1152]{1,0:T(8,128)(2,1)}, u32[]{:S(2)}, u32[]{:S(2)}) collective-permute-start(bf16[160,1152]{1,0:T(8,128)(2,1)} %fusion.76), channel_id=1, source_target_pairs={{0,2},{1,3},{2,0},{3,1},{4,6},{5,7},{6,4},{7,5},{8,10},{9,11},{10,... | collective-permute-start | bytes 1105928 | tf_op jit(solution)/shard_map/ppermute | solution.py:21
  283.5 340.4 %reduce-scatter.5.cloned.1.call-start = ((), (), s32[]{:S(2)}) async-start(), calls=%async_computation.7 | async-start | bytes 6635520 | tf_op jit(solution)/shard_map/reduce_scatter | solution.py:587
  311.3 10.7 %collective-permute-start.20 = (bf16[160,1152]{1,0:T(8,128)(2,1)}, bf16[160,1152]{1,0:T(8,128)(2,1)S(1)}, u32[]{:S(2)}, u32[]{:S(2)}) collective-permute-start(bf16[160,1152]{1,0:T(8,128)(2,1)} %get-tuple-element.182), channel_id=1, source_target_pairs={{0,16},{16,0},{1,17},{17,1},{2,18},{18,2},{3,19},{19,3},{4,20},{20... | collective-permute-start | bytes 1105928 | tf_op jit(solution)/shard_map/ppermute | solution.py:21
  312.8 10.4 %collective-permute-start.21 = (bf16[160,1152]{1,0:T(8,128)(2,1)}, bf16[160,1152]{1,0:T(8,128)(2,1)S(1)}, u32[]{:S(2)}, u32[]{:S(2)}) collective-permute-start(bf16[160,1152]{1,0:T(8,128)(2,1)} %get-tuple-element.183), channel_id=1, source_target_pairs={{0,2},{1,3},{2,0},{3,1},{4,6},{5,7},{6,4},{7,5},{8,10},{9,11},{10,... | collective-permute-start | bytes 1105928 | tf_op jit(solution)/shard_map/ppermute | solution.py:21
  323.3 17.5 %collective-permute-start.22 = (bf16[2,160,1152]{2,1,0:T(8,128)(2,1)S(1)}, bf16[2,160,1152]{2,1,0:T(8,128)(2,1)S(1)}, u32[]{:S(2)}, u32[]{:S(2)}) collective-permute-start(bf16[2,160,1152]{2,1,0:T(8,128)(2,1)S(1)} %pad_maximum_fusion.14), channel_id=1, source_target_pairs={{0,2},{1,3},{2,0},{3,1},{4,6},{5,7},{6,4},{7,5},{8,10},{9,11},{10,... | collective-permute-start | bytes 2211848 | tf_op jit(solution)/shard_map/ppermute | solution.py:21
  324.9 17.2 %collective-permute-start.23 = (bf16[2,160,1152]{2,1,0:T(8,128)(2,1)S(1)}, bf16[2,160,1152]{2,1,0:T(8,128)(2,1)S(1)}, u32[]{:S(2)}, u32[]{:S(2)}) collective-permute-start(bf16[2,160,1152]{2,1,0:T(8,128)(2,1)S(1)} %pad_maximum_fusion.15), channel_id=1, source_target_pairs={{0,16},{16,0},{1,17},{17,1},{2,18},{18,2},{3,19},{19,3},{4,20},{20... | collective-permute-start | bytes 2211848 | tf_op jit(solution)/shard_map/ppermute | solution.py:21
  342.7 15.3 %collective-permute-start.24 = (bf16[640,2304]{1,0:T(8,128)(2,1)S(1)}, bf16[640,2304]{1,0:T(8,128)(2,1)S(1)}, u32[]{:S(2)}, u32[]{:S(2)}) collective-permute-start(bf16[640,2304]{1,0:T(8,128)(2,1)S(1)} %bitcast.345), channel_id=1, source_target_pairs={{0,1},{1,0},{2,3},{3,2},{4,5},{5,4},{6,7},{7,6},{8,9},{9,8},{10,11... | collective-permute-start | bytes 8847368 | tf_op jit(solution)/shard_map/ppermute | solution.py:21
  437.6 18.6 %collective-permute-start.26 = (bf16[2,160,1152]{2,1,0:T(8,128)(2,1)S(1)}, bf16[2,160,1152]{2,1,0:T(8,128)(2,1)S(1)}, u32[]{:S(2)}, u32[]{:S(2)}) collective-permute-start(bf16[2,160,1152]{2,1,0:T(8,128)(2,1)S(1)} %slice_bitcast_fusion.17), channel_id=1, source_target_pairs={{0,16},{16,0},{1,17},{17,1},{2,18},{18,2},{3,19},{19,3},{4,20},{20... | collective-permute-start | bytes 2211848 | tf_op jit(solution)/shard_map/ppermute | solution.py:21
  439.2 18.3 %collective-permute-start.27 = (bf16[2,160,1152]{2,1,0:T(8,128)(2,1)S(1)}, bf16[2,160,1152]{2,1,0:T(8,128)(2,1)S(1)}, u32[]{:S(2)}, u32[]{:S(2)}) collective-permute-start(bf16[2,160,1152]{2,1,0:T(8,128)(2,1)S(1)} %slice_bitcast_fusion.16), channel_id=1, source_target_pairs={{0,2},{1,3},{2,0},{3,1},{4,6},{5,7},{6,4},{7,5},{8,10},{9,11},{10,... | collective-permute-start | bytes 2211848 | tf_op jit(solution)/shard_map/ppermute | solution.py:21
  486.9 15.5 %collective-permute-start.32 = (bf16[2,160,1152]{2,1,0:T(8,128)(2,1)S(1)}, bf16[2,160,1152]{2,1,0:T(8,128)(2,1)S(1)}, u32[]{:S(2)}, u32[]{:S(2)}) collective-permute-start(bf16[2,160,1152]{2,1,0:T(8,128)(2,1)S(1)} %pad_maximum_fusion.16), channel_id=1, source_target_pairs={{0,2},{1,3},{2,0},{3,1},{4,6},{5,7},{6,4},{7,5},{8,10},{9,11},{10,... | collective-permute-start | bytes 2211848 | tf_op jit(solution)/shard_map/ppermute | solution.py:21
  488.4 14.7 %collective-permute-start.33 = (bf16[2,160,1152]{2,1,0:T(8,128)(2,1)S(1)}, bf16[2,160,1152]{2,1,0:T(8,128)(2,1)S(1)}, u32[]{:S(2)}, u32[]{:S(2)}) collective-permute-start(bf16[2,160,1152]{2,1,0:T(8,128)(2,1)S(1)} %pad_maximum_fusion.17), channel_id=1, source_target_pairs={{0,16},{16,0},{1,17},{17,1},{2,18},{18,2},{3,19},{19,3},{4,20},{20... | collective-permute-start | bytes 2211848 | tf_op jit(solution)/shard_map/ppermute | solution.py:21
  523.7 198.6 %reduce-scatter.7.cloned.1.call-start = ((), (), s32[]{:S(2)}) async-start(), calls=%async_computation.8 | async-start | bytes 6635520 | tf_op jit(solution)/shard_map/reduce_scatter | solution.py:587
  548.1 10.2 %collective-permute-start.35 = (bf16[640,2304]{1,0:T(8,128)(2,1)}, bf16[640,2304]{1,0:T(8,128)(2,1)S(1)}, u32[]{:S(2)}, u32[]{:S(2)}) collective-permute-start(bf16[640,2304]{1,0:T(8,128)(2,1)} %shard_map.249), channel_id=1, source_target_pairs={{0,1},{1,0},{2,3},{3,2},{4,5},{5,4},{6,7},{7,6},{8,9},{9,8},{10,11... | collective-permute-start | bytes 8847368 | tf_op jit(solution)/shard_map/ppermute | solution.py:21
  577.0 19.1 %collective-permute-start.36 = (bf16[2,160,1152]{2,1,0:T(8,128)(2,1)}, bf16[2,160,1152]{2,1,0:T(8,128)(2,1)S(1)}, u32[]{:S(2)}, u32[]{:S(2)}) collective-permute-start(bf16[2,160,1152]{2,1,0:T(8,128)(2,1)} %slice_bitcast_fusion.11), channel_id=1, source_target_pairs={{0,16},{16,0},{1,17},{17,1},{2,18},{18,2},{3,19},{19,3},{4,20},{20... | collective-permute-start | bytes 2211848 | tf_op jit(solution)/shard_map/ppermute | solution.py:21
  578.3 18.7 %collective-permute-start.37 = (bf16[2,160,1152]{2,1,0:T(8,128)(2,1)S(1)}, bf16[2,160,1152]{2,1,0:T(8,128)(2,1)}, u32[]{:S(2)}, u32[]{:S(2)}) collective-permute-start(bf16[2,160,1152]{2,1,0:T(8,128)(2,1)S(1)} %slice_bitcast_fusion.10), channel_id=1, source_target_pairs={{0,2},{1,3},{2,0},{3,1},{4,6},{5,7},{6,4},{7,5},{8,10},{9,11},{10,... | collective-permute-start | bytes 2211848 | tf_op jit(solution)/shard_map/ppermute | solution.py:21
  601.2 15.2 %collective-permute-start.38 = (bf16[160,1152]{1,0:T(8,128)(2,1)}, bf16[160,1152]{1,0:T(8,128)(2,1)}, u32[]{:S(2)}, u32[]{:S(2)}) collective-permute-start(bf16[160,1152]{1,0:T(8,128)(2,1)} %fusion.80), channel_id=1, source_target_pairs={{0,2},{1,3},{2,0},{3,1},{4,6},{5,7},{6,4},{7,5},{8,10},{9,11},{10,... | collective-permute-start | bytes 1105928 | tf_op jit(solution)/shard_map/ppermute | solution.py:21
  601.8 16.0 %collective-permute-start.39 = (bf16[160,1152]{1,0:T(8,128)(2,1)}, bf16[160,1152]{1,0:T(8,128)(2,1)}, u32[]{:S(2)}, u32[]{:S(2)}) collective-permute-start(bf16[160,1152]{1,0:T(8,128)(2,1)} %fusion.81), channel_id=1, source_target_pairs={{0,16},{16,0},{1,17},{17,1},{2,18},{18,2},{3,19},{19,3},{4,20},{20... | collective-permute-start | bytes 1105928 | tf_op jit(solution)/shard_map/ppermute | solution.py:21
  603.1 229.6 %reduce-scatter.9.cloned.1.call-start = ((), (), s32[]{:S(2)}) async-start(), calls=%async_computation.9 | async-start | bytes 2949120 | tf_op jit(solution)/shard_map/reduce_scatter | solution.py:587
  634.6 16.8 %collective-permute-start.42 = (bf16[2,160,1152]{2,1,0:T(8,128)(2,1)S(1)}, bf16[2,160,1152]{2,1,0:T(8,128)(2,1)S(1)}, u32[]{:S(2)}, u32[]{:S(2)}) collective-permute-start(bf16[2,160,1152]{2,1,0:T(8,128)(2,1)S(1)} %pad_maximum_fusion.18), channel_id=1, source_target_pairs={{0,2},{1,3},{2,0},{3,1},{4,6},{5,7},{6,4},{7,5},{8,10},{9,11},{10,... | collective-permute-start | bytes 2211848 | tf_op jit(solution)/shard_map/ppermute | solution.py:21
  635.9 16.3 %collective-permute-start.43 = (bf16[2,160,1152]{2,1,0:T(8,128)(2,1)S(1)}, bf16[2,160,1152]{2,1,0:T(8,128)(2,1)S(1)}, u32[]{:S(2)}, u32[]{:S(2)}) collective-permute-start(bf16[2,160,1152]{2,1,0:T(8,128)(2,1)S(1)} %pad_maximum_fusion.19), channel_id=1, source_target_pairs={{0,16},{16,0},{1,17},{17,1},{2,18},{18,2},{3,19},{19,3},{4,20},{20... | collective-permute-start | bytes 2211848 | tf_op jit(solution)/shard_map/ppermute | solution.py:21
  669.5 31.6 %collective-permute-start.45 = (bf16[576,1152]{1,0:T(8,128)(2,1)}, bf16[576,1152]{1,0:T(8,128)(2,1)}, u32[]{:S(2)}, u32[]{:S(2)}) collective-permute-start(bf16[576,1152]{1,0:T(8,128)(2,1)} %reduce-scatter.5.cloned.1.call-done), channel_id=1, source_target_pairs={{0,16},{16,0},{1,17},{17,1},{2,18},{18,2},{3,19},{19,3},{4,20},{20... | collective-permute-start | bytes 3981320 | tf_op jit(solution)/shard_map/ppermute | solution.py:21
  672.6 49.6 %collective-permute-start.47 = (bf16[160,2304]{1,0:T(8,128)(2,1)S(1)}, bf16[160,2304]{1,0:T(8,128)(2,1)}, u32[]{:S(2)}, u32[]{:S(2)}) collective-permute-start(bf16[160,2304]{1,0:T(8,128)(2,1)S(1)} %copy-done.54), channel_id=1, source_target_pairs={{0,2},{1,3},{2,0},{3,1},{4,6},{5,7},{6,4},{7,5},{8,10},{9,11},{10,... | collective-permute-start | bytes 2211848 | tf_op jit(solution)/shard_map/ppermute | solution.py:21
  703.4 16.5 %collective-permute-start.46 = (bf16[2,640,256]{2,1,0:T(8,128)(2,1)}, bf16[2,640,256]{2,1,0:T(8,128)(2,1)}, u32[]{:S(2)}, u32[]{:S(2)}) collective-permute-start(bf16[2,640,256]{2,1,0:T(8,128)(2,1)} %get-tuple-element.323), channel_id=1, source_target_pairs={{0,16},{16,0},{1,17},{17,1},{2,18},{18,2},{3,19},{19,3},{4,20},{20... | collective-permute-start | bytes 1966088 | tf_op jit(solution)/shard_map/ppermute | solution.py:21
  722.3 212.4 %reduce-scatter.11.cloned.1.call-start = ((), (), s32[]{:S(2)}) async-start(), calls=%async_computation.10 | async-start | bytes 6635520 | tf_op jit(solution)/shard_map/reduce_scatter | solution.py:587
  722.5 15.6 %collective-permute-start.48 = (bf16[2,640,256]{2,1,0:T(8,128)(2,1)}, bf16[2,640,256]{2,1,0:T(8,128)(2,1)S(1)}, u32[]{:S(2)}, u32[]{:S(2)}) collective-permute-start(bf16[2,640,256]{2,1,0:T(8,128)(2,1)} %get-tuple-element.258), channel_id=1, source_target_pairs={{0,16},{16,0},{1,17},{17,1},{2,18},{18,2},{3,19},{19,3},{4,20},{20... | collective-permute-start | bytes 1966088 | tf_op jit(solution)/shard_map/ppermute | solution.py:21
  723.7 28.7 %collective-permute-start.49 = (bf16[2,640,256]{2,1,0:T(8,128)(2,1)}, bf16[2,640,256]{2,1,0:T(8,128)(2,1)S(1)}, u32[]{:S(2)}, u32[]{:S(2)}) collective-permute-start(bf16[2,640,256]{2,1,0:T(8,128)(2,1)} %fusion.29), channel_id=1, source_target_pairs={{0,4},{4,8},{8,12},{12,0},{1,5},{5,9},{9,13},{13,1},{2,6},{6,10},{... | collective-permute-start | bytes 1966088 | tf_op jit(solution)/shard_map/ppermute | solution.py:38
  753.7 44.3 %collective-permute-start.52 = (bf16[576,1152]{1,0:T(8,128)(2,1)S(1)}, bf16[576,1152]{1,0:T(8,128)(2,1)S(1)}, u32[]{:S(2)}, u32[]{:S(2)}) collective-permute-start(bf16[576,1152]{1,0:T(8,128)(2,1)S(1)} %copy-done.49), channel_id=1, source_target_pairs={{0,16},{16,0},{1,17},{17,1},{2,18},{18,2},{3,19},{19,3},{4,20},{20... | collective-permute-start | bytes 3981320 | tf_op jit(solution)/shard_map/ppermute | solution.py:21
  754.7 37.1 %collective-permute-start.50 = (bf16[2,640,256]{2,1,0:T(8,128)(2,1)S(1)}, bf16[2,640,256]{2,1,0:T(8,128)(2,1)S(1)}, u32[]{:S(2)}, u32[]{:S(2)}) collective-permute-start(bf16[2,640,256]{2,1,0:T(8,128)(2,1)S(1)} %copy-done.57), channel_id=1, source_target_pairs={{0,16},{16,0},{1,17},{17,1},{2,18},{18,2},{3,19},{19,3},{4,20},{20... | collective-permute-start | bytes 1966088 | tf_op jit(solution)/shard_map/ppermute | solution.py:21
  755.8 40.9 %collective-permute-start.51 = (bf16[2,640,256]{2,1,0:T(8,128)(2,1)S(1)}, bf16[2,640,256]{2,1,0:T(8,128)(2,1)S(1)}, u32[]{:S(2)}, u32[]{:S(2)}) collective-permute-start(bf16[2,640,256]{2,1,0:T(8,128)(2,1)S(1)} %fusion.25), channel_id=1, source_target_pairs={{0,4},{4,8},{8,12},{12,0},{1,5},{5,9},{9,13},{13,1},{2,6},{6,10},{... | collective-permute-start | bytes 1966088 | tf_op jit(solution)/shard_map/ppermute | solution.py:38
  799.1 19.2 %collective-permute-start.53 = (bf16[2,640,256]{2,1,0:T(8,128)(2,1)S(1)}, bf16[2,640,256]{2,1,0:T(8,128)(2,1)S(1)}, u32[]{:S(2)}, u32[]{:S(2)}) collective-permute-start(bf16[2,640,256]{2,1,0:T(8,128)(2,1)S(1)} %get-tuple-element.267), channel_id=1, source_target_pairs={{0,16},{16,0},{1,17},{17,1},{2,18},{18,2},{3,19},{19,3},{4,20},{20... | collective-permute-start | bytes 1966088 | tf_op jit(solution)/shard_map/ppermute | solution.py:21
  800.3 27.7 %collective-permute-start.54 = (bf16[2,640,256]{2,1,0:T(8,128)(2,1)S(1)}, bf16[2,640,256]{2,1,0:T(8,128)(2,1)}, u32[]{:S(2)}, u32[]{:S(2)}) collective-permute-start(bf16[2,640,256]{2,1,0:T(8,128)(2,1)S(1)} %fusion.27), channel_id=1, source_target_pairs={{0,4},{4,8},{8,12},{12,0},{1,5},{5,9},{9,13},{13,1},{2,6},{6,10},{... | collective-permute-start | bytes 1966088 | tf_op jit(solution)/shard_map/ppermute | solution.py:38
  846.5 16.1 %collective-permute-start.56 = (bf16[576,512]{1,0:T(8,128)(2,1)S(1)}, bf16[576,512]{1,0:T(8,128)(2,1)S(1)}, u32[]{:S(2)}, u32[]{:S(2)}) collective-permute-start(bf16[576,512]{1,0:T(8,128)(2,1)S(1)} %copy-done.58), channel_id=1, source_target_pairs={{0,16},{16,0},{1,17},{17,1},{2,18},{18,2},{3,19},{19,3},{4,20},{20... | collective-permute-start | bytes 1769480 | tf_op jit(solution)/shard_map/ppermute | solution.py:21
  862.6 18.4 %collective-permute-start.57 = (bf16[2,160,1152]{2,1,0:T(8,128)(2,1)S(1)}, bf16[2,160,1152]{2,1,0:T(8,128)(2,1)S(1)}, u32[]{:S(2)}, u32[]{:S(2)}) collective-permute-start(bf16[2,160,1152]{2,1,0:T(8,128)(2,1)S(1)} %slice_bitcast_fusion.5), channel_id=1, source_target_pairs={{0,16},{16,0},{1,17},{17,1},{2,18},{18,2},{3,19},{19,3},{4,20},{20... | collective-permute-start | bytes 2211848 | tf_op jit(solution)/shard_map/ppermute | solution.py:21
  864.4 17.9 %collective-permute-start.58 = (bf16[2,160,1152]{2,1,0:T(8,128)(2,1)S(1)}, bf16[2,160,1152]{2,1,0:T(8,128)(2,1)S(1)}, u32[]{:S(2)}, u32[]{:S(2)}) collective-permute-start(bf16[2,160,1152]{2,1,0:T(8,128)(2,1)S(1)} %slice_bitcast_fusion.4), channel_id=1, source_target_pairs={{0,2},{1,3},{2,0},{3,1},{4,6},{5,7},{6,4},{7,5},{8,10},{9,11},{10,... | collective-permute-start | bytes 2211848 | tf_op jit(solution)/shard_map/ppermute | solution.py:21
  882.7 25.3 %collective-permute-start.59 = (bf16[160,1152]{1,0:T(8,128)(2,1)S(1)}, bf16[160,1152]{1,0:T(8,128)(2,1)S(1)}, u32[]{:S(2)}, u32[]{:S(2)}) collective-permute-start(bf16[160,1152]{1,0:T(8,128)(2,1)S(1)} %fusion.82), channel_id=1, source_target_pairs={{0,2},{1,3},{2,0},{3,1},{4,6},{5,7},{6,4},{7,5},{8,10},{9,11},{10,... | collective-permute-start | bytes 1105928 | tf_op jit(solution)/shard_map/ppermute | solution.py:21
  886.8 39.1 %collective-permute-start.61 = (bf16[576,256]{1,0:T(8,128)(2,1)S(1)}, bf16[576,256]{1,0:T(8,128)(2,1)S(1)}, u32[]{:S(2)}, u32[]{:S(2)}) collective-permute-start(bf16[576,256]{1,0:T(8,128)(2,1)S(1)} %get-tuple-element.282), channel_id=1, source_target_pairs={{0,4},{4,0},{8,12},{12,8},{1,5},{5,1},{9,13},{13,9},{2,6},{6,2},{1... | collective-permute-start | bytes 884744 | tf_op jit(solution)/shard_map/ppermute | solution.py:21
  903.9 22.0 %collective-permute-start.62 = (bf16[576,256]{1,0:T(8,128)(2,1)S(1)}, bf16[576,256]{1,0:T(8,128)(2,1)S(1)}, u32[]{:S(2)}, u32[]{:S(2)}) collective-permute-start(bf16[576,256]{1,0:T(8,128)(2,1)S(1)} %get-tuple-element.283), channel_id=1, source_target_pairs={{0,8},{4,12},{8,0},{12,4},{1,9},{5,13},{9,1},{13,5},{2,10},{6,14},... | collective-permute-start | bytes 884744 | tf_op jit(solution)/shard_map/ppermute | solution.py:21
  906.0 28.7 %collective-permute-start.63 = (bf16[576,256]{1,0:T(8,128)(2,1)S(1)}, bf16[576,256]{1,0:T(8,128)(2,1)}, u32[]{:S(2)}, u32[]{:S(2)}) collective-permute-start(bf16[576,256]{1,0:T(8,128)(2,1)S(1)} %get-tuple-element.284), channel_id=1, source_target_pairs={{0,12},{4,8},{8,4},{12,0},{1,13},{5,9},{9,5},{13,1},{2,14},{6,10},... | collective-permute-start | bytes 884744 | tf_op jit(solution)/shard_map/ppermute | solution.py:21
  934.8 9.9 collective-permute-start.69
  941.7 17.6 %collective-permute-start.64 = (bf16[160,2304]{1,0:T(8,128)(2,1)S(1)}, bf16[160,2304]{1,0:T(8,128)(2,1)S(1)}, u32[]{:S(2)}, u32[]{:S(2)}) collective-permute-start(bf16[160,2304]{1,0:T(8,128)(2,1)S(1)} %fusion.19), channel_id=1, source_target_pairs={{0,2},{1,3},{2,0},{3,1},{4,6},{5,7},{6,4},{7,5},{8,10},{9,11},{10,... | collective-permute-start | bytes 2211848 | tf_op jit(solution)/shard_map/ppermute | solution.py:21
  941.7 39.7 %collective-permute-start.67 = (bf16[576,1152]{1,0:T(8,128)(2,1)}, bf16[576,1152]{1,0:T(8,128)(2,1)S(1)}, u32[]{:S(2)}, u32[]{:S(2)}) collective-permute-start(bf16[576,1152]{1,0:T(8,128)(2,1)} %reduce-scatter.11.cloned.1.call-done), channel_id=1, source_target_pairs={{0,16},{16,0},{1,17},{17,1},{2,18},{18,2},{3,19},{19,3},{4,20},{20... | collective-permute-start | bytes 3981320 | tf_op jit(solution)/shard_map/ppermute | solution.py:21
  944.7 14.7 %collective-permute-start.70 = (f32[4,2304]{1,0:T(4,128)S(1)}, f32[4,2304]{1,0:T(4,128)S(1)}, u32[]{:S(2)}, u32[]{:S(2)}) collective-permute-start(f32[4,2304]{1,0:T(4,128)S(1)} %fusion.100), channel_id=1, source_target_pairs={{0,8},{4,12},{8,0},{12,4},{1,9},{5,13},{9,1},{13,5},{2,10},{6,14},... | collective-permute-start | bytes 110600 | tf_op jit(solution)/shard_map/ppermute | solution.py:21
  959.4 16.3 %collective-permute-start.66 = (bf16[2,160,2304]{2,1,0:T(8,128)(2,1)S(1)}, bf16[2,160,2304]{2,1,0:T(8,128)(2,1)S(1)}, u32[]{:S(2)}, u32[]{:S(2)}) collective-permute-start(bf16[2,160,2304]{2,1,0:T(8,128)(2,1)S(1)} %pad_maximum_fusion.13), channel_id=1, source_target_pairs={{0,1},{1,0},{2,3},{3,2},{4,5},{5,4},{6,7},{7,6},{8,9},{9,8},{10,11... | collective-permute-start | bytes 4423688 | tf_op jit(solution)/shard_map/ppermute | solution.py:21
  960.6 21.9 %collective-permute-start.65 = (bf16[2,160,2304]{2,1,0:T(8,128)(2,1)S(1)}, bf16[2,160,2304]{2,1,0:T(8,128)(2,1)S(1)}, u32[]{:S(2)}, u32[]{:S(2)}) collective-permute-start(bf16[2,160,2304]{2,1,0:T(8,128)(2,1)S(1)} %copy-done.47), channel_id=1, source_target_pairs={{0,1},{1,0},{2,3},{3,2},{4,5},{5,4},{6,7},{7,6},{8,9},{9,8},{10,11... | collective-permute-start | bytes 4423688 | tf_op jit(solution)/shard_map/ppermute | solution.py:21
  (85 other events, 695.8 us)
Sparse Core Ops, SparseCore 0:
  32.0 136.2 all-gather.3
  201.6 109.6 all-gather.5
  312.9 97.4 all-gather.7
  523.8 92.2 reduce-scatter.4
  619.0 95.3 reduce-scatter.6
  722.4 71.0 reduce-scatter.8
  818.4 107.2 reduce-scatter.10
